TPU v7x, 32 devices: a whole 2x2x4 slice. The times are simulated.
32 devices in a mesh: blk: 16 (over z, y, x), lag: 2 (over core).
Axes of the slice: x: 2, y: 2, z: 4, core: 2. Of those that a mesh axis runs over, the one named last changes fastest.
Arguments:
- history: bfloat16 [64, 16384], P('lag', 'blk'), may hold values from -6 to 6
- tile_blocks: bfloat16 [2048, 128, 128], P('blk'), may hold values from -0.5 to 0.5
- tile_target: int32 [2048], P('blk'), may hold values from 0 to 7
- tile_source: int32 [2048], P('blk'), may hold values from 0 to 127, as said below
- tile_offset: int32 [2048], P('blk'), may hold values from 0 to 63
- delay_bins: int32 [128], replicated, may hold values from 0 to 63
- incident: float32 [16384], P('blk'), may hold values from -6 to 6
- self_inv: float32 [128, 128, 128], P('blk'), may hold values from -0.125 to 0.125
Outputs:
- pressure: float32 [16384], P('blk')
Inputs may be any that keep to these rules, and one draw needn't show every extreme that they name: `tile_source`: among the 128 tiles of one index of blk, at most 16 have a source block on any one index of blk (source blocks i * 8 to i * 8 + 7 for index i); in every draw, for every index of blk, some index of blk is the source of exactly 16 of its tiles.
All inputs are finite; a program needn't handle non-finite values.
Results may differ from a plain program's by a relative error of at most 0.0003.
Values may be sent and summed in bfloat16 or wider, within the bound.
No kernel may reach another device: no remote copies, remote signals or barrier semaphores. Data moves between devices by JAX's collectives and lax.ppermute only.
A program may use at most 64 MiB of HBM per device.

v0:
```python
import jax
import jax.numpy as jnp
from jax import lax
from jax.sharding import PartitionSpec as P


def select_rows(table, index, valid):
    row_ids = jnp.arange(table.shape[0], dtype=jnp.int32)
    onehot = ((index[:, None] == row_ids[None, :]) & valid[:, None]).astype(jnp.bfloat16)
    picked = jnp.dot(onehot, table, preferred_element_type=jnp.float32)
    return picked


def body(
    history, tile_blocks, tile_target, tile_source, tile_offset, delay_bins, incident, self_inv
):
    lag_rows = history.shape[0]
    tile_size = tile_blocks.shape[1]
    slab_blocks = self_inv.shape[0]
    lag_devices = lax.axis_size("lag")
    total_lags = lag_rows * lag_devices
    lag_first = lax.axis_index("lag") * lag_rows
    block_ids = jnp.arange(delay_bins.shape[0], dtype=jnp.int32)
    looked = jnp.sum(
        jnp.where(tile_source[:, None] == block_ids[None, :], delay_bins[None, :], 0), axis=1
    )
    lag_all = (tile_offset + looked) % total_lags
    lag_local = lag_all - lag_first
    owned_lag = (lag_local >= 0) & (lag_local < lag_rows)
    lag_pick = jnp.clip(lag_local, 0, lag_rows - 1)
    shard_piece = lax.all_gather(history, "blk", axis=1, tiled=True)
    span_blocks = shard_piece.shape[1] // tile_size
    piece_table = shard_piece.reshape(lag_rows * span_blocks, tile_size)
    inside = owned_lag & (tile_source >= 0) & (tile_source < span_blocks)
    index = lag_pick * span_blocks + jnp.clip(tile_source, 0, span_blocks - 1)
    picked = select_rows(piece_table, index, inside)
    vectors = picked.astype(jnp.bfloat16)
    contrib = jnp.einsum("tij,tj->ti", tile_blocks, vectors, preferred_element_type=jnp.float32)
    slab_ids = jnp.arange(slab_blocks, dtype=jnp.int32)
    onehot = (tile_target[None, :] == slab_ids[:, None]).astype(jnp.float32)
    partial_value = jnp.dot(
        onehot, contrib, precision=lax.Precision.HIGHEST, preferred_element_type=jnp.float32
    )
    summed = lax.psum(partial_value, "lag")
    excite = incident.reshape(slab_blocks, tile_size) - summed
    solved = jnp.einsum("bij,bj->bi", self_inv, excite, precision=lax.Precision.HIGHEST)
    return solved.reshape(slab_blocks * tile_size)


def solution(mesh):
    return jax.shard_map(
        body,
        mesh=mesh,
        in_specs=(
            P("lag", "blk"),
            P("blk", None, None),
            P("blk"),
            P("blk"),
            P("blk"),
            P(),
            P("blk"),
            P("blk", None, None),
        ),
        out_specs=P("blk"),
        check_vma=False,
    )
```

profile of v0, /device:TPU:0, one launch (start us, length us, event | category | flops | bytes accessed | tf_op | source)
XLA Modules:
  0.0 85.4 jit_solution(9417445111670891639)
XLA Ops:
  6.5 0.0 copy-start
  6.5 0.0 all-gather.2.cloned.1.call-start
  6.5 0.7 all-gather.2.cloned.1.call-update
  7.3 0.8 select_reduce_fusion
  8.1 0.7 compare_and_fusion
  8.8 0.7 clamp_add_fusion
  9.5 0.0 copy-start.2
  9.5 0.0 copy-start.1
  9.5 58.3 %all-gather.2.cloned.1.call-done = bf16[32,16384]{1,0:T(8,128)(2,1)} async-done(((bf16[32,1024]{1,0:T(8,128)(2,1)}), bf16[32,16384]{1,0:T(8,128)(2,1)}) %all-gather.2.cloned.1.call-update) | async-done | bytes 1048592 | tf_op jit(solution)/shard_map/all_gather | solution.py:31
  67.8 1.6 %reshape.15 = bf16[4096,128]{1,0:T(8,128)(2,1)S(1)} reshape(bf16[32,16384]{1,0:T(8,128)(2,1)} %all-gather.2.cloned.1.call-done) | data formatting | bytes 2097152 | tf_op jit(solution)/shard_map/reshape | solution.py:33
  69.4 0.6 fusion.6
  70.0 4.4 %fusion.11 = f32[128,1,128]{2,1,0:T(1,128)S(1)} fusion(bf16[128,128,128]{2,1,0:T(8,128)(2,1)} %param.9, bf16[128,128,1]{1,0,2:T(8,128)(2,1)S(1)} %fusion.6), kind=kOutput, calls=%fused_computation.7 | convolution fusion | flops 4194304 | bytes 4292608 | tf_op jit(solution)/shard_map/tij,tj->ti/dot_general | solution.py:38
  74.4 0.0 copy-done.2
  74.4 0.2 fusion.13
  74.6 2.5 %psum.7 = f32[8,128]{1,0:T(8,128)S(1)} all-reduce(f32[8,128]{1,0:T(8,128)S(1)} %fusion.13), channel_id=1, replica_groups=mesh['blk'=16,'lag'=2] {'lag'}, use_global_device_ids=true, to_apply=%region_1.2 | all-reduce | flops 1024 | bytes 8192 | tf_op jit(solution)/shard_map/psum | solution.py:44
  77.0 0.0 copy-done.1
  77.1 0.0 copy-done
  77.1 1.5 %fusion.18 = f32[8,1,128]{2,1,0:T(1,128)} fusion(f32[8,128,1]{1,2,0:T(1,128)S(1)} %bitcast.19, f32[8,128,128]{2,1,0:T(8,128)S(1)} %copy-done), kind=kOutput, calls=%fused_computation.22 | convolution fusion | flops 1572864 | bytes 532480 | tf_op jit(solution)/shard_map/bij,bj->bi/dot_general | solution.py:46
  (1 shorter events, 0.0 us)
Async XLA Ops:
  6.5 70.5 %copy-start = (f32[8,128,128]{2,1,0:T(8,128)S(1)}, f32[8,128,128]{2,1,0:T(8,128)}, u32[]{:S(2)}) copy-start(f32[8,128,128]{2,1,0:T(8,128)} %param.15) | copy-start | bytes 1572868
  6.5 61.3 %all-gather.2.cloned.1.call-start = ((), (), s32[]{:S(2)}) async-start(), calls=%async_computation | async-start | bytes 1114112 | tf_op jit(solution)/shard_map/all_gather | solution.py:31
  9.5 65.0 %copy-start.2 = (s32[128]{0:T(128)S(1)}, s32[128]{0:T(128)}, u32[]{:S(2)}) copy-start(s32[128]{0:T(128)} %param.10) | copy-start | bytes 1540
  9.5 67.6 %copy-start.1 = (f32[1024]{0:T(1024)S(1)}, f32[1024]{0:T(1024)}, u32[]{:S(2)}) copy-start(f32[1024]{0:T(1024)} %param.14) | copy-start | bytes 12292
Sparse Core Ops, SparseCore 0:
  10.1 57.6 all-gather.1
where the time goes:
time: 85.7 us; the launch traced here: 85.4 us
  waiting for transfers between devices  59 us (69%)
  between operations  13.4 us (16%)
  matrix products  6.75 us (8%)
  blocking collectives  2.47 us (3%)
  other arithmetic  2.2 us (3%)
  local copies, waits for them, and re-layouts  1.56 us (2%)
    all_gather x1, waiting for transfers between devices, body(): shard_piece = lax.all_gather(history, 'blk', axis=1, tiled=True)  58.3 us
    dot_general x1, matrix products, body(): jnp.einsum('tij,tj->ti', tile_blocks, vectors, preferred_element_type=jnp...  4.43 us
    psum x1, blocking collectives, body(): summed = lax.psum(partial_value, 'lag')  2.47 us
  transfers between devices with their start and end apart: 1, of which 1 were waited for; matrix products, arithmetic and copies ran while one was open for 3% of the time, Pallas kernels for 0%

commit v1 on v0

v1 whole, which is shorter than its diff:
```python
import functools

import jax
import jax.numpy as jnp
from jax import lax
from jax.experimental import pallas as pl
from jax.experimental.pallas import tpu as pltpu
from jax.sharding import PartitionSpec as P

NT_DIMS = (((1,), (1,)), ((), ()))
VMEM = pl.BlockSpec(memory_space=pltpu.VMEM)
SMEM = pl.BlockSpec(memory_space=pltpu.SMEM)


def select_kernel(size, rows_ref, table_ref, out_ref):
    pieces, lags, width = table_ref.shape
    table = jnp.concatenate(
        [
            table_ref[p, :, b * size : (b + 1) * size]
            for p in range(pieces)
            for b in range(width // size)
        ],
        axis=0,
    )
    tiles = rows_ref.shape[1]
    lane = lax.broadcasted_iota(jnp.int32, (tiles, size), 1)
    for d in range(rows_ref.shape[0]):
        row = jnp.transpose(jnp.broadcast_to(rows_ref[d : d + 1, :], (size, tiles)))
        onehot = jnp.concatenate(
            [
                jnp.where(row == lane + first, 1.0, 0.0).astype(jnp.bfloat16)
                for first in range(0, table.shape[0], size)
            ],
            axis=1,
        )
        picked = jnp.dot(onehot, table, preferred_element_type=jnp.float32)
        out_ref[d] = picked.astype(out_ref.dtype)


def couple_kernel(target_ref, mine_ref, other_ref, tiles_ref, incident_ref, inverse_ref, out_ref):
    blocks, size = incident_ref.shape
    tiles = tiles_ref.shape[0]
    vectors = mine_ref[...].astype(jnp.float32) + other_ref[...].astype(jnp.float32)
    block_id = lax.broadcasted_iota(jnp.int32, (blocks, size), 0)
    total = jnp.zeros((blocks, size), jnp.float32)
    group = 16
    for first in range(0, tiles, group):
        left = jnp.concatenate(
            [
                jnp.where(
                    block_id == target_ref[t],
                    jnp.broadcast_to(vectors[t : t + 1, :], (blocks, size)),
                    0.0,
                ).astype(jnp.bfloat16)
                for t in range(first, first + group)
            ],
            axis=1,
        )
        right = jnp.concatenate([tiles_ref[t] for t in range(first, first + group)], axis=1)
        total = total + lax.dot_general(left, right, NT_DIMS, preferred_element_type=jnp.float32)
    excite = incident_ref[...] - total
    for b in range(blocks):
        out_ref[b : b + 1, :] = lax.dot_general(
            excite[b : b + 1, :],
            inverse_ref[b],
            NT_DIMS,
            precision=lax.Precision.HIGHEST,
            preferred_element_type=jnp.float32,
        )


def body(
    history, tile_blocks, tile_target, tile_source, tile_offset, delay_bins, incident, self_inv
):
    lag_rows = history.shape[0]
    tile_count, size = tile_blocks.shape[:2]
    slab_blocks = self_inv.shape[0]
    n_blk, n_lag = lax.axis_size("blk"), lax.axis_size("lag")
    blk, lag = lax.axis_index("blk"), lax.axis_index("lag")
    total_lags = lag_rows * n_lag
    all_blocks = delay_bins.shape[0]
    bits = n_blk.bit_length() - 1
    gather_bits = [1 << i for i in range(bits // 2)]
    exchange_bits = [1 << i for i in range(bits // 2, bits)]
    crossed = n_lag == 2

    def hop(value, bit):
        flip = 1 if crossed else 0
        pairs = [
            (j * n_lag + c, (j ^ bit) * n_lag + (c ^ flip)) for j in range(n_blk) for c in range(n_lag)
        ]
        return lax.ppermute(value, ("blk", "lag"), pairs)

    pieces = history[None]
    for bit in gather_bits:
        pieces = jnp.concatenate([pieces, hop(pieces, bit)], axis=0)
    n_pieces = pieces.shape[0]

    block_ids = jnp.arange(all_blocks, dtype=jnp.int32)
    looked = jnp.sum(
        jnp.where(tile_source[:, None] == block_ids[None, :], delay_bins[None, :], 0), axis=1
    )
    requests = (((tile_offset + looked) % total_lags) * all_blocks + tile_source)[None]
    for bit in exchange_bits:
        requests = jnp.concatenate([requests, hop(requests, bit)], axis=0)

    source = requests % all_blocks
    wanted_lag = requests // all_blocks
    piece = (source // slab_blocks) ^ blk
    if crossed:
        flips = jnp.zeros_like(piece)
        for bit in gather_bits:
            flips = flips ^ ((piece // bit) % 2)
        half = lag ^ flips
    else:
        half = lag
    lag_local = wanted_lag - half * lag_rows
    inside = (piece < n_pieces) & (lag_local >= 0) & (lag_local < lag_rows)
    row = (piece * slab_blocks + source % slab_blocks) * lag_rows + lag_local
    rows = jnp.where(inside, row, -1)

    picked = pl.pallas_call(
        functools.partial(select_kernel, size),
        out_shape=jax.ShapeDtypeStruct((rows.shape[0], tile_count, size), jnp.bfloat16),
        in_specs=[VMEM, VMEM],
        out_specs=VMEM,
        name="select",
    )(rows, pieces)

    held = picked
    for i, bit in enumerate(exchange_bits):
        held = held.reshape((-1, 2) + held.shape[1:])
        keep, send = held[:, 0], held[:, 1]
        held = keep + hop(send, bit)
    mine = held.reshape(tile_count, size)
    if n_lag == 2:
        other = lax.ppermute(mine, "lag", [(0, 1), (1, 0)])
    else:
        other = lax.psum(mine, "lag") - mine

    solved = pl.pallas_call(
        couple_kernel,
        out_shape=jax.ShapeDtypeStruct((slab_blocks, size), jnp.float32),
        in_specs=[SMEM, VMEM, VMEM, VMEM, VMEM, VMEM],
        out_specs=VMEM,
        name="couple",
    )(tile_target, mine, other, tile_blocks, incident.reshape(slab_blocks, size), self_inv)
    return solved.reshape(slab_blocks * size)


def solution(mesh):
    return jax.shard_map(
        body,
        mesh=mesh,
        in_specs=(
            P("lag", "blk"),
            P("blk", None, None),
            P("blk"),
            P("blk"),
            P("blk"),
            P(),
            P("blk"),
            P("blk", None, None),
        ),
        out_specs=P("blk"),
        check_vma=False,
    )
```

time: 85.7 us -> 35.3 us (0.41)
  waiting for transfers between devices: 59 us -> 6.12 us
  between operations: 13.4 us -> 0.03 us
  starting transfers between devices: 0.01 us -> 13.1 us
  Pallas kernels: 0 us -> 8.83 us
  matrix products: 6.75 us -> 0 us
  other arithmetic: 2.2 us -> 5.44 us
  blocking collectives: 2.47 us -> 0 us
    all_gather x1 -> x0, waiting for transfers between devices: 58.3 us -> none  [body(): shard_piece = lax.all_gather(history, 'blk', axis=1, tiled=True)]
    ppermute x0 -> x7, starting transfers between devices: none -> 13.1 us  [the longest x6 12.7 us: hop(): return lax.ppermute(value, ('blk', 'lag'), pairs)]
    pallas_call x0 -> x2, Pallas kernels: none -> 8.83 us  [the longest x1 6.66 us: body(): pl.pallas_call(couple_kernel, out_shape=jax.ShapeDtypeStruct((slab_blocks...]
    dot_general x4 -> x0, matrix products: 6.75 us -> none  [the longest x1 4.43 us: body(): jnp.einsum('tij,tj->ti', tile_blocks, vectors, preferred_element_type=jnp...]
    ppermute x0 -> x7, waiting for transfers between devices: none -> 6.12 us  [the longest x6 5.26 us: hop(): return lax.ppermute(value, ('blk', 'lag'), pairs)]
    psum x1 -> x0, blocking collectives: 2.47 us -> none  [body(): summed = lax.psum(partial_value, 'lag')]
    concatenate x0 -> x3, other arithmetic: none -> 2.43 us  [the longest x2 2.42 us: body(): pieces = jnp.concatenate([pieces, hop(pieces, bit)], axis=0)]
    reshape x1 -> x0, local copies, waits for them, and re-layouts: 1.55 us -> none  [body(): piece_table = shard_piece.reshape(lag_rows * span_blocks, tile_size)]
  transfers between devices with their start and end apart: 1 -> 7, of which waited for: 1 -> 4; matrix products, arithmetic and copies ran while one was open for 3% -> 9% of each run, Pallas kernels for 0% -> 0%
where the time goes in v1:
time: 35.3 us; the launch traced here: 35 us
  starting transfers between devices  13.1 us (37%)
  Pallas kernels  8.83 us (25%)
  waiting for transfers between devices  6.12 us (17%)
  other arithmetic  5.44 us (15%)
  local copies, waits for them, and re-layouts  1.45 us (4%)
    ppermute x6, starting transfers between devices, hop(): return lax.ppermute(value, ('blk', 'lag'), pairs)  12.7 us
    pallas_call x1, Pallas kernels, body(): pl.pallas_call(couple_kernel, out_shape=jax.ShapeDtypeStruct((slab_blocks...  6.66 us
    ppermute x6, waiting for transfers between devices, hop(): return lax.ppermute(value, ('blk', 'lag'), pairs)  5.26 us
    concatenate x2, other arithmetic, body(): pieces = jnp.concatenate([pieces, hop(pieces, bit)], axis=0)  2.42 us
    pallas_call x1, Pallas kernels, body(): pl.pallas_call(functools.partial(select_kernel, size), out_shape=jax.Shap...  2.17 us
    ppermute x1, waiting for transfers between devices, body(): other = lax.ppermute(mine, 'lag', [(0, 1), (1, 0)])  0.86 us
    reshape x1, other arithmetic, body(): held = held.reshape((-1, 2) + held.shape[1:])  0.85 us
    squeeze x2, local copies, waits for them, and re-layouts, body(): keep, send = (held[:, 0], held[:, 1])  0.85 us
  transfers between devices with their start and end apart: 7, of which 4 were waited for; matrix products, arithmetic and copies ran while one was open for 9% of the time, Pallas kernels for 0%

profile of v1, /device:TPU:0, one launch (start us, length us, event | category | flops | bytes accessed | tf_op | source)
XLA Modules:
  0.0 35.0 jit_solution(4154007659832735889)
XLA Ops:
  0.0 2.4 %collective-permute-start.2 = (bf16[1,32,1024]{2,1,0:T(8,128)(2,1)}, bf16[1,32,1024]{2,1,0:T(8,128)(2,1)S(1)}, u32[]{:S(2)}, u32[]{:S(2)}) collective-permute-start(bf16[1,32,1024]{2,1,0:T(8,128)(2,1)} %bitcast.32), channel_id=1, source_target_pairs={{0,3},{1,2},{2,1},{3,0},{4,7},{5,6},{6,5},{7,4},{8,11},{9,10},{10,... | collective-permute-start | bytes 196616 | tf_op jit(solution)/shard_map/ppermute | solution.py:92
  2.4 0.8 %select_reduce_fusion = s32[128]{0:T(128)S(1)} fusion(s32[128]{0:T(128)} %param.13, s32[128]{0:T(128)} %param.11), kind=kLoop, calls=%fused_computation.6 | loop fusion | flops 49024 | bytes 1536 | tf_op jit(solution)/shard_map/reduce_sum | solution.py:100
  3.2 0.7 %fusion.22 = s32[1,128]{1,0:T(1,128)S(1)} fusion(s32[128]{0:T(128)} %param.11, s32[128]{0:T(128)} %param.12, s32[128]{0:T(128)S(1)} %select_reduce_fusion), kind=kLoop, calls=%fused_computation.56 | loop fusion | flops 1792 | bytes 2048 | tf_op jit(solution)/shard_map/broadcast_in_dim | solution.py:103
  3.9 1.9 %collective-permute-start = (s32[1,128]{1,0:T(1,128)S(1)}, s32[1,128]{1,0:T(1,128)S(1)}, u32[]{:S(2)}, u32[]{:S(2)}) collective-permute-start(s32[1,128]{1,0:T(1,128)S(1)} %fusion.22), channel_id=1, source_target_pairs={{0,9},{1,8},{2,11},{3,10},{4,13},{5,12},{6,15},{7,14},{8,1},{9,0},... | collective-permute-start | bytes 1544 | tf_op jit(solution)/shard_map/ppermute | solution.py:92
  5.8 0.0 collective-permute-done.2
  5.8 0.9 %pad_maximum_fusion.1 = bf16[2,32,1024]{2,1,0:T(8,128)(2,1)S(1)} fusion(bf16[1,32,1024]{2,1,0:T(8,128)(2,1)S(1)} %collective-permute-done.2, bf16[1,32,1024]{2,1,0:T(8,128)(2,1)} %bitcast.33), kind=kLoop, calls=%fused_computation.1 | loop fusion | flops 65536 | bytes 262144 | tf_op jit(solution)/shard_map/concatenate | solution.py:96
  6.7 1.5 %collective-permute-start.3 = (bf16[2,32,1024]{2,1,0:T(8,128)(2,1)S(1)}, bf16[2,32,1024]{2,1,0:T(8,128)(2,1)S(1)}, u32[]{:S(2)}, u32[]{:S(2)}) collective-permute-start(bf16[2,32,1024]{2,1,0:T(8,128)(2,1)S(1)} %pad_maximum_fusion.1), channel_id=1, source_target_pairs={{0,5},{1,4},{2,7},{3,6},{4,1},{5,0},{6,3},{7,2},{8,13},{9,12},{10,... | collective-permute-start | bytes 393224 | tf_op jit(solution)/shard_map/ppermute | solution.py:92
  8.2 0.0 collective-permute-done
  8.2 2.7 %collective-permute-start.1 = (s32[2,128]{1,0:T(2,128)S(1)}, s32[2,128]{1,0:T(2,128)S(1)}, u32[]{:S(2)}, u32[]{:S(2)}) collective-permute-start(s32[2,128]{1,0:T(2,128)S(1)} %pad_add_fusion.1), channel_id=1, source_target_pairs={{0,17},{1,16},{2,19},{3,18},{4,21},{5,20},{6,23},{7,22},{8,25},{9,... | collective-permute-start | bytes 3080 | tf_op jit(solution)/shard_map/ppermute | solution.py:92
  10.9 1.3 %collective-permute-done.1 = s32[2,128]{1,0:T(2,128)S(1)} collective-permute-done((s32[2,128]{1,0:T(2,128)S(1)}, s32[2,128]{1,0:T(2,128)S(1)}, u32[]{:S(2)}, u32[]{:S(2)}) %collective-permute-start.1) | collective-permute-done | bytes 1056 | tf_op jit(solution)/shard_map/ppermute | solution.py:92
  12.2 0.6 %fusion.13.rows_ref = s32[4,128]{1,0:T(4,128)} fusion(s32[2,128]{1,0:T(2,128)S(1)} %collective-permute-done.1, s32[1,128]{1,0:T(1,128)S(1)} %collective-permute-done, s32[1,128]{1,0:T(1,128)S(1)} %fusion.22, s32[]{:T(128)S(6)} %axis_index.25, s32[]{:T(128)S(6)} %axis_index.23), kind=kLoop, calls=%fused_computation.41 | loop fusion | flops 43520 | bytes 4104 | tf_op jit(solution)/shard_map/jit(_where)/select_n | solution.py:120
  12.8 0.0 collective-permute-done.3
  12.8 1.6 %pad_maximum_fusion.table_ref = bf16[4,32,1024]{2,1,0:T(8,128)(2,1)} fusion(bf16[2,32,1024]{2,1,0:T(8,128)(2,1)S(1)} %collective-permute-done.3, bf16[1,32,1024]{2,1,0:T(8,128)(2,1)S(1)} %collective-permute-done.2, bf16[1,32,1024]{2,1,0:T(8,128)(2,1)} %bitcast.34), kind=kLoop, calls=%fused_computation | loop fusion | flops 262144 | bytes 524288 | tf_op jit(solution)/shard_map/concatenate | solution.py:96
  14.4 2.2 %select.25 = bf16[4,128,128]{2,1,0:T(8,128)(2,1)} custom-call(s32[4,128]{1,0:T(4,128)} %fusion.13.rows_ref, bf16[4,32,1024]{2,1,0:T(8,128)(2,1)} %pad_maximum_fusion.table_ref), custom_call_target="tpu_custom_call" | custom-call | tf_op jit(solution)/shard_map/select/pallas_call | solution.py:122
  16.5 0.8 %slice_bitcast_fusion = bf16[2,128,128]{2,1,0:T(8,128)(2,1)S(1)} fusion(bf16[2,2,128,128]{3,2,1,0:T(8,128)(2,1)} %bitcast.30), kind=kLoop, calls=%fused_computation.2 | loop fusion | bytes 131072 | tf_op jit(solution)/shard_map/squeeze | solution.py:133
  17.4 1.6 %collective-permute-start.4 = (bf16[2,128,128]{2,1,0:T(8,128)(2,1)S(1)}, bf16[2,128,128]{2,1,0:T(8,128)(2,1)S(1)}, u32[]{:S(2)}, u32[]{:S(2)}) collective-permute-start(bf16[2,128,128]{2,1,0:T(8,128)(2,1)S(1)} %slice_bitcast_fusion), channel_id=1, source_target_pairs={{0,9},{1,8},{2,11},{3,10},{4,13},{5,12},{6,15},{7,14},{8,1},{9,0},... | collective-permute-start | bytes 196616 | tf_op jit(solution)/shard_map/ppermute | solution.py:92
  19.0 2.2 %collective-permute-done.4 = bf16[2,128,128]{2,1,0:T(8,128)(2,1)S(1)} collective-permute-done((bf16[2,128,128]{2,1,0:T(8,128)(2,1)S(1)}, bf16[2,128,128]{2,1,0:T(8,128)(2,1)S(1)}, u32[]{:S(2)}, u32[]{:S(2)}) %collective-permute-start.4) | collective-permute-done | bytes 65568 | tf_op jit(solution)/shard_map/ppermute | solution.py:92
  21.2 0.9 %fusion.1 = bf16[1,2,128,128]{3,2,1,0:T(8,128)(2,1)S(1)} fusion(bf16[2,128,128]{2,1,0:T(8,128)(2,1)S(1)} %collective-permute-done.4, bf16[2,2,128,128]{3,2,1,0:T(8,128)(2,1)} %bitcast.31), kind=kLoop, calls=%fused_computation.5 | loop fusion | flops 32768 | bytes 196608 | tf_op jit(solution)/shard_map/reshape | solution.py:132
  22.1 2.6 %collective-permute-start.5 = (bf16[1,128,128]{2,1,0:T(8,128)(2,1)S(1)}, bf16[1,128,128]{2,1,0:T(8,128)(2,1)S(1)}, u32[]{:S(2)}, u32[]{:S(2)}) collective-permute-start(bf16[1,128,128]{2,1,0:T(8,128)(2,1)S(1)} %slice_bitcast_fusion.2), channel_id=1, source_target_pairs={{0,17},{1,16},{2,19},{3,18},{4,21},{5,20},{6,23},{7,22},{8,25},{9,... | collective-permute-start | bytes 98312 | tf_op jit(solution)/shard_map/ppermute | solution.py:92
  24.7 1.7 %collective-permute-done.5 = bf16[1,128,128]{2,1,0:T(8,128)(2,1)S(1)} collective-permute-done((bf16[1,128,128]{2,1,0:T(8,128)(2,1)S(1)}, bf16[1,128,128]{2,1,0:T(8,128)(2,1)S(1)}, u32[]{:S(2)}, u32[]{:S(2)}) %collective-permute-start.5) | collective-permute-done | bytes 32800 | tf_op jit(solution)/shard_map/ppermute | solution.py:92
  26.4 0.0 copy-start
  26.4 0.4 %collective-permute-start.6 = (bf16[128,128]{1,0:T(8,128)(2,1)S(1)}, bf16[128,128]{1,0:T(8,128)(2,1)S(1)}, u32[]{:S(2)}, u32[]{:S(2)}) collective-permute-start(bf16[128,128]{1,0:T(8,128)(2,1)S(1)} %fusion.3.mine_ref), channel_id=1, source_target_pairs={{0,1},{1,0},{2,3},{3,2},{4,5},{5,4},{6,7},{7,6},{8,9},{9,8},{10,11... | collective-permute-start | bytes 98312 | tf_op jit(solution)/shard_map/ppermute | solution.py:137
  26.8 0.9 %collective-permute-done.6.other_ref = bf16[128,128]{1,0:T(8,128)(2,1)S(1)} collective-permute-done((bf16[128,128]{1,0:T(8,128)(2,1)S(1)}, bf16[128,128]{1,0:T(8,128)(2,1)S(1)}, u32[]{:S(2)}, u32[]{:S(2)}) %collective-permute-start.6) | collective-permute-done | bytes 32800 | tf_op jit(solution)/shard_map/ppermute | solution.py:137
  27.7 0.0 copy-start.1
  27.7 0.0 copy-done
  27.7 0.6 %copy-done.1 = bf16[128,128]{1,0:T(8,128)(2,1)} copy-done((bf16[128,128]{1,0:T(8,128)(2,1)}, bf16[128,128]{1,0:T(8,128)(2,1)S(1)}, u32[]{:S(2)}) %copy-start.1) | copy-done | bytes 32792
  28.3 6.7 %couple.1 = f32[8,128]{1,0:T(8,128)} custom-call(s32[128]{0:T(128)} %target_ref.1, bf16[128,128]{1,0:T(8,128)(2,1)} %copy-done, bf16[128,128]{1,0:T(8,128)(2,1)} %copy-done.1, bf16[128,128,128]{2,1,0:T(8,128)(2,1)} %tiles_ref.1, f32[8,128]{1,0:T(8,128)} %bitcast.35, f32[8,128,128]{2,1,0:T(8,128)} %inverse_ref.1), custom_call_target="tpu_custom_call" | custom-call | tf_op jit(solution)/shard_map/couple/pallas_call | solution.py:141
  (3 shorter events, 0.0 us)
Async XLA Ops:
  0.0 5.8 %collective-permute-start.2 = (bf16[1,32,1024]{2,1,0:T(8,128)(2,1)}, bf16[1,32,1024]{2,1,0:T(8,128)(2,1)S(1)}, u32[]{:S(2)}, u32[]{:S(2)}) collective-permute-start(bf16[1,32,1024]{2,1,0:T(8,128)(2,1)} %bitcast.32), channel_id=1, source_target_pairs={{0,3},{1,2},{2,1},{3,0},{4,7},{5,6},{6,5},{7,4},{8,11},{9,10},{10,... | collective-permute-start | bytes 196616 | tf_op jit(solution)/shard_map/ppermute | solution.py:92
  3.9 4.3 %collective-permute-start = (s32[1,128]{1,0:T(1,128)S(1)}, s32[1,128]{1,0:T(1,128)S(1)}, u32[]{:S(2)}, u32[]{:S(2)}) collective-permute-start(s32[1,128]{1,0:T(1,128)S(1)} %fusion.22), channel_id=1, source_target_pairs={{0,9},{1,8},{2,11},{3,10},{4,13},{5,12},{6,15},{7,14},{8,1},{9,0},... | collective-permute-start | bytes 1544 | tf_op jit(solution)/shard_map/ppermute | solution.py:92
  6.7 6.1 %collective-permute-start.3 = (bf16[2,32,1024]{2,1,0:T(8,128)(2,1)S(1)}, bf16[2,32,1024]{2,1,0:T(8,128)(2,1)S(1)}, u32[]{:S(2)}, u32[]{:S(2)}) collective-permute-start(bf16[2,32,1024]{2,1,0:T(8,128)(2,1)S(1)} %pad_maximum_fusion.1), channel_id=1, source_target_pairs={{0,5},{1,4},{2,7},{3,6},{4,1},{5,0},{6,3},{7,2},{8,13},{9,12},{10,... | collective-permute-start | bytes 393224 | tf_op jit(solution)/shard_map/ppermute | solution.py:92
  8.2 4.0 %collective-permute-start.1 = (s32[2,128]{1,0:T(2,128)S(1)}, s32[2,128]{1,0:T(2,128)S(1)}, u32[]{:S(2)}, u32[]{:S(2)}) collective-permute-start(s32[2,128]{1,0:T(2,128)S(1)} %pad_add_fusion.1), channel_id=1, source_target_pairs={{0,17},{1,16},{2,19},{3,18},{4,21},{5,20},{6,23},{7,22},{8,25},{9,... | collective-permute-start | bytes 3080 | tf_op jit(solution)/shard_map/ppermute | solution.py:92
  17.4 3.8 %collective-permute-start.4 = (bf16[2,128,128]{2,1,0:T(8,128)(2,1)S(1)}, bf16[2,128,128]{2,1,0:T(8,128)(2,1)S(1)}, u32[]{:S(2)}, u32[]{:S(2)}) collective-permute-start(bf16[2,128,128]{2,1,0:T(8,128)(2,1)S(1)} %slice_bitcast_fusion), channel_id=1, source_target_pairs={{0,9},{1,8},{2,11},{3,10},{4,13},{5,12},{6,15},{7,14},{8,1},{9,0},... | collective-permute-start | bytes 196616 | tf_op jit(solution)/shard_map/ppermute | solution.py:92
  22.1 4.3 %collective-permute-start.5 = (bf16[1,128,128]{2,1,0:T(8,128)(2,1)S(1)}, bf16[1,128,128]{2,1,0:T(8,128)(2,1)S(1)}, u32[]{:S(2)}, u32[]{:S(2)}) collective-permute-start(bf16[1,128,128]{2,1,0:T(8,128)(2,1)S(1)} %slice_bitcast_fusion.2), channel_id=1, source_target_pairs={{0,17},{1,16},{2,19},{3,18},{4,21},{5,20},{6,23},{7,22},{8,25},{9,... | collective-permute-start | bytes 98312 | tf_op jit(solution)/shard_map/ppermute | solution.py:92
  26.4 1.3 %copy-start = (bf16[128,128]{1,0:T(8,128)(2,1)}, bf16[128,128]{1,0:T(8,128)(2,1)S(1)}, u32[]{:S(2)}) copy-start(bf16[128,128]{1,0:T(8,128)(2,1)S(1)} %fusion.3.mine_ref) | copy-start | bytes 98308
  26.4 1.3 %collective-permute-start.6 = (bf16[128,128]{1,0:T(8,128)(2,1)S(1)}, bf16[128,128]{1,0:T(8,128)(2,1)S(1)}, u32[]{:S(2)}, u32[]{:S(2)}) collective-permute-start(bf16[128,128]{1,0:T(8,128)(2,1)S(1)} %fusion.3.mine_ref), channel_id=1, source_target_pairs={{0,1},{1,0},{2,3},{3,2},{4,5},{5,4},{6,7},{7,6},{8,9},{9,8},{10,11... | collective-permute-start | bytes 98312 | tf_op jit(solution)/shard_map/ppermute | solution.py:137
  27.7 0.6 %copy-start.1 = (bf16[128,128]{1,0:T(8,128)(2,1)}, bf16[128,128]{1,0:T(8,128)(2,1)S(1)}, u32[]{:S(2)}) copy-start(bf16[128,128]{1,0:T(8,128)(2,1)S(1)} %collective-permute-done.6.other_ref) | copy-start | bytes 98308

commit v2 on v0

v2 whole, which is shorter than its diff:
```python
import jax
import jax.numpy as jnp
from jax import lax
from jax.experimental import pallas as pl
from jax.experimental.pallas import tpu as pltpu
from jax.sharding import PartitionSpec as P

NT_DIMS = (((1,), (1,)), ((), ()))


VMEM = pl.BlockSpec(memory_space=pltpu.VMEM)
ANY = pl.BlockSpec(memory_space=pl.ANY)


def call(kernel, name, outs, held=(), loaded=(), left=(), scratch=(), cost=0):
    return pl.pallas_call(
        kernel,
        out_shape=outs,
        in_specs=[VMEM] * (len(held) + len(loaded)) + [ANY] * len(left),
        out_specs=jax.tree.map(lambda _: VMEM, outs),
        scratch_shapes=scratch,
        compiler_params=pltpu.CompilerParams(vmem_limit_bytes=16 * 1024 * 1024),
        cost_estimate=pl.CostEstimate(flops=0, bytes_accessed=cost, transcendentals=0),
        name=name,
    )(
        *(pltpu.with_memory_space_constraint(a, pltpu.VMEM) for a in held),
        *(pltpu.with_memory_space_constraint(a, pltpu.HBM) for a in loaded + left),
    )


def in_vmem(a):
    return pltpu.VMEM(a.shape, a.dtype)


def request_kernel(total_lags, shift, source_ref, offset_ref, delay_ref, history_ref, code_ref, own_ref):
    source = source_ref[...]
    lane = source.shape[1]
    chunk = 128
    looked = jnp.zeros_like(source)
    for first in range(0, delay_ref.shape[1], chunk):
        delay = jnp.transpose(jnp.broadcast_to(delay_ref[:, first : first + chunk], (lane, chunk)))
        block = lax.broadcasted_iota(jnp.int32, (chunk, lane), 0) + first
        looked = looked + jnp.sum(jnp.where(block == source, delay, 0), axis=0, keepdims=True)
    lag = offset_ref[...] + looked
    lag = jnp.where(lag >= total_lags, lag - total_lags, lag)
    code_ref[...] = (lag << shift) | source
    own_ref[...] = history_ref[...]


def join_kernel(*refs):
    pairs = len(refs) // 3
    for i in range(pairs):
        mine_ref, other_ref, out_ref = refs[2 * i], refs[2 * i + 1], refs[2 * pairs + i]
        rows = mine_ref.shape[0]
        out_ref[:rows] = mine_ref[...]
        out_ref[rows:] = other_ref[...]


def select_kernel(plan, near_ref, far_ref, *refs):
    *piece_refs, keep_ref, send_ref = refs
    size, slab_shift, shift, lag_rows, crossed = plan
    blk, lag = lax.axis_index("blk"), lax.axis_index("lag")
    slabs = [r[q] for r in piece_refs for q in range(r.shape[0])]
    width = slabs[0].shape[1]
    table = jnp.concatenate(
        [s[:, b : b + size] for s in slabs for b in range(0, width, size)], axis=0
    )
    code = jnp.concatenate([near_ref[...], far_ref[...]], axis=0)
    tiles = code.shape[1]
    source = code & ((1 << shift) - 1)
    wanted = code >> shift
    piece = (source >> slab_shift) ^ blk
    if crossed:
        flips, rest = jnp.zeros_like(piece), piece
        for _ in range((len(slabs) - 1).bit_length()):
            flips = flips ^ (rest & 1)
            rest = rest >> 1
        half = flips ^ lag
    else:
        half = jnp.zeros_like(piece) + lag
    local = wanted - half * lag_rows
    inside = (piece < len(slabs)) & (local >= 0) & (local < lag_rows)
    row = ((piece << slab_shift) + (source & ((1 << slab_shift) - 1))) * lag_rows + local
    row = jnp.where(inside, row, -1)
    lane = lax.broadcasted_iota(jnp.int32, (tiles, size), 1)
    for d in range(code.shape[0]):
        mine = jnp.transpose(jnp.broadcast_to(row[d : d + 1, :], (size, tiles)))
        onehot = jnp.concatenate(
            [
                jnp.where(mine == lane + first, 1.0, 0.0).astype(jnp.bfloat16)
                for first in range(0, table.shape[0], size)
            ],
            axis=1,
        )
        picked = jnp.dot(onehot, table, preferred_element_type=jnp.float32).astype(jnp.bfloat16)
        (send_ref if d % 2 else keep_ref)[d // 2] = picked


def stage_kernel(count, held_ref, *refs):
    sources, passed_ref, targets, sems = refs[:count], refs[count], refs[count + 1 : -1], refs[-1]
    copies = [pltpu.make_async_copy(s, t, sems.at[i]) for i, (s, t) in enumerate(zip(sources, targets))]
    for copy in copies:
        copy.start()
    passed_ref[...] = held_ref[...]
    for copy in copies:
        copy.wait()


def couple_kernel(mine_ref, other_ref, tiles_ref, target_ref, incident_ref, inverse_ref, out_ref):
    blocks, size = incident_ref.shape
    tiles = tiles_ref.shape[0]
    vectors = mine_ref[...].astype(jnp.float32) + other_ref[...].astype(jnp.float32)
    target = jnp.transpose(jnp.broadcast_to(target_ref[...], (size, tiles)))
    left = jnp.stack([jnp.where(target == b, vectors, 0.0) for b in range(blocks)], axis=0)
    left = left.astype(jnp.bfloat16).reshape(blocks, tiles * size)
    right = jnp.concatenate([tiles_ref[t] for t in range(tiles)], axis=1)
    total = lax.dot_general(left, right, NT_DIMS, preferred_element_type=jnp.float32)
    excite = incident_ref[...] - total
    lane = lax.broadcasted_iota(jnp.int32, (size, blocks), 1)
    solved = jnp.zeros((size, blocks), jnp.float32)
    for b in range(blocks):
        product = inverse_ref[b] * jnp.broadcast_to(excite[b : b + 1, :], (size, size))
        solved = jnp.where(lane == b, jnp.sum(product, axis=1, keepdims=True), solved)
    out_ref[...] = jnp.transpose(solved)


def body(
    history, tile_blocks, tile_target, tile_source, tile_offset, delay_bins, incident, self_inv
):
    lag_rows = history.shape[0]
    tile_count, size = tile_blocks.shape[:2]
    slab_blocks = self_inv.shape[0]
    n_blk, n_lag = lax.axis_size("blk"), lax.axis_size("lag")
    all_blocks = delay_bins.shape[0]
    bits = n_blk.bit_length() - 1
    shift = all_blocks.bit_length() - 1
    slab_shift = slab_blocks.bit_length() - 1
    gather_bits = [1 << i for i in range(bits // 2)]
    exchange_bits = [1 << i for i in range(bits // 2, bits)]
    crossed = n_lag == 2

    def hop(value, bit):
        flip = 1 if crossed else 0
        pairs = [
            (j * n_lag + c, (j ^ bit) * n_lag + (c ^ flip)) for j in range(n_blk) for c in range(n_lag)
        ]
        return lax.ppermute(value, ("blk", "lag"), pairs)

    first = hop(history[None], gather_bits[0])
    code, own = call(
        lambda *refs: request_kernel(lag_rows * n_lag, shift, *refs),
        "request",
        (pltpu.VMEM((1, tile_count), jnp.int32), in_vmem(history)),
        loaded=(tile_source[None], tile_offset[None], delay_bins[None], history),
    )

    pieces, arrived = own[None], first
    for i in range(max(len(exchange_bits), len(gather_bits)) - 1):
        pairs = []
        if i < len(exchange_bits) - 1:
            pairs += [code, hop(code, exchange_bits[i])]
        if i < len(gather_bits) - 1:
            pairs += [pieces, arrived]
        joined = list(
            call(
                join_kernel,
                "join",
                tuple(
                    pltpu.VMEM((2 * a.shape[0],) + a.shape[1:], a.dtype) for a in pairs[::2]
                ),
                held=tuple(pairs),
            )
        )
        if i < len(exchange_bits) - 1:
            code = joined.pop(0)
        if i < len(gather_bits) - 1:
            pieces = joined.pop(0)
            arrived = hop(pieces, gather_bits[i + 1])
    far_code, far_pieces = hop(code, exchange_bits[-1]), arrived

    half = code.shape[0]
    picked = (half, tile_count, size)
    keep, send = call(
        lambda *refs: select_kernel((size, slab_shift, shift, lag_rows, crossed), *refs),
        "select",
        (pltpu.VMEM(picked, jnp.bfloat16), pltpu.VMEM(picked, jnp.bfloat16)),
        held=(code, far_code, pieces, far_pieces),
    )

    late = (tile_blocks, tile_target[None], incident.reshape(slab_blocks, size), self_inv)
    keep, *staged = call(
        lambda *refs: stage_kernel(len(late), *refs),
        "stage",
        tuple(in_vmem(a) for a in (keep,) + late),
        held=(keep,),
        left=late,
        scratch=[pltpu.SemaphoreType.DMA((len(late),))],
        cost=tile_blocks.size * 2,
    )

    for bit in exchange_bits:
        held = keep + hop(send, bit)
        keep, send = held[0::2], held[1::2]
    mine = held.reshape(tile_count, size)
    if n_lag == 2:
        other = lax.ppermute(mine, "lag", [(0, 1), (1, 0)])
    else:
        other = lax.psum(mine, "lag") - mine

    solved = call(
        couple_kernel,
        "couple",
        jax.ShapeDtypeStruct((slab_blocks, size), jnp.float32),
        held=(mine, other) + tuple(staged),
    )
    return solved.reshape(slab_blocks * size)


def solution(mesh):
    return jax.shard_map(
        body,
        mesh=mesh,
        in_specs=(
            P("lag", "blk"),
            P("blk", None, None),
            P("blk"),
            P("blk"),
            P("blk"),
            P(),
            P("blk"),
            P("blk", None, None),
        ),
        out_specs=P("blk"),
        check_vma=False,
    )
```

time: 85.7 us -> 24.8 us (0.29)
  waiting for transfers between devices: 59 us -> 6.46 us
  between operations: 13.4 us -> 0.04 us
  starting transfers between devices: 0.01 us -> 12.1 us
  matrix products: 6.75 us -> 0 us
  Pallas kernels: 0 us -> 6.09 us
  blocking collectives: 2.47 us -> 0 us
  other arithmetic: 2.2 us -> 0.03 us
  local copies, waits for them, and re-layouts: 1.56 us -> 0.01 us
    all_gather x1 -> x0, waiting for transfers between devices: 58.3 us -> none  [body(): shard_piece = lax.all_gather(history, 'blk', axis=1, tiled=True)]
    ppermute x0 -> x7, starting transfers between devices: none -> 12.1 us  [the longest x6 11.9 us: hop(): return lax.ppermute(value, ('blk', 'lag'), pairs)]
    dot_general x4 -> x0, matrix products: 6.75 us -> none  [the longest x1 4.43 us: body(): jnp.einsum('tij,tj->ti', tile_blocks, vectors, preferred_element_type=jnp...]
    ppermute x0 -> x7, waiting for transfers between devices: none -> 6.46 us  [the longest x6 5.38 us: hop(): return lax.ppermute(value, ('blk', 'lag'), pairs)]
    pallas_call x0 -> x5, Pallas kernels: none -> 6.09 us  [call(): pl.pallas_call(kernel, out_shape=outs, in_specs=[VMEM] * (len(held) + len...]
    psum x1 -> x0, blocking collectives: 2.47 us -> none  [body(): summed = lax.psum(partial_value, 'lag')]
    reshape x1 -> x0, local copies, waits for them, and re-layouts: 1.55 us -> none  [body(): piece_table = shard_piece.reshape(lag_rows * span_blocks, tile_size)]
  transfers between devices with their start and end apart: 1 -> 7, of which waited for: 1 -> 5; matrix products, arithmetic and copies ran while one was open for 3% -> 0% of each run, Pallas kernels for 0% -> 14%
where the time goes in v2:
time: 24.8 us; the launch traced here: 24.7 us
  starting transfers between devices  12.1 us (49%)
  waiting for transfers between devices  6.46 us (26%)
  Pallas kernels  6.09 us (25%)
    ppermute x6, starting transfers between devices, hop(): return lax.ppermute(value, ('blk', 'lag'), pairs)  11.9 us
    pallas_call x5, Pallas kernels, call(): pl.pallas_call(kernel, out_shape=outs, in_specs=[VMEM] * (len(held) + len...  6.09 us
    ppermute x6, waiting for transfers between devices, hop(): return lax.ppermute(value, ('blk', 'lag'), pairs)  5.38 us
    ppermute x1, waiting for transfers between devices, body(): other = lax.ppermute(mine, 'lag', [(0, 1), (1, 0)])  1.08 us
  transfers between devices with their start and end apart: 7, of which 5 were waited for; matrix products, arithmetic and copies ran while one was open for 0% of the time, Pallas kernels for 14%

profile of v2, /device:TPU:0, one launch (start us, length us, event | category | flops | bytes accessed | tf_op | source)
XLA Modules:
  0.0 24.7 jit_solution(13416009427821835103)
XLA Ops:
  0.0 2.4 %collective-permute-start.1 = (bf16[1,32,1024]{2,1,0:T(8,128)(2,1)}, bf16[1,32,1024]{2,1,0:T(8,128)(2,1)S(1)}, u32[]{:S(2)}, u32[]{:S(2)}) collective-permute-start(bf16[1,32,1024]{2,1,0:T(8,128)(2,1)} %bitcast.11), channel_id=1, source_target_pairs={{0,3},{1,2},{2,1},{3,0},{4,7},{5,6},{6,5},{7,4},{8,11},{9,10},{10,... | collective-permute-start | bytes 196616 | tf_op jit(solution)/shard_map/ppermute | solution.py:147
  2.4 1.0 %request.1 = (s32[1,128]{1,0:T(1,128)S(1)}, bf16[32,1024]{1,0:T(8,128)(2,1)S(1)}) custom-call(s32[1,128]{1,0:T(1,128)} %bitcast.13, s32[1,128]{1,0:T(1,128)} %bitcast.14, s32[1,128]{1,0:T(1,128)} %bitcast.15, bf16[32,1024]{1,0:T(8,128)(2,1)} %refs_3_.1), custom_call_target="tpu_custom_call" | custom-call | tf_op jit(solution)/shard_map/request/pallas_call | solution.py:16
  3.4 1.9 %collective-permute-start = (s32[1,128]{1,0:T(1,128)S(1)}, s32[1,128]{1,0:T(1,128)S(1)}, u32[]{:S(2)}, u32[]{:S(2)}) collective-permute-start(s32[1,128]{1,0:T(1,128)S(1)} %get-tuple-element.16.refs_0_), channel_id=1, source_target_pairs={{0,9},{1,8},{2,11},{3,10},{4,13},{5,12},{6,15},{7,14},{8,1},{9,0},... | collective-permute-start | bytes 1544 | tf_op jit(solution)/shard_map/ppermute | solution.py:147
  5.3 1.3 %collective-permute-done.refs_1_ = s32[1,128]{1,0:T(1,128)S(1)} collective-permute-done((s32[1,128]{1,0:T(1,128)S(1)}, s32[1,128]{1,0:T(1,128)S(1)}, u32[]{:S(2)}, u32[]{:S(2)}) %collective-permute-start) | collective-permute-done | bytes 544 | tf_op jit(solution)/shard_map/ppermute | solution.py:147
  6.6 0.0 collective-permute-done.1.refs_3_
  6.6 1.7 %collective-permute-start.3 = (bf16[2,32,1024]{2,1,0:T(8,128)(2,1)S(1)}, bf16[2,32,1024]{2,1,0:T(8,128)(2,1)S(1)}, u32[]{:S(2)}, u32[]{:S(2)}) collective-permute-start(bf16[2,32,1024]{2,1,0:T(8,128)(2,1)S(1)} %get-tuple-element.19.refs_2_), channel_id=1, source_target_pairs={{0,5},{1,4},{2,7},{3,6},{4,1},{5,0},{6,3},{7,2},{8,13},{9,12},{10,... | collective-permute-start | bytes 393224 | tf_op jit(solution)/shard_map/ppermute | solution.py:147
  8.3 2.2 %collective-permute-start.2 = (s32[2,128]{1,0:T(2,128)S(1)}, s32[2,128]{1,0:T(2,128)S(1)}, u32[]{:S(2)}, u32[]{:S(2)}) collective-permute-start(s32[2,128]{1,0:T(2,128)S(1)} %get-tuple-element.18.refs_0_), channel_id=1, source_target_pairs={{0,17},{1,16},{2,19},{3,18},{4,21},{5,20},{6,23},{7,22},{8,25},{9,... | collective-permute-start | bytes 3080 | tf_op jit(solution)/shard_map/ppermute | solution.py:147
  10.5 1.7 %collective-permute-done.2.refs_1_ = s32[2,128]{1,0:T(2,128)S(1)} collective-permute-done((s32[2,128]{1,0:T(2,128)S(1)}, s32[2,128]{1,0:T(2,128)S(1)}, u32[]{:S(2)}, u32[]{:S(2)}) %collective-permute-start.2) | collective-permute-done | bytes 1056 | tf_op jit(solution)/shard_map/ppermute | solution.py:147
  12.2 0.0 collective-permute-done.3.refs_3_
  12.2 0.6 %select.1 = (bf16[2,128,128]{2,1,0:T(8,128)(2,1)S(1)}, bf16[2,128,128]{2,1,0:T(8,128)(2,1)S(1)}) custom-call(s32[2,128]{1,0:T(2,128)S(1)} %get-tuple-element.18.refs_0_, s32[2,128]{1,0:T(2,128)S(1)} %collective-permute-done.2.refs_1_, bf16[2,32,1024]{2,1,0:T(8,128)(2,1)S(1)} %get-tuple-element.19.refs_2_, bf16[2,32,1024]{2,1,0:T(8,128)(2,1)S(1)} %collective-permute-done.3.refs_3_), custom_call_target="tpu_custom_call" | custom-call | tf_op jit(solution)/shard_map/select/pallas_call | solution.py:16
  12.8 1.4 %collective-permute-start.4 = (bf16[2,128,128]{2,1,0:T(8,128)(2,1)S(1)}, bf16[2,128,128]{2,1,0:T(8,128)(2,1)S(1)}, u32[]{:S(2)}, u32[]{:S(2)}) collective-permute-start(bf16[2,128,128]{2,1,0:T(8,128)(2,1)S(1)} %get-tuple-element.22), channel_id=1, source_target_pairs={{0,9},{1,8},{2,11},{3,10},{4,13},{5,12},{6,15},{7,14},{8,1},{9,0},... | collective-permute-start | bytes 196616 | tf_op jit(solution)/shard_map/ppermute | solution.py:147
  14.1 2.4 %stage.1 = (bf16[2,128,128]{2,1,0:T(8,128)(2,1)S(1)}, bf16[128,128,128]{2,1,0:T(8,128)(2,1)S(1)}, s32[1,128]{1,0:T(1,128)S(1)}, f32[8,128]{1,0:T(8,128)S(1)}, f32[8,128,128]{2,1,0:T(8,128)S(1)}) custom-call(bf16[2,128,128]{2,1,0:T(8,128)(2,1)S(1)} %get-tuple-element.20.refs_0_, bf16[128,128,128]{2,1,0:T(8,128)(2,1)} %refs_1_.1, s32[1,128]{1,0:T(1,128)} %bitcast.16, ...), custom_call_target="tpu_custom_call" | custom-call | bytes 4194304 | tf_op jit(solution)/shard_map/stage/pallas_call | solution.py:16
  16.5 0.4 %collective-permute-done.4 = bf16[2,128,128]{2,1,0:T(8,128)(2,1)S(1)} collective-permute-done((bf16[2,128,128]{2,1,0:T(8,128)(2,1)S(1)}, bf16[2,128,128]{2,1,0:T(8,128)(2,1)S(1)}, u32[]{:S(2)}, u32[]{:S(2)}) %collective-permute-start.4) | collective-permute-done | bytes 65568 | tf_op jit(solution)/shard_map/ppermute | solution.py:147
  17.0 2.4 %collective-permute-start.5 = (bf16[1,128,128]{2,1,0:T(8,128)(2,1)S(1)}, bf16[1,128,128]{2,1,0:T(8,128)(2,1)S(1)}, u32[]{:S(2)}, u32[]{:S(2)}) collective-permute-start(bf16[1,128,128]{2,1,0:T(8,128)(2,1)S(1)} %slice.11), channel_id=1, source_target_pairs={{0,17},{1,16},{2,19},{3,18},{4,21},{5,20},{6,23},{7,22},{8,25},{9,... | collective-permute-start | bytes 98312 | tf_op jit(solution)/shard_map/ppermute | solution.py:147
  19.4 2.0 %collective-permute-done.5 = bf16[1,128,128]{2,1,0:T(8,128)(2,1)S(1)} collective-permute-done((bf16[1,128,128]{2,1,0:T(8,128)(2,1)S(1)}, bf16[1,128,128]{2,1,0:T(8,128)(2,1)S(1)}, u32[]{:S(2)}, u32[]{:S(2)}) %collective-permute-start.5) | collective-permute-done | bytes 32800 | tf_op jit(solution)/shard_map/ppermute | solution.py:147
  21.3 0.1 collective-permute-start.6
  21.5 1.1 %collective-permute-done.6.other_ref = bf16[128,128]{1,0:T(8,128)(2,1)S(1)} collective-permute-done((bf16[128,128]{1,0:T(8,128)(2,1)S(1)}, bf16[128,128]{1,0:T(8,128)(2,1)S(1)}, u32[]{:S(2)}, u32[]{:S(2)}) %collective-permute-start.6) | collective-permute-done | bytes 32800 | tf_op jit(solution)/shard_map/ppermute | solution.py:206
  22.6 2.1 %couple.1 = f32[8,128]{1,0:T(8,128)} custom-call(bf16[128,128]{1,0:T(8,128)(2,1)S(1)} %fusion.mine_ref, bf16[128,128]{1,0:T(8,128)(2,1)S(1)} %collective-permute-done.6.other_ref, bf16[128,128,128]{2,1,0:T(8,128)(2,1)S(1)} %get-tuple-element.23.tiles_ref, s32[1,128]{1,0:T(1,128)S(1)} %get-tuple-element.24.target_ref, ...), custom_call_target="tpu_custom_call" | custom-call | tf_op jit(solution)/shard_map/couple/pallas_call | solution.py:16
  (4 shorter events, 0.0 us)
Async XLA Ops:
  0.0 6.6 %collective-permute-start.1 = (bf16[1,32,1024]{2,1,0:T(8,128)(2,1)}, bf16[1,32,1024]{2,1,0:T(8,128)(2,1)S(1)}, u32[]{:S(2)}, u32[]{:S(2)}) collective-permute-start(bf16[1,32,1024]{2,1,0:T(8,128)(2,1)} %bitcast.11), channel_id=1, source_target_pairs={{0,3},{1,2},{2,1},{3,0},{4,7},{5,6},{6,5},{7,4},{8,11},{9,10},{10,... | collective-permute-start | bytes 196616 | tf_op jit(solution)/shard_map/ppermute | solution.py:147
  3.4 3.2 %collective-permute-start = (s32[1,128]{1,0:T(1,128)S(1)}, s32[1,128]{1,0:T(1,128)S(1)}, u32[]{:S(2)}, u32[]{:S(2)}) collective-permute-start(s32[1,128]{1,0:T(1,128)S(1)} %get-tuple-element.16.refs_0_), channel_id=1, source_target_pairs={{0,9},{1,8},{2,11},{3,10},{4,13},{5,12},{6,15},{7,14},{8,1},{9,0},... | collective-permute-start | bytes 1544 | tf_op jit(solution)/shard_map/ppermute | solution.py:147
  6.6 5.6 %collective-permute-start.3 = (bf16[2,32,1024]{2,1,0:T(8,128)(2,1)S(1)}, bf16[2,32,1024]{2,1,0:T(8,128)(2,1)S(1)}, u32[]{:S(2)}, u32[]{:S(2)}) collective-permute-start(bf16[2,32,1024]{2,1,0:T(8,128)(2,1)S(1)} %get-tuple-element.19.refs_2_), channel_id=1, source_target_pairs={{0,5},{1,4},{2,7},{3,6},{4,1},{5,0},{6,3},{7,2},{8,13},{9,12},{10,... | collective-permute-start | bytes 393224 | tf_op jit(solution)/shard_map/ppermute | solution.py:147
  8.3 3.9 %collective-permute-start.2 = (s32[2,128]{1,0:T(2,128)S(1)}, s32[2,128]{1,0:T(2,128)S(1)}, u32[]{:S(2)}, u32[]{:S(2)}) collective-permute-start(s32[2,128]{1,0:T(2,128)S(1)} %get-tuple-element.18.refs_0_), channel_id=1, source_target_pairs={{0,17},{1,16},{2,19},{3,18},{4,21},{5,20},{6,23},{7,22},{8,25},{9,... | collective-permute-start | bytes 3080 | tf_op jit(solution)/shard_map/ppermute | solution.py:147
  12.8 4.2 %collective-permute-start.4 = (bf16[2,128,128]{2,1,0:T(8,128)(2,1)S(1)}, bf16[2,128,128]{2,1,0:T(8,128)(2,1)S(1)}, u32[]{:S(2)}, u32[]{:S(2)}) collective-permute-start(bf16[2,128,128]{2,1,0:T(8,128)(2,1)S(1)} %get-tuple-element.22), channel_id=1, source_target_pairs={{0,9},{1,8},{2,11},{3,10},{4,13},{5,12},{6,15},{7,14},{8,1},{9,0},... | collective-permute-start | bytes 196616 | tf_op jit(solution)/shard_map/ppermute | solution.py:147
  17.0 4.4 %collective-permute-start.5 = (bf16[1,128,128]{2,1,0:T(8,128)(2,1)S(1)}, bf16[1,128,128]{2,1,0:T(8,128)(2,1)S(1)}, u32[]{:S(2)}, u32[]{:S(2)}) collective-permute-start(bf16[1,128,128]{2,1,0:T(8,128)(2,1)S(1)} %slice.11), channel_id=1, source_target_pairs={{0,17},{1,16},{2,19},{3,18},{4,21},{5,20},{6,23},{7,22},{8,25},{9,... | collective-permute-start | bytes 98312 | tf_op jit(solution)/shard_map/ppermute | solution.py:147
  21.3 1.2 %collective-permute-start.6 = (bf16[128,128]{1,0:T(8,128)(2,1)S(1)}, bf16[128,128]{1,0:T(8,128)(2,1)S(1)}, u32[]{:S(2)}, u32[]{:S(2)}) collective-permute-start(bf16[128,128]{1,0:T(8,128)(2,1)S(1)} %fusion.mine_ref), channel_id=1, source_target_pairs={{0,1},{1,0},{2,3},{3,2},{4,5},{5,4},{6,7},{7,6},{8,9},{9,8},{10,11... | collective-permute-start | bytes 98312 | tf_op jit(solution)/shard_map/ppermute | solution.py:206

commit v3 on v2

--- a/solution.py
+++ b/solution.py
@@ -5,14 +5,12 @@
 from jax.experimental.pallas import tpu as pltpu
 from jax.sharding import PartitionSpec as P
 
-NT_DIMS = (((1,), (1,)), ((), ()))
-
 
 VMEM = pl.BlockSpec(memory_space=pltpu.VMEM)
 ANY = pl.BlockSpec(memory_space=pl.ANY)
 
 
-def call(kernel, name, outs, held=(), loaded=(), left=(), scratch=(), cost=0):
+def call(kernel, name, outs, held=(), loaded=(), left=(), scratch=(), cost=0, flops=0):
     return pl.pallas_call(
         kernel,
         out_shape=outs,
@@ -20,7 +18,7 @@
         out_specs=jax.tree.map(lambda _: VMEM, outs),
         scratch_shapes=scratch,
         compiler_params=pltpu.CompilerParams(vmem_limit_bytes=16 * 1024 * 1024),
-        cost_estimate=pl.CostEstimate(flops=0, bytes_accessed=cost, transcendentals=0),
+        cost_estimate=pl.CostEstimate(flops=flops, bytes_accessed=cost, transcendentals=0),
         name=name,
     )(
         *(pltpu.with_memory_space_constraint(a, pltpu.VMEM) for a in held),
@@ -32,7 +30,16 @@
     return pltpu.VMEM(a.shape, a.dtype)
 
 
-def request_kernel(total_lags, shift, source_ref, offset_ref, delay_ref, history_ref, code_ref, own_ref):
+def request_kernel(total_lags, shift, *refs):
+    code_ref, own_ref, source_ref, offset_ref, delay_ref, sems = refs[4:]
+    copies = [
+        pltpu.make_async_copy(s, t, sems.at[i])
+        for i, (s, t) in enumerate(zip(refs[:4], (source_ref, offset_ref, delay_ref, own_ref)))
+    ]
+    for copy in copies:
+        copy.start()
+    for copy in copies[:3]:
+        copy.wait()
     source = source_ref[...]
     lane = source.shape[1]
     chunk = 128
@@ -44,7 +51,7 @@
     lag = offset_ref[...] + looked
     lag = jnp.where(lag >= total_lags, lag - total_lags, lag)
     code_ref[...] = (lag << shift) | source
-    own_ref[...] = history_ref[...]
+    copies[3].wait()
 
 
 def join_kernel(*refs):
@@ -96,25 +103,48 @@
         (send_ref if d % 2 else keep_ref)[d // 2] = picked
 
 
-def stage_kernel(count, held_ref, *refs):
-    sources, passed_ref, targets, sems = refs[:count], refs[count], refs[count + 1 : -1], refs[-1]
-    copies = [pltpu.make_async_copy(s, t, sems.at[i]) for i, (s, t) in enumerate(zip(sources, targets))]
-    for copy in copies:
+def stage_kernel(first, held_ref, tiles_in, *refs):
+    others = (len(refs) - 4) // 2
+    rest_in, passed_ref, tiles_ref = refs[:others], refs[others], refs[others + 1]
+    rest_ref, buffer, sems = refs[others + 2 : -2], refs[-2], refs[-1]
+    tiles, size = buffer.shape[:2]
+    parts = sems.shape[0] - others
+    width = tiles // parts
+    copies = [
+        pltpu.make_async_copy(
+            tiles_in.at[pl.ds(first + i * width, width)],
+            buffer.at[pl.ds(i * width, width)],
+            sems.at[i],
+        )
+        for i in range(parts)
+    ]
+    rest = [
+        pltpu.make_async_copy(s, t, sems.at[parts + i])
+        for i, (s, t) in enumerate(zip(rest_in, rest_ref))
+    ]
+    for copy in copies + rest:
         copy.start()
     passed_ref[...] = held_ref[...]
-    for copy in copies:
+    for i in range(parts):
+        copies[i].wait()
+        for t in range(i * width, (i + 1) * width):
+            tiles_ref[t * size : (t + 1) * size, :] = jnp.transpose(buffer[t])
+    for copy in rest:
         copy.wait()
 
 
-def couple_kernel(mine_ref, other_ref, tiles_ref, target_ref, incident_ref, inverse_ref, out_ref):
+def couple_kernel(mine_ref, other_ref, run0_ref, target_ref, incident_ref, run1_ref, run2_ref, inverse_ref, out_ref):
     blocks, size = incident_ref.shape
-    tiles = tiles_ref.shape[0]
+    tiles = mine_ref.shape[0]
     vectors = mine_ref[...].astype(jnp.float32) + other_ref[...].astype(jnp.float32)
     target = jnp.transpose(jnp.broadcast_to(target_ref[...], (size, tiles)))
     left = jnp.stack([jnp.where(target == b, vectors, 0.0) for b in range(blocks)], axis=0)
     left = left.astype(jnp.bfloat16).reshape(blocks, tiles * size)
-    right = jnp.concatenate([tiles_ref[t] for t in range(tiles)], axis=1)
-    total = lax.dot_general(left, right, NT_DIMS, preferred_element_type=jnp.float32)
+    total, first = jnp.zeros((blocks, size), jnp.float32), 0
+    for run_ref in (run0_ref, run1_ref, run2_ref):
+        part = left[:, first : first + run_ref.shape[0]]
+        total = total + jnp.dot(part, run_ref[...], preferred_element_type=jnp.float32)
+        first += run_ref.shape[0]
     excite = incident_ref[...] - total
     lane = lax.broadcasted_iota(jnp.int32, (size, blocks), 1)
     solved = jnp.zeros((size, blocks), jnp.float32)
@@ -151,35 +181,56 @@
         lambda *refs: request_kernel(lag_rows * n_lag, shift, *refs),
         "request",
         (pltpu.VMEM((1, tile_count), jnp.int32), in_vmem(history)),
-        loaded=(tile_source[None], tile_offset[None], delay_bins[None], history),
-    )
-
+        left=(tile_source[None], tile_offset[None], delay_bins[None], history),
+        scratch=[
+            pltpu.VMEM((1, tile_count), jnp.int32),
+            pltpu.VMEM((1, tile_count), jnp.int32),
+            pltpu.VMEM((1, all_blocks), jnp.int32),
+            pltpu.SemaphoreType.DMA((4,)),
+        ],
+    )
+
+    for bit in exchange_bits[:-1]:
+        (code,) = call(
+            join_kernel,
+            "join",
+            (pltpu.VMEM((2 * code.shape[0], tile_count), jnp.int32),),
+            held=(code, hop(code, bit)),
+            cost=1 << 28, flops=1<<35,
+        )
+    far_code = hop(code, exchange_bits[-1])
     pieces, arrived = own[None], first
-    for i in range(max(len(exchange_bits), len(gather_bits)) - 1):
-        pairs = []
-        if i < len(exchange_bits) - 1:
-            pairs += [code, hop(code, exchange_bits[i])]
-        if i < len(gather_bits) - 1:
-            pairs += [pieces, arrived]
-        joined = list(
-            call(
-                join_kernel,
-                "join",
-                tuple(
-                    pltpu.VMEM((2 * a.shape[0],) + a.shape[1:], a.dtype) for a in pairs[::2]
-                ),
-                held=tuple(pairs),
-            )
-        )
-        if i < len(exchange_bits) - 1:
-            code = joined.pop(0)
-        if i < len(gather_bits) - 1:
-            pieces = joined.pop(0)
-            arrived = hop(pieces, gather_bits[i + 1])
-    far_code, far_pieces = hop(code, exchange_bits[-1]), arrived
-
-    half = code.shape[0]
-    picked = (half, tile_count, size)
+    for bit in gather_bits[1:]:
+        (pieces,) = call(
+            join_kernel,
+            "gather",
+            (pltpu.VMEM((2 * pieces.shape[0],) + pieces.shape[1:], pieces.dtype),),
+            held=(pieces, arrived),
+        )
+        arrived = hop(pieces, bit)
+    far_pieces = arrived
+
+    cuts = [0, tile_count // 4, tile_count * 5 // 8, tile_count]
+
+    def stage(run, held, *rest):
+        count = cuts[run + 1] - cuts[run]
+        return call(
+            lambda *refs: stage_kernel(cuts[run], *refs),
+            "stage" + str(run),
+            (in_vmem(held), pltpu.VMEM((count * size, size), tile_blocks.dtype))
+            + tuple(in_vmem(a) for a in rest),
+            held=(held,),
+            left=(tile_blocks,) + rest,
+            scratch=[
+                pltpu.VMEM((count, size, size), tile_blocks.dtype),
+                pltpu.SemaphoreType.DMA((max(count // 16, 1) + len(rest),)),
+            ],
+            cost=count * size * size * 2,
+        )
+
+    code, *staged = stage(0, code, tile_target[None], incident.reshape(slab_blocks, size))
+
+    picked = (code.shape[0], tile_count, size)
     keep, send = call(
         lambda *refs: select_kernel((size, slab_shift, shift, lag_rows, crossed), *refs),
         "select",
@@ -187,21 +238,21 @@
         held=(code, far_code, pieces, far_pieces),
     )
 
-    late = (tile_blocks, tile_target[None], incident.reshape(slab_blocks, size), self_inv)
-    keep, *staged = call(
-        lambda *refs: stage_kernel(len(late), *refs),
-        "stage",
-        tuple(in_vmem(a) for a in (keep,) + late),
-        held=(keep,),
-        left=late,
-        scratch=[pltpu.SemaphoreType.DMA((len(late),))],
-        cost=tile_blocks.size * 2,
-    )
-
+    ended = []
     for bit in exchange_bits:
-        held = keep + hop(send, bit)
-        keep, send = held[0::2], held[1::2]
-    mine = held.reshape(tile_count, size)
+        if send.shape[0] > 1:
+            passed = hop(send[1:], bit)
+            ended.append(hop(send[:1], bit))
+            if bit == exchange_bits[0]:
+                keep, *more = stage(1, keep)
+                staged += more
+            send = keep[1::2] + passed[0::2]
+            keep = jnp.concatenate([keep[:1], keep[2::2] + passed[1::2]], axis=0)
+        else:
+            keep, *more = stage(2, keep, self_inv)
+            staged += more
+            ended.append(hop(send, bit))
+    mine = sum(ended, keep).reshape(tile_count, size)
     if n_lag == 2:
         other = lax.ppermute(mine, "lag", [(0, 1), (1, 0)])
     else:

time: 24.8 us -> 22.9 us (0.923)
  waiting for transfers between devices: 6.46 us -> 1.04 us
  Pallas kernels: 6.09 us -> 7.87 us
  starting transfers between devices: 12.1 us -> 13.7 us
    ppermute x6 -> x7, waiting for transfers between devices: 5.38 us -> 0.12 us  [hop(): return lax.ppermute(value, ('blk', 'lag'), pairs)]
    pallas_call x5 -> x8, Pallas kernels: 6.09 us -> 7.87 us  [call(): pl.pallas_call(kernel, out_shape=outs, in_specs=[VMEM] * (len(held) + len...]
    ppermute x6 -> x7, starting transfers between devices: 11.9 us -> 13.3 us  [hop(): return lax.ppermute(value, ('blk', 'lag'), pairs)]
  transfers between devices with their start and end apart: 7 -> 8, of which waited for: 5 -> 2; matrix products, arithmetic and copies ran while one was open for 0% -> 0% of each run, Pallas kernels for 14% -> 25%
where the time goes in v3:
time: 22.9 us; the launch traced here: 22.7 us
  starting transfers between devices  13.7 us (60%)
  Pallas kernels  7.87 us (34%)
  waiting for transfers between devices  1.04 us (5%)
    ppermute x7, starting transfers between devices, hop(): return lax.ppermute(value, ('blk', 'lag'), pairs)  13.3 us
    pallas_call x8, Pallas kernels, call(): pl.pallas_call(kernel, out_shape=outs, in_specs=[VMEM] * (len(held) + len...  7.87 us
    ppermute x1, waiting for transfers between devices, body(): other = lax.ppermute(mine, 'lag', [(0, 1), (1, 0)])  0.92 us
  transfers between devices with their start and end apart: 8, of which 2 were waited for; matrix products, arithmetic and copies ran while one was open for 0% of the time, Pallas kernels for 25%

profile of v3, /device:TPU:0, one launch (start us, length us, event | category | flops | bytes accessed | tf_op | source)
XLA Modules:
  0.0 22.7 jit_solution(16701580009410862835)
XLA Ops:
  0.0 2.4 %collective-permute-start.2 = (bf16[1,32,1024]{2,1,0:T(8,128)(2,1)}, bf16[1,32,1024]{2,1,0:T(8,128)(2,1)S(1)}, u32[]{:S(2)}, u32[]{:S(2)}) collective-permute-start(bf16[1,32,1024]{2,1,0:T(8,128)(2,1)} %bitcast.11), channel_id=1, source_target_pairs={{0,3},{1,2},{2,1},{3,0},{4,7},{5,6},{6,5},{7,4},{8,11},{9,10},{10,... | collective-permute-start | bytes 196616 | tf_op jit(solution)/shard_map/ppermute | solution.py:177
  2.4 0.9 %request.1 = (s32[1,128]{1,0:T(1,128)S(1)}, bf16[32,1024]{1,0:T(8,128)(2,1)S(1)}) custom-call(s32[1,128]{1,0:T(1,128)} %bitcast.13, s32[1,128]{1,0:T(1,128)} %bitcast.14, s32[1,128]{1,0:T(1,128)} %bitcast.15, bf16[32,1024]{1,0:T(8,128)(2,1)} %refs_3_.1), custom_call_target="tpu_custom_call" | custom-call | tf_op jit(solution)/shard_map/request/pallas_call | solution.py:14
  3.3 1.9 %collective-permute-start = (s32[1,128]{1,0:T(1,128)S(1)}, s32[1,128]{1,0:T(1,128)S(1)}, u32[]{:S(2)}, u32[]{:S(2)}) collective-permute-start(s32[1,128]{1,0:T(1,128)S(1)} %get-tuple-element.18.refs_0_), channel_id=1, source_target_pairs={{0,9},{1,8},{2,11},{3,10},{4,13},{5,12},{6,15},{7,14},{8,1},{9,0},... | collective-permute-start | bytes 1544 | tf_op jit(solution)/shard_map/ppermute | solution.py:177
  5.3 0.0 collective-permute-done.2.refs_1_
  5.3 2.1 %collective-permute-start.3 = (bf16[2,32,1024]{2,1,0:T(8,128)(2,1)S(1)}, bf16[2,32,1024]{2,1,0:T(8,128)(2,1)S(1)}, u32[]{:S(2)}, u32[]{:S(2)}) collective-permute-start(bf16[2,32,1024]{2,1,0:T(8,128)(2,1)S(1)} %gather.1.refs_2_), channel_id=1, source_target_pairs={{0,5},{1,4},{2,7},{3,6},{4,1},{5,0},{6,3},{7,2},{8,13},{9,12},{10,... | collective-permute-start | bytes 393224 | tf_op jit(solution)/shard_map/ppermute | solution.py:177
  7.3 0.0 collective-permute-done.refs_1_
  7.3 2.6 %collective-permute-start.1 = (s32[2,128]{1,0:T(2,128)S(1)}, s32[2,128]{1,0:T(2,128)S(1)}, u32[]{:S(2)}, u32[]{:S(2)}) collective-permute-start(s32[2,128]{1,0:T(2,128)S(1)} %join.1.refs_0_), channel_id=1, source_target_pairs={{0,17},{1,16},{2,19},{3,18},{4,21},{5,20},{6,23},{7,22},{8,25},{9,... | collective-permute-start | bytes 3080 | tf_op jit(solution)/shard_map/ppermute | solution.py:177
  10.0 1.5 %stage0.1 = (s32[2,128]{1,0:T(2,128)S(1)}, bf16[4096,128]{1,0:T(8,128)(2,1)S(1)}, s32[1,128]{1,0:T(1,128)S(1)}, f32[8,128]{1,0:T(8,128)S(1)}) custom-call(s32[2,128]{1,0:T(2,128)S(1)} %join.1.refs_0_, bf16[128,128,128]{2,1,0:T(8,128)(2,1)} %refs_1_.5, s32[1,128]{1,0:T(1,128)} %bitcast.16, f32[8,128]{1,0:T(8,128)} %bitcast.12), custom_call_target="tpu_custom_call" | custom-call | bytes 1048576 | tf_op jit(solution)/shard_map/stage0/pallas_call | solution.py:14
  11.4 0.0 collective-permute-done.1.refs_1_
  11.4 0.0 collective-permute-done.3.refs_3_
  11.4 0.6 %select.1 = (bf16[2,128,128]{2,1,0:T(8,128)(2,1)S(1)}, bf16[2,128,128]{2,1,0:T(8,128)(2,1)S(1)}) custom-call(s32[2,128]{1,0:T(2,128)S(1)} %get-tuple-element.19.refs_0_, s32[2,128]{1,0:T(2,128)S(1)} %collective-permute-done.1.refs_1_, bf16[2,32,1024]{2,1,0:T(8,128)(2,1)S(1)} %gather.1.refs_2_, bf16[2,32,1024]{2,1,0:T(8,128)(2,1)S(1)} %collective-permute-done.3.refs_3_), custom_call_target="tpu_custom_call" | custom-call | tf_op jit(solution)/shard_map/select/pallas_call | solution.py:14
  12.0 1.5 %collective-permute-start.5 = (bf16[1,128,128]{2,1,0:T(8,128)(2,1)S(1)}, bf16[1,128,128]{2,1,0:T(8,128)(2,1)S(1)}, u32[]{:S(2)}, u32[]{:S(2)}) collective-permute-start(bf16[1,128,128]{2,1,0:T(8,128)(2,1)S(1)} %get-tuple-element.32), channel_id=1, source_target_pairs={{0,9},{1,8},{2,11},{3,10},{4,13},{5,12},{6,15},{7,14},{8,1},{9,0},... | collective-permute-start | bytes 98312 | tf_op jit(solution)/shard_map/ppermute | solution.py:177
  13.5 0.3 %collective-permute-start.4 = (bf16[1,128,128]{2,1,0:T(8,128)(2,1)S(1)}, bf16[1,128,128]{2,1,0:T(8,128)(2,1)S(1)}, u32[]{:S(2)}, u32[]{:S(2)}) collective-permute-start(bf16[1,128,128]{2,1,0:T(8,128)(2,1)S(1)} %get-tuple-element.31), channel_id=1, source_target_pairs={{0,9},{1,8},{2,11},{3,10},{4,13},{5,12},{6,15},{7,14},{8,1},{9,0},... | collective-permute-start | bytes 98312 | tf_op jit(solution)/shard_map/ppermute | solution.py:177
  13.9 1.6 %stage1.1 = (bf16[2,128,128]{2,1,0:T(8,128)(2,1)S(1)}, bf16[6144,128]{1,0:T(8,128)(2,1)S(1)}) custom-call(bf16[2,128,128]{2,1,0:T(8,128)(2,1)S(1)} %get-tuple-element.21.refs_0_, bf16[128,128,128]{2,1,0:T(8,128)(2,1)} %refs_1_.5), custom_call_target="tpu_custom_call" | custom-call | bytes 1572864 | tf_op jit(solution)/shard_map/stage1/pallas_call | solution.py:14
  15.5 0.0 collective-permute-done.5
  15.5 2.5 %collective-permute-start.6 = (bf16[1,128,128]{2,1,0:T(8,128)(2,1)S(1)}, bf16[1,128,128]{2,1,0:T(8,128)(2,1)S(1)}, u32[]{:S(2)}, u32[]{:S(2)}) collective-permute-start(bf16[1,128,128]{2,1,0:T(8,128)(2,1)S(1)} %get-tuple-element.34), channel_id=1, source_target_pairs={{0,17},{1,16},{2,19},{3,18},{4,21},{5,20},{6,23},{7,22},{8,25},{9,... | collective-permute-start | bytes 98312 | tf_op jit(solution)/shard_map/ppermute | solution.py:177
  18.1 1.6 %stage2.1 = (bf16[1,128,128]{2,1,0:T(8,128)(2,1)S(1)}, bf16[6144,128]{1,0:T(8,128)(2,1)S(1)}, f32[8,128,128]{2,1,0:T(8,128)S(1)}) custom-call(bf16[1,128,128]{2,1,0:T(8,128)(2,1)S(1)} %get-tuple-element.33.refs_0_, bf16[128,128,128]{2,1,0:T(8,128)(2,1)} %refs_1_.5, f32[8,128,128]{2,1,0:T(8,128)} %refs_2_.1), custom_call_target="tpu_custom_call" | custom-call | bytes 1572864 | tf_op jit(solution)/shard_map/stage2/pallas_call | solution.py:14
  19.7 0.0 collective-permute-done.4
  19.7 0.1 collective-permute-done.6
  19.8 0.3 %collective-permute-start.7 = (bf16[128,128]{1,0:T(8,128)(2,1)S(1)}, bf16[128,128]{1,0:T(8,128)(2,1)S(1)}, u32[]{:S(2)}, u32[]{:S(2)}) collective-permute-start(bf16[128,128]{1,0:T(8,128)(2,1)S(1)} %add_bitcast_fusion.mine_ref), channel_id=1, source_target_pairs={{0,1},{1,0},{2,3},{3,2},{4,5},{5,4},{6,7},{7,6},{8,9},{9,8},{10,11... | collective-permute-start | bytes 98312 | tf_op jit(solution)/shard_map/ppermute | solution.py:257
  20.2 0.9 %collective-permute-done.7.other_ref = bf16[128,128]{1,0:T(8,128)(2,1)S(1)} collective-permute-done((bf16[128,128]{1,0:T(8,128)(2,1)S(1)}, bf16[128,128]{1,0:T(8,128)(2,1)S(1)}, u32[]{:S(2)}, u32[]{:S(2)}) %collective-permute-start.7) | collective-permute-done | bytes 32800 | tf_op jit(solution)/shard_map/ppermute | solution.py:257
  21.1 1.6 %couple.1 = f32[8,128]{1,0:T(8,128)} custom-call(bf16[128,128]{1,0:T(8,128)(2,1)S(1)} %add_bitcast_fusion.mine_ref, bf16[128,128]{1,0:T(8,128)(2,1)S(1)} %collective-permute-done.7.other_ref, bf16[4096,128]{1,0:T(8,128)(2,1)S(1)} %get-tuple-element.25.run0_ref, s32[1,128]{1,0:T(1,128)S(1)} %get-tuple-element.26.target_ref, ...), custom_call_target="tpu_custom_call" | custom-call | tf_op jit(solution)/shard_map/couple/pallas_call | solution.py:14
  (5 shorter events, 0.0 us)
Async XLA Ops:
  0.0 5.3 %collective-permute-start.2 = (bf16[1,32,1024]{2,1,0:T(8,128)(2,1)}, bf16[1,32,1024]{2,1,0:T(8,128)(2,1)S(1)}, u32[]{:S(2)}, u32[]{:S(2)}) collective-permute-start(bf16[1,32,1024]{2,1,0:T(8,128)(2,1)} %bitcast.11), channel_id=1, source_target_pairs={{0,3},{1,2},{2,1},{3,0},{4,7},{5,6},{6,5},{7,4},{8,11},{9,10},{10,... | collective-permute-start | bytes 196616 | tf_op jit(solution)/shard_map/ppermute | solution.py:177
  3.3 4.0 %collective-permute-start = (s32[1,128]{1,0:T(1,128)S(1)}, s32[1,128]{1,0:T(1,128)S(1)}, u32[]{:S(2)}, u32[]{:S(2)}) collective-permute-start(s32[1,128]{1,0:T(1,128)S(1)} %get-tuple-element.18.refs_0_), channel_id=1, source_target_pairs={{0,9},{1,8},{2,11},{3,10},{4,13},{5,12},{6,15},{7,14},{8,1},{9,0},... | collective-permute-start | bytes 1544 | tf_op jit(solution)/shard_map/ppermute | solution.py:177
  5.3 6.2 %collective-permute-start.3 = (bf16[2,32,1024]{2,1,0:T(8,128)(2,1)S(1)}, bf16[2,32,1024]{2,1,0:T(8,128)(2,1)S(1)}, u32[]{:S(2)}, u32[]{:S(2)}) collective-permute-start(bf16[2,32,1024]{2,1,0:T(8,128)(2,1)S(1)} %gather.1.refs_2_), channel_id=1, source_target_pairs={{0,5},{1,4},{2,7},{3,6},{4,1},{5,0},{6,3},{7,2},{8,13},{9,12},{10,... | collective-permute-start | bytes 393224 | tf_op jit(solution)/shard_map/ppermute | solution.py:177
  7.3 4.1 %collective-permute-start.1 = (s32[2,128]{1,0:T(2,128)S(1)}, s32[2,128]{1,0:T(2,128)S(1)}, u32[]{:S(2)}, u32[]{:S(2)}) collective-permute-start(s32[2,128]{1,0:T(2,128)S(1)} %join.1.refs_0_), channel_id=1, source_target_pairs={{0,17},{1,16},{2,19},{3,18},{4,21},{5,20},{6,23},{7,22},{8,25},{9,... | collective-permute-start | bytes 3080 | tf_op jit(solution)/shard_map/ppermute | solution.py:177
  12.0 3.5 %collective-permute-start.5 = (bf16[1,128,128]{2,1,0:T(8,128)(2,1)S(1)}, bf16[1,128,128]{2,1,0:T(8,128)(2,1)S(1)}, u32[]{:S(2)}, u32[]{:S(2)}) collective-permute-start(bf16[1,128,128]{2,1,0:T(8,128)(2,1)S(1)} %get-tuple-element.32), channel_id=1, source_target_pairs={{0,9},{1,8},{2,11},{3,10},{4,13},{5,12},{6,15},{7,14},{8,1},{9,0},... | collective-permute-start | bytes 98312 | tf_op jit(solution)/shard_map/ppermute | solution.py:177
  13.5 6.2 %collective-permute-start.4 = (bf16[1,128,128]{2,1,0:T(8,128)(2,1)S(1)}, bf16[1,128,128]{2,1,0:T(8,128)(2,1)S(1)}, u32[]{:S(2)}, u32[]{:S(2)}) collective-permute-start(bf16[1,128,128]{2,1,0:T(8,128)(2,1)S(1)} %get-tuple-element.31), channel_id=1, source_target_pairs={{0,9},{1,8},{2,11},{3,10},{4,13},{5,12},{6,15},{7,14},{8,1},{9,0},... | collective-permute-start | bytes 98312 | tf_op jit(solution)/shard_map/ppermute | solution.py:177
  15.5 4.3 %collective-permute-start.6 = (bf16[1,128,128]{2,1,0:T(8,128)(2,1)S(1)}, bf16[1,128,128]{2,1,0:T(8,128)(2,1)S(1)}, u32[]{:S(2)}, u32[]{:S(2)}) collective-permute-start(bf16[1,128,128]{2,1,0:T(8,128)(2,1)S(1)} %get-tuple-element.34), channel_id=1, source_target_pairs={{0,17},{1,16},{2,19},{3,18},{4,21},{5,20},{6,23},{7,22},{8,25},{9,... | collective-permute-start | bytes 98312 | tf_op jit(solution)/shard_map/ppermute | solution.py:177
  19.8 1.3 %collective-permute-start.7 = (bf16[128,128]{1,0:T(8,128)(2,1)S(1)}, bf16[128,128]{1,0:T(8,128)(2,1)S(1)}, u32[]{:S(2)}, u32[]{:S(2)}) collective-permute-start(bf16[128,128]{1,0:T(8,128)(2,1)S(1)} %add_bitcast_fusion.mine_ref), channel_id=1, source_target_pairs={{0,1},{1,0},{2,3},{3,2},{4,5},{5,4},{6,7},{7,6},{8,9},{9,8},{10,11... | collective-permute-start | bytes 98312 | tf_op jit(solution)/shard_map/ppermute | solution.py:257

commit v4 on v2

v4 whole, which is shorter than its diff:
```python
import jax
import jax.numpy as jnp
from jax import lax
from jax.experimental import pallas as pl
from jax.experimental.pallas import tpu as pltpu
from jax.sharding import PartitionSpec as P


VMEM = pl.BlockSpec(memory_space=pltpu.VMEM)


def call(kernel, name, outs, *operands, weight=0):
    return pl.pallas_call(
        kernel,
        out_shape=outs,
        in_specs=[VMEM] * len(operands),
        out_specs=jax.tree.map(lambda _: VMEM, outs),
        compiler_params=pltpu.CompilerParams(vmem_limit_bytes=16 * 1024 * 1024),
        cost_estimate=pl.CostEstimate(
            flops=weight << 32, bytes_accessed=weight << 24, transcendentals=0
        ),
        name=name,
    )(*(pltpu.with_memory_space_constraint(a, pltpu.VMEM) for a in operands))


def in_vmem(a):
    return pltpu.VMEM(a.shape, a.dtype)


def ids_kernel(out_ref):
    out_ref[...] = lax.broadcasted_iota(jnp.int32, out_ref.shape, 0)


def request_kernel(total_lags, shift, ids_ref, source_ref, offset_ref, delay_ref, code_ref):
    source = source_ref[...]
    chunk, lane = ids_ref.shape
    looked = jnp.zeros_like(source)
    for first in range(0, delay_ref.shape[1], chunk):
        delay = jnp.transpose(jnp.broadcast_to(delay_ref[:, first : first + chunk], (lane, chunk)))
        block = ids_ref[...] + first
        looked = looked + jnp.sum(jnp.where(block == source, delay, 0), axis=0, keepdims=True)
    lag = offset_ref[...] + looked
    lag = jnp.where(lag >= total_lags, lag - total_lags, lag)
    code_ref[...] = (lag << shift) | source


def join_kernel(mine_ref, other_ref, out_ref):
    rows = mine_ref.shape[0]
    out_ref[:rows] = mine_ref[...]
    out_ref[rows:] = other_ref[...]


def select_kernel(plan, places, near_ref, far_ref, near_pieces_ref, far_pieces_ref, *out_refs):
    size, slab_shift, shift, lag_shift, split = plan
    blk, lag = lax.axis_index("blk"), lax.axis_index("lag")
    slabs = [r[q] for r in (near_pieces_ref, far_pieces_ref) for q in range(r.shape[0])]
    width = slabs[0].shape[1]
    table = jnp.concatenate(
        [s[:, b : b + size] for s in slabs for b in range(0, width, size)], axis=0
    )
    code = jnp.concatenate([near_ref[...], far_ref[...]], axis=0)
    tiles = code.shape[1]
    source = code & ((1 << shift) - 1)
    wanted = code >> shift
    piece = (source >> slab_shift) ^ blk
    half = wanted >> lag_shift
    if split:
        low, high = split
        same, turn = half == lag, jnp.where(lag == 0, low, high)
        slab = jnp.where((piece == 0) & same, 0, -1)
        slab = jnp.where(piece == turn, jnp.where(same, 1, 2), slab)
        slab = jnp.where((piece == low + high) & jnp.logical_not(same), 3, slab)
    else:
        slab = jnp.where((piece < len(slabs)) & (half == lag), piece, -1)
    within = ((source & ((1 << slab_shift) - 1)) << lag_shift) + (wanted & ((1 << lag_shift) - 1))
    row = (slab << (slab_shift + lag_shift)) + within
    row = jnp.where(slab >= 0, row, -1)
    lane = lax.broadcasted_iota(jnp.int32, (tiles, size), 1)
    for d, out, index in places:
        mine = jnp.transpose(jnp.broadcast_to(row[d : d + 1, :], (size, tiles)))
        onehot = jnp.concatenate(
            [
                jnp.where(mine == lane + first, 1.0, 0.0).astype(jnp.bfloat16)
                for first in range(0, table.shape[0], size)
            ],
            axis=1,
        )
        picked = jnp.dot(onehot, table, preferred_element_type=jnp.float32)
        out_refs[out][index] = picked.astype(jnp.bfloat16)


def turn_kernel(held_ref, tiles_ref, passed_ref, turned_ref):
    tiles, size = tiles_ref.shape[:2]
    passed_ref[...] = held_ref[...]
    for t in range(tiles):
        turned_ref[t * size : (t + 1) * size, :] = jnp.transpose(tiles_ref[t])


def couple_kernel(
    mine_ref, other_ref, turned_ref, target_ref, incident_ref, inverse_ref, out_ref
):
    blocks, size = incident_ref.shape
    tiles = mine_ref.shape[0]
    vectors = mine_ref[...].astype(jnp.float32) + other_ref[...].astype(jnp.float32)
    target = jnp.transpose(jnp.broadcast_to(target_ref[...], (size, tiles)))
    left = jnp.stack([jnp.where(target == b, vectors, 0.0) for b in range(blocks)], axis=0)
    left = left.astype(jnp.bfloat16).reshape(blocks, tiles * size)
    total = jnp.dot(left, turned_ref[...], preferred_element_type=jnp.float32)
    excite = incident_ref[...] - total
    lane = lax.broadcasted_iota(jnp.int32, (size, blocks), 1)
    solved = jnp.zeros((size, blocks), jnp.float32)
    for b in range(blocks):
        product = inverse_ref[b] * jnp.broadcast_to(excite[b : b + 1, :], (size, size))
        solved = jnp.where(lane == b, jnp.sum(product, axis=1, keepdims=True), solved)
    out_ref[...] = jnp.transpose(solved)


def body(
    history, tile_blocks, tile_target, tile_source, tile_offset, delay_bins, incident, self_inv
):
    lag_rows = history.shape[0]
    tile_count, size = tile_blocks.shape[:2]
    slab_blocks = self_inv.shape[0]
    n_blk, n_lag = lax.axis_size("blk"), lax.axis_size("lag")
    all_blocks = delay_bins.shape[0]
    bits = n_blk.bit_length() - 1
    shift = all_blocks.bit_length() - 1
    slab_shift = slab_blocks.bit_length() - 1
    gather_bits = [1 << i for i in range(bits // 2)]
    exchange_bits = [1 << i for i in range(bits // 2, bits)]
    lag_shift = lag_rows.bit_length() - 1
    paired = n_lag == 2 and len(gather_bits) == 2

    def hop(value, bit, other=None, flip=1):
        bits_of, flip = [bit, bit if other is None else other], flip if paired else 0
        pairs = [
            (j * n_lag + c, (j ^ bits_of[c % 2]) * n_lag + (c ^ flip))
            for j in range(n_blk)
            for c in range(n_lag)
        ]
        return lax.ppermute(value, ("blk", "lag"), pairs)

    if paired:
        first = hop(history[None], *gather_bits, flip=0)
    else:
        first = hop(history[None], gather_bits[0])
    ids = call(ids_kernel, "ids", pltpu.VMEM((min(all_blocks, 128), tile_count), jnp.int32), weight=8)
    code = call(
        lambda *refs: request_kernel(lag_rows * n_lag, shift, *refs),
        "request",
        pltpu.VMEM((1, tile_count), jnp.int32),
        ids,
        tile_source[None],
        tile_offset[None],
        delay_bins[None],
    )

    def join(name, mine, other, weight):
        shape = (2 * mine.shape[0],) + mine.shape[1:]
        return call(join_kernel, name, pltpu.VMEM(shape, mine.dtype), mine, other, weight=weight)

    for bit in exchange_bits[:0:-1]:
        code = join("join", code, hop(code, bit), 8)
    far_code = hop(code, exchange_bits[0])
    pieces, arrived = history[None], first
    for bit in gather_bits[1:]:
        pieces = join("gather", pieces, arrived, 0)
        arrived = hop(pieces, bit, gather_bits[0]) if paired else hop(pieces, bit)

    half = code.shape[0]
    plan = (size, slab_shift, shift, lag_shift, gather_bits if paired else None)

    def select(name, sizes, places, weight):
        places = [
            (sum(((d >> i) & 1) << (len(exchange_bits) - 1 - i) for i in range(len(exchange_bits))), out, k)
            for d, out, k in places
        ]
        return call(
            lambda *refs: select_kernel(plan, places, *refs),
            name,
            [pltpu.VMEM((n, tile_count, size), jnp.bfloat16) for n in sizes],
            code,
            far_code,
            pieces,
            arrived,
            weight=weight,
        )

    (send,) = select("select_send", [half - 1], [(2 * k + 1, 0, k - 1) for k in range(1, half)], 16)
    direct, keep = select(
        "select_keep", [1, half], [(1, 0, 0)] + [(2 * k, 1, k) for k in range(half)], 16
    )

    ended = []
    for bit in exchange_bits:
        if keep.shape[0] > 1:
            passed = hop(send, bit)
            ended.append(hop(direct, bit))
            onward = keep[1::2] + passed[0::2]
            direct, send = onward[:1], onward[1:]
            keep = jnp.concatenate([keep[:1], keep[2::2] + passed[1::2]], axis=0)
        else:
            keep, turned = call(
                turn_kernel,
                "turn",
                (in_vmem(keep), pltpu.VMEM((tile_count * size, size), tile_blocks.dtype)),
                keep,
                tile_blocks,
                weight=4,
            )
            ended.append(hop(direct, bit))
    mine = sum(ended, keep).reshape(tile_count, size)
    if n_lag == 2:
        other = lax.ppermute(mine, "lag", [(0, 1), (1, 0)])
    else:
        other = lax.psum(mine, "lag") - mine

    solved = call(
        couple_kernel,
        "couple",
        jax.ShapeDtypeStruct((slab_blocks, size), jnp.float32),
        mine,
        other,
        turned,
        tile_target[None],
        incident.reshape(slab_blocks, size),
        self_inv,
    )
    return solved.reshape(slab_blocks * size)


def solution(mesh):
    return jax.shard_map(
        body,
        mesh=mesh,
        in_specs=(
            P("lag", "blk"),
            P("blk", None, None),
            P("blk"),
            P("blk"),
            P("blk"),
            P(),
            P("blk"),
            P("blk", None, None),
        ),
        out_specs=P("blk"),
        check_vma=False,
    )
```

time: 24.8 us -> 21.5 us (0.87)
  Pallas kernels: 6.09 us -> 3.61 us
  waiting for transfers between devices: 6.46 us -> 4.13 us
  starting transfers between devices: 12.1 us -> 13.4 us
    pallas_call x5 -> x8, Pallas kernels: 6.09 us -> 3.61 us  [call(): pl.pallas_call(kernel, out_shape=outs, in_specs=[VMEM] * len(operands), o...]
    ppermute x6 -> x7, waiting for transfers between devices: 5.38 us -> 3.27 us  [hop(): return lax.ppermute(value, ('blk', 'lag'), pairs)]
    ppermute x6 -> x7, starting transfers between devices: 11.9 us -> 12.9 us  [hop(): return lax.ppermute(value, ('blk', 'lag'), pairs)]
    ppermute x1, starting transfers between devices: 0.12 us -> 0.5 us  [body(): other = lax.ppermute(mine, 'lag', [(0, 1), (1, 0)])]
  transfers between devices with their start and end apart: 7 -> 8, of which waited for: 5 -> 5; matrix products, arithmetic and copies ran while one was open for 0% -> 0% of each run, Pallas kernels for 14% -> 8%
where the time goes in v4:
time: 21.5 us; the launch traced here: 21.3 us
  starting transfers between devices  13.4 us (62%)
  waiting for transfers between devices  4.13 us (19%)
  Pallas kernels  3.61 us (17%)
    ppermute x7, starting transfers between devices, hop(): return lax.ppermute(value, ('blk', 'lag'), pairs)  12.9 us
    pallas_call x8, Pallas kernels, call(): pl.pallas_call(kernel, out_shape=outs, in_specs=[VMEM] * len(operands), o...  3.61 us
    ppermute x7, waiting for transfers between devices, hop(): return lax.ppermute(value, ('blk', 'lag'), pairs)  3.27 us
    ppermute x1, waiting for transfers between devices, body(): other = lax.ppermute(mine, 'lag', [(0, 1), (1, 0)])  0.86 us
    ppermute x1, starting transfers between devices, body(): other = lax.ppermute(mine, 'lag', [(0, 1), (1, 0)])  0.5 us
  transfers between devices with their start and end apart: 8, of which 5 were waited for; matrix products, arithmetic and copies ran while one was open for 0% of the time, Pallas kernels for 8%

profile of v4, /device:TPU:0, one launch (start us, length us, event | category | flops | bytes accessed | tf_op | source)
XLA Modules:
  0.0 21.3 jit_solution(12174225350421259991)
XLA Ops:
  0.0 0.0 copy-start.3
  0.0 0.0 copy-start.4
  0.0 3.0 %collective-permute-start.2 = (bf16[1,32,1024]{2,1,0:T(8,128)(2,1)}, bf16[1,32,1024]{2,1,0:T(8,128)(2,1)S(1)}, u32[]{:S(2)}, u32[]{:S(2)}) collective-permute-start(bf16[1,32,1024]{2,1,0:T(8,128)(2,1)} %bitcast.9), channel_id=1, source_target_pairs={{0,2},{1,5},{2,0},{3,7},{4,6},{5,1},{6,4},{7,3},{8,10},{9,13},{10,... | collective-permute-start | bytes 196616 | tf_op jit(solution)/shard_map/ppermute | solution.py:141
  3.0 0.0 copy-done.3
  3.0 0.0 copy-done.4
  3.0 0.0 copy-done.5
  3.1 0.1 request.1.mine_ref
  3.2 1.8 %collective-permute-start = (s32[1,128]{1,0:T(1,128)S(1)}, s32[1,128]{1,0:T(1,128)S(1)}, u32[]{:S(2)}, u32[]{:S(2)}) collective-permute-start(s32[1,128]{1,0:T(1,128)S(1)} %request.1.mine_ref), channel_id=1, source_target_pairs={{0,17},{1,16},{2,19},{3,18},{4,21},{5,20},{6,23},{7,22},{8,25},{9,... | collective-permute-start | bytes 1544 | tf_op jit(solution)/shard_map/ppermute | solution.py:141
  5.0 0.5 %collective-permute-done.2.other_ref = bf16[1,32,1024]{2,1,0:T(8,128)(2,1)S(1)} collective-permute-done((bf16[1,32,1024]{2,1,0:T(8,128)(2,1)}, bf16[1,32,1024]{2,1,0:T(8,128)(2,1)S(1)}, u32[]{:S(2)}, u32[]{:S(2)}) %collective-permute-start.2) | collective-permute-done | bytes 65568 | tf_op jit(solution)/shard_map/ppermute | solution.py:141
  5.5 0.0 copy-done.1
  5.5 1.6 %collective-permute-start.3 = (bf16[2,32,1024]{2,1,0:T(8,128)(2,1)S(1)}, bf16[2,32,1024]{2,1,0:T(8,128)(2,1)S(1)}, u32[]{:S(2)}, u32[]{:S(2)}) collective-permute-start(bf16[2,32,1024]{2,1,0:T(8,128)(2,1)S(1)} %gather.1.refs_2_), channel_id=1, source_target_pairs={{0,5},{1,2},{2,7},{3,0},{4,1},{5,6},{6,3},{7,4},{8,13},{9,10},{10,... | collective-permute-start | bytes 393224 | tf_op jit(solution)/shard_map/ppermute | solution.py:141
  7.1 0.0 collective-permute-done.other_ref
  7.1 1.7 %collective-permute-start.1 = (s32[2,128]{1,0:T(2,128)S(1)}, s32[2,128]{1,0:T(2,128)S(1)}, u32[]{:S(2)}, u32[]{:S(2)}) collective-permute-start(s32[2,128]{1,0:T(2,128)S(1)} %join.1.refs_0_), channel_id=1, source_target_pairs={{0,9},{1,8},{2,11},{3,10},{4,13},{5,12},{6,15},{7,14},{8,1},{9,0},... | collective-permute-start | bytes 3080 | tf_op jit(solution)/shard_map/ppermute | solution.py:141
  8.9 1.3 %collective-permute-done.1.refs_1_ = s32[2,128]{1,0:T(2,128)S(1)} collective-permute-done((s32[2,128]{1,0:T(2,128)S(1)}, s32[2,128]{1,0:T(2,128)S(1)}, u32[]{:S(2)}, u32[]{:S(2)}) %collective-permute-start.1) | collective-permute-done | bytes 1056 | tf_op jit(solution)/shard_map/ppermute | solution.py:141
  10.2 0.0 collective-permute-done.3.refs_3_
  10.2 0.3 %select_send.1 = bf16[1,128,128]{2,1,0:T(8,128)(2,1)S(1)} custom-call(s32[2,128]{1,0:T(2,128)S(1)} %join.1.refs_0_, s32[2,128]{1,0:T(2,128)S(1)} %collective-permute-done.1.refs_1_, bf16[2,32,1024]{2,1,0:T(8,128)(2,1)S(1)} %gather.1.refs_2_, bf16[2,32,1024]{2,1,0:T(8,128)(2,1)S(1)} %collective-permute-done.3.refs_3_), custom_call_target="tpu_custom_call" | custom-call | flops 68719476736 | bytes 268435456 | tf_op jit(solution)/shard_map/select_send/pallas_call | solution.py:13
  10.5 0.0 copy-start.7
  10.5 1.8 %collective-permute-start.5 = (bf16[1,128,128]{2,1,0:T(8,128)(2,1)S(1)}, bf16[1,128,128]{2,1,0:T(8,128)(2,1)S(1)}, u32[]{:S(2)}, u32[]{:S(2)}) collective-permute-start(bf16[1,128,128]{2,1,0:T(8,128)(2,1)S(1)} %select_send.1), channel_id=1, source_target_pairs={{0,9},{1,8},{2,11},{3,10},{4,13},{5,12},{6,15},{7,14},{8,1},{9,0},... | collective-permute-start | bytes 98312 | tf_op jit(solution)/shard_map/ppermute | solution.py:141
  12.2 0.5 %select_keep.1 = (bf16[1,128,128]{2,1,0:T(8,128)(2,1)S(1)}, bf16[2,128,128]{2,1,0:T(8,128)(2,1)S(1)}) custom-call(s32[2,128]{1,0:T(2,128)S(1)} %join.1.refs_0_, s32[2,128]{1,0:T(2,128)S(1)} %collective-permute-done.1.refs_1_, bf16[2,32,1024]{2,1,0:T(8,128)(2,1)S(1)} %gather.1.refs_2_, bf16[2,32,1024]{2,1,0:T(8,128)(2,1)S(1)} %collective-permute-done.3.refs_3_), custom_call_target="tpu_custom_call" | custom-call | flops 68719476736 | bytes 268435456 | tf_op jit(solution)/shard_map/select_keep/pallas_call | solution.py:13
  12.7 0.1 collective-permute-start.4
  12.8 1.1 %collective-permute-done.5 = bf16[1,128,128]{2,1,0:T(8,128)(2,1)S(1)} collective-permute-done((bf16[1,128,128]{2,1,0:T(8,128)(2,1)S(1)}, bf16[1,128,128]{2,1,0:T(8,128)(2,1)S(1)}, u32[]{:S(2)}, u32[]{:S(2)}) %collective-permute-start.5) | collective-permute-done | bytes 32800 | tf_op jit(solution)/shard_map/ppermute | solution.py:141
  13.9 2.8 %collective-permute-start.6 = (bf16[1,128,128]{2,1,0:T(8,128)(2,1)S(1)}, bf16[1,128,128]{2,1,0:T(8,128)(2,1)S(1)}, u32[]{:S(2)}, u32[]{:S(2)}) collective-permute-start(bf16[1,128,128]{2,1,0:T(8,128)(2,1)S(1)} %get-tuple-element.14), channel_id=1, source_target_pairs={{0,17},{1,16},{2,19},{3,18},{4,21},{5,20},{6,23},{7,22},{8,25},{9,... | collective-permute-start | bytes 98312 | tf_op jit(solution)/shard_map/ppermute | solution.py:141
  16.7 0.0 copy-done.7
  16.7 1.1 %turn.1 = (bf16[1,128,128]{2,1,0:T(8,128)(2,1)S(1)}, bf16[16384,128]{1,0:T(8,128)(2,1)S(1)}) custom-call(bf16[1,128,128]{2,1,0:T(8,128)(2,1)S(1)} %get-tuple-element.13.held_ref, bf16[128,128,128]{2,1,0:T(8,128)(2,1)S(1)} %copy-done.7), custom_call_target="tpu_custom_call" | custom-call | flops 17179869184 | bytes 67108864 | tf_op jit(solution)/shard_map/turn/pallas_call | solution.py:13
  17.8 0.0 collective-permute-done.4
  17.8 0.4 %collective-permute-done.6 = bf16[1,128,128]{2,1,0:T(8,128)(2,1)S(1)} collective-permute-done((bf16[1,128,128]{2,1,0:T(8,128)(2,1)S(1)}, bf16[1,128,128]{2,1,0:T(8,128)(2,1)S(1)}, u32[]{:S(2)}, u32[]{:S(2)}) %collective-permute-start.6) | collective-permute-done | bytes 32800 | tf_op jit(solution)/shard_map/ppermute | solution.py:141
  18.3 0.5 %collective-permute-start.7 = (bf16[128,128]{1,0:T(8,128)(2,1)S(1)}, bf16[128,128]{1,0:T(8,128)(2,1)S(1)}, u32[]{:S(2)}, u32[]{:S(2)}) collective-permute-start(bf16[128,128]{1,0:T(8,128)(2,1)S(1)} %add_bitcast_fusion.mine_ref), channel_id=1, source_target_pairs={{0,1},{1,0},{2,3},{3,2},{4,5},{5,4},{6,7},{7,6},{8,9},{9,8},{10,11... | collective-permute-start | bytes 98312 | tf_op jit(solution)/shard_map/ppermute | solution.py:214
  18.8 0.9 %collective-permute-done.7.other_ref = bf16[128,128]{1,0:T(8,128)(2,1)S(1)} collective-permute-done((bf16[128,128]{1,0:T(8,128)(2,1)S(1)}, bf16[128,128]{1,0:T(8,128)(2,1)S(1)}, u32[]{:S(2)}, u32[]{:S(2)}) %collective-permute-start.7) | collective-permute-done | bytes 32800 | tf_op jit(solution)/shard_map/ppermute | solution.py:214
  19.6 0.0 copy-done
  19.6 0.0 copy-done.2
  19.7 0.0 copy-done.6
  19.7 1.6 %couple.1 = f32[8,128]{1,0:T(8,128)} custom-call(bf16[128,128]{1,0:T(8,128)(2,1)S(1)} %add_bitcast_fusion.mine_ref, bf16[128,128]{1,0:T(8,128)(2,1)S(1)} %collective-permute-done.7.other_ref, bf16[16384,128]{1,0:T(8,128)(2,1)S(1)} %get-tuple-element.12.turned_ref, s32[1,128]{1,0:T(1,128)S(1)} %bitcast.15, f32[8,128]{1,0:T(8,128)S(1)} %bitcast.11, ...), custom_call_target="tpu_custom_call" | custom-call | tf_op jit(solution)/shard_map/couple/pallas_call | solution.py:13
  (10 shorter events, 0.0 us)
Async XLA Ops:
  0.0 3.0 %copy-start.3 = (s32[128]{0:T(128)S(1)}, s32[128]{0:T(128)}, u32[]{:S(2)}) copy-start(s32[128]{0:T(128)} %param.11) | copy-start | bytes 1540
  0.0 3.0 %copy-start.4 = (s32[128]{0:T(128)S(1)}, s32[128]{0:T(128)}, u32[]{:S(2)}) copy-start(s32[128]{0:T(128)} %param.12) | copy-start | bytes 1540
  0.0 3.0 %copy-start.5 = (s32[128]{0:T(128)S(1)}, s32[128]{0:T(128)}, u32[]{:S(2)}) copy-start(s32[128]{0:T(128)} %param.13) | copy-start | bytes 1540
  0.0 5.5 %copy-start.1 = (bf16[32,1024]{1,0:T(8,128)(2,1)S(1)}, bf16[32,1024]{1,0:T(8,128)(2,1)}, u32[]{:S(2)}) copy-start(bf16[32,1024]{1,0:T(8,128)(2,1)} %param.8) | copy-start | bytes 196612
  0.0 5.5 %collective-permute-start.2 = (bf16[1,32,1024]{2,1,0:T(8,128)(2,1)}, bf16[1,32,1024]{2,1,0:T(8,128)(2,1)S(1)}, u32[]{:S(2)}, u32[]{:S(2)}) collective-permute-start(bf16[1,32,1024]{2,1,0:T(8,128)(2,1)} %bitcast.9), channel_id=1, source_target_pairs={{0,2},{1,5},{2,0},{3,7},{4,6},{5,1},{6,4},{7,3},{8,10},{9,13},{10,... | collective-permute-start | bytes 196616 | tf_op jit(solution)/shard_map/ppermute | solution.py:141
  3.2 4.0 %collective-permute-start = (s32[1,128]{1,0:T(1,128)S(1)}, s32[1,128]{1,0:T(1,128)S(1)}, u32[]{:S(2)}, u32[]{:S(2)}) collective-permute-start(s32[1,128]{1,0:T(1,128)S(1)} %request.1.mine_ref), channel_id=1, source_target_pairs={{0,17},{1,16},{2,19},{3,18},{4,21},{5,20},{6,23},{7,22},{8,25},{9,... | collective-permute-start | bytes 1544 | tf_op jit(solution)/shard_map/ppermute | solution.py:141
  5.5 4.7 %collective-permute-start.3 = (bf16[2,32,1024]{2,1,0:T(8,128)(2,1)S(1)}, bf16[2,32,1024]{2,1,0:T(8,128)(2,1)S(1)}, u32[]{:S(2)}, u32[]{:S(2)}) collective-permute-start(bf16[2,32,1024]{2,1,0:T(8,128)(2,1)S(1)} %gather.1.refs_2_), channel_id=1, source_target_pairs={{0,5},{1,2},{2,7},{3,0},{4,1},{5,6},{6,3},{7,4},{8,13},{9,10},{10,... | collective-permute-start | bytes 393224 | tf_op jit(solution)/shard_map/ppermute | solution.py:141
  7.1 3.0 %collective-permute-start.1 = (s32[2,128]{1,0:T(2,128)S(1)}, s32[2,128]{1,0:T(2,128)S(1)}, u32[]{:S(2)}, u32[]{:S(2)}) collective-permute-start(s32[2,128]{1,0:T(2,128)S(1)} %join.1.refs_0_), channel_id=1, source_target_pairs={{0,9},{1,8},{2,11},{3,10},{4,13},{5,12},{6,15},{7,14},{8,1},{9,0},... | collective-permute-start | bytes 3080 | tf_op jit(solution)/shard_map/ppermute | solution.py:141
  10.5 6.2 %copy-start.7 = (bf16[128,128,128]{2,1,0:T(8,128)(2,1)S(1)}, bf16[128,128,128]{2,1,0:T(8,128)(2,1)}, u32[]{:S(2)}) copy-start(bf16[128,128,128]{2,1,0:T(8,128)(2,1)} %tiles_ref.1) | copy-start | bytes 12582916
  10.5 3.4 %collective-permute-start.5 = (bf16[1,128,128]{2,1,0:T(8,128)(2,1)S(1)}, bf16[1,128,128]{2,1,0:T(8,128)(2,1)S(1)}, u32[]{:S(2)}, u32[]{:S(2)}) collective-permute-start(bf16[1,128,128]{2,1,0:T(8,128)(2,1)S(1)} %select_send.1), channel_id=1, source_target_pairs={{0,9},{1,8},{2,11},{3,10},{4,13},{5,12},{6,15},{7,14},{8,1},{9,0},... | collective-permute-start | bytes 98312 | tf_op jit(solution)/shard_map/ppermute | solution.py:141
  12.7 5.1 %collective-permute-start.4 = (bf16[1,128,128]{2,1,0:T(8,128)(2,1)S(1)}, bf16[1,128,128]{2,1,0:T(8,128)(2,1)S(1)}, u32[]{:S(2)}, u32[]{:S(2)}) collective-permute-start(bf16[1,128,128]{2,1,0:T(8,128)(2,1)S(1)} %get-tuple-element.11), channel_id=1, source_target_pairs={{0,9},{1,8},{2,11},{3,10},{4,13},{5,12},{6,15},{7,14},{8,1},{9,0},... | collective-permute-start | bytes 98312 | tf_op jit(solution)/shard_map/ppermute | solution.py:141
  13.9 4.4 %collective-permute-start.6 = (bf16[1,128,128]{2,1,0:T(8,128)(2,1)S(1)}, bf16[1,128,128]{2,1,0:T(8,128)(2,1)S(1)}, u32[]{:S(2)}, u32[]{:S(2)}) collective-permute-start(bf16[1,128,128]{2,1,0:T(8,128)(2,1)S(1)} %get-tuple-element.14), channel_id=1, source_target_pairs={{0,17},{1,16},{2,19},{3,18},{4,21},{5,20},{6,23},{7,22},{8,25},{9,... | collective-permute-start | bytes 98312 | tf_op jit(solution)/shard_map/ppermute | solution.py:141
  16.7 3.0 %copy-start = (f32[8,128,128]{2,1,0:T(8,128)S(1)}, f32[8,128,128]{2,1,0:T(8,128)}, u32[]{:S(2)}) copy-start(f32[8,128,128]{2,1,0:T(8,128)} %inverse_ref.1) | copy-start | bytes 1572868
  16.7 3.0 %copy-start.2 = (f32[1024]{0:T(1024)S(1)}, f32[1024]{0:T(1024)}, u32[]{:S(2)}) copy-start(f32[1024]{0:T(1024)} %param.14) | copy-start | bytes 12292
  16.7 3.0 %copy-start.6 = (s32[128]{0:T(128)S(1)}, s32[128]{0:T(128)}, u32[]{:S(2)}) copy-start(s32[128]{0:T(128)} %param.10) | copy-start | bytes 1540
  18.3 1.4 %collective-permute-start.7 = (bf16[128,128]{1,0:T(8,128)(2,1)S(1)}, bf16[128,128]{1,0:T(8,128)(2,1)S(1)}, u32[]{:S(2)}, u32[]{:S(2)}) collective-permute-start(bf16[128,128]{1,0:T(8,128)(2,1)S(1)} %add_bitcast_fusion.mine_ref), channel_id=1, source_target_pairs={{0,1},{1,0},{2,3},{3,2},{4,5},{5,4},{6,7},{7,6},{8,9},{9,8},{10,11... | collective-permute-start | bytes 98312 | tf_op jit(solution)/shard_map/ppermute | solution.py:214

commit v5 on v4

--- a/solution.py
+++ b/solution.py
@@ -1,3 +1,5 @@
+import typing
+
 import jax
 import jax.numpy as jnp
 from jax import lax
@@ -7,6 +9,17 @@
 
 
 VMEM = pl.BlockSpec(memory_space=pltpu.VMEM)
+
+
+class Plan(typing.NamedTuple):
+    size: int
+    slab_shift: int
+    shift: int
+    lag_shift: int
+    pieces: int
+    cap: int
+    slots: int
+    split: tuple
 
 
 def call(kernel, name, outs, *operands, weight=0):
@@ -31,7 +44,7 @@
     out_ref[...] = lax.broadcasted_iota(jnp.int32, out_ref.shape, 0)
 
 
-def request_kernel(total_lags, shift, ids_ref, source_ref, offset_ref, delay_ref, code_ref):
+def request_kernel(total_lags, shift, slab_shift, ids_ref, source_ref, offset_ref, delay_ref, code_ref):
     source = source_ref[...]
     chunk, lane = ids_ref.shape
     looked = jnp.zeros_like(source)
@@ -41,7 +54,14 @@
         looked = looked + jnp.sum(jnp.where(block == source, delay, 0), axis=0, keepdims=True)
     lag = offset_ref[...] + looked
     lag = jnp.where(lag >= total_lags, lag - total_lags, lag)
-    code_ref[...] = (lag << shift) | source
+    code_ref[:, :lane] = (lag << shift) | source
+    owner = source >> slab_shift
+    other = jnp.transpose(jnp.broadcast_to(owner, (lane, lane)))
+    earlier = lax.broadcasted_iota(jnp.int32, (lane, lane), 0) < lax.broadcasted_iota(
+        jnp.int32, (lane, lane), 1
+    )
+    alike = jnp.where((other == owner) & earlier, 1, 0)
+    code_ref[:, lane:] = jnp.sum(alike, axis=0, keepdims=True)
 
 
 def join_kernel(mine_ref, other_ref, out_ref):
@@ -50,8 +70,18 @@
     out_ref[rows:] = other_ref[...]
 
 
-def select_kernel(plan, places, near_ref, far_ref, near_pieces_ref, far_pieces_ref, *out_refs):
-    size, slab_shift, shift, lag_shift, split = plan
+def ordinal(plan, piece, lag):
+    if not plan.split:
+        return jnp.where(piece < plan.pieces, piece, -1)
+    low, high = plan.split
+    turn = jnp.where(lag == 0, low, high)
+    return jnp.where(
+        piece == 0, 0, jnp.where(piece == turn, 1, jnp.where(piece == low + high, 2, -1))
+    )
+
+
+def select_kernel(plan, groups, near_ref, far_ref, near_pieces_ref, far_pieces_ref, *out_refs):
+    size, cap, lag_shift = plan.size, plan.cap, plan.lag_shift
     blk, lag = lax.axis_index("blk"), lax.axis_index("lag")
     slabs = [r[q] for r in (near_pieces_ref, far_pieces_ref) for q in range(r.shape[0])]
     width = slabs[0].shape[1]
@@ -59,41 +89,80 @@
         [s[:, b : b + size] for s in slabs for b in range(0, width, size)], axis=0
     )
     code = jnp.concatenate([near_ref[...], far_ref[...]], axis=0)
-    tiles = code.shape[1]
-    source = code & ((1 << shift) - 1)
-    wanted = code >> shift
-    piece = (source >> slab_shift) ^ blk
+    tiles = code.shape[1] // 2
+    address, place = code[:, :tiles], code[:, tiles:]
+    source = address & ((1 << plan.shift) - 1)
+    wanted = address >> plan.shift
+    piece = (source >> plan.slab_shift) ^ blk
     half = wanted >> lag_shift
-    if split:
-        low, high = split
+    if plan.split:
+        low, high = plan.split
         same, turn = half == lag, jnp.where(lag == 0, low, high)
         slab = jnp.where((piece == 0) & same, 0, -1)
         slab = jnp.where(piece == turn, jnp.where(same, 1, 2), slab)
         slab = jnp.where((piece == low + high) & jnp.logical_not(same), 3, slab)
     else:
-        slab = jnp.where((piece < len(slabs)) & (half == lag), piece, -1)
-    within = ((source & ((1 << slab_shift) - 1)) << lag_shift) + (wanted & ((1 << lag_shift) - 1))
-    row = (slab << (slab_shift + lag_shift)) + within
+        slab = jnp.where((piece < plan.pieces) & (half == lag), piece, -1)
+    inner = (source & ((1 << plan.slab_shift) - 1)) << lag_shift
+    row = (slab << (plan.slab_shift + lag_shift)) + inner + (wanted & ((1 << lag_shift) - 1))
     row = jnp.where(slab >= 0, row, -1)
-    lane = lax.broadcasted_iota(jnp.int32, (tiles, size), 1)
-    for d, out, index in places:
-        mine = jnp.transpose(jnp.broadcast_to(row[d : d + 1, :], (size, tiles)))
+    rank = ordinal(plan, piece, lag)
+    slot = jnp.where(rank >= 0, rank * cap + place, -1)
+
+    def picked(chosen):
+        lane = lax.broadcasted_iota(jnp.int32, chosen.shape, 1)
         onehot = jnp.concatenate(
             [
-                jnp.where(mine == lane + first, 1.0, 0.0).astype(jnp.bfloat16)
+                jnp.where(chosen == lane + first, 1.0, 0.0).astype(jnp.bfloat16)
                 for first in range(0, table.shape[0], size)
             ],
             axis=1,
         )
-        picked = jnp.dot(onehot, table, preferred_element_type=jnp.float32)
-        out_refs[out][index] = picked.astype(jnp.bfloat16)
-
-
-def turn_kernel(held_ref, tiles_ref, passed_ref, turned_ref):
+        return jnp.dot(onehot, table, preferred_element_type=jnp.float32).astype(jnp.bfloat16)
+
+    slot_id = lax.broadcasted_iota(jnp.int32, (plan.slots, tiles), 0)
+    for group, out_ref in zip(groups, out_refs):
+        for k, d in enumerate(group):
+            if d is None:
+                out_ref[...] = picked(jnp.transpose(jnp.broadcast_to(row[:1], (size, tiles))))
+            else:
+                there = jnp.where(slot_id == slot[d : d + 1], row[d : d + 1] + 1, 0)
+                chosen = jnp.sum(there, axis=1, keepdims=True) - 1
+                chosen = jnp.broadcast_to(chosen, (plan.slots, size))
+                out_ref[k * plan.slots : (k + 1) * plan.slots, :] = picked(chosen)
+
+
+def turn_kernel(plan, held_ref, code_ref, tiles_ref, passed_ref, turned_ref, *map_refs):
     tiles, size = tiles_ref.shape[:2]
     passed_ref[...] = held_ref[...]
+    blk, lag = lax.axis_index("blk"), lax.axis_index("lag")
+    source = code_ref[:, :tiles] & ((1 << plan.shift) - 1)
+    place = code_ref[:, tiles:]
+    apart = (source >> plan.slab_shift) ^ blk
+    piece, plane = apart & (plan.pieces - 1), apart >> (plan.pieces.bit_length() - 1)
+    sender = jnp.zeros_like(plane) + lag
+    if plan.split:
+        for i in range(len(map_refs)):
+            sender = sender ^ ((plane >> i) & 1)
+    rank = ordinal(plan, piece, sender)
+    for i, map_ref in enumerate(map_refs):
+        column = ((plane - (1 << i)) * plan.slots) + rank * plan.cap + place
+        column = jnp.where((rank >= 0) & ((plane >> i) == 1), column, -1)
+        column = jnp.transpose(jnp.broadcast_to(column, (size, tiles)))[:, : map_ref.shape[1]]
+        lane = lax.broadcasted_iota(jnp.int32, map_ref.shape, 1)
+        map_ref[...] = jnp.where(column == lane, 1.0, 0.0).astype(map_ref.dtype)
     for t in range(tiles):
         turned_ref[t * size : (t + 1) * size, :] = jnp.transpose(tiles_ref[t])
+
+
+def spread_kernel(*refs):
+    hops = (len(refs) - 2) // 2
+    total = refs[0][...].astype(jnp.float32)
+    for map_ref, rows_ref in zip(refs[1 : 1 + hops], refs[1 + hops : 1 + 2 * hops]):
+        total = total + jnp.dot(
+            map_ref[...], rows_ref[...], preferred_element_type=jnp.float32
+        )
+    refs[-1][...] = total.astype(refs[-1].dtype)
 
 
 def couple_kernel(
@@ -130,6 +199,18 @@
     exchange_bits = [1 << i for i in range(bits // 2, bits)]
     lag_shift = lag_rows.bit_length() - 1
     paired = n_lag == 2 and len(gather_bits) == 2
+    cap = 2 * tile_count // n_blk
+    n_pieces = 1 << len(gather_bits)
+    plan = Plan(
+        size,
+        slab_shift,
+        shift,
+        lag_shift,
+        n_pieces,
+        cap,
+        (3 if paired else n_pieces) * cap,
+        tuple(gather_bits) if paired else (),
+    )
 
     def hop(value, bit, other=None, flip=1):
         bits_of, flip = [bit, bit if other is None else other], flip if paired else 0
@@ -146,9 +227,9 @@
         first = hop(history[None], gather_bits[0])
     ids = call(ids_kernel, "ids", pltpu.VMEM((min(all_blocks, 128), tile_count), jnp.int32), weight=8)
     code = call(
-        lambda *refs: request_kernel(lag_rows * n_lag, shift, *refs),
+        lambda *refs: request_kernel(lag_rows * n_lag, shift, slab_shift, *refs),
         "request",
-        pltpu.VMEM((1, tile_count), jnp.int32),
+        pltpu.VMEM((1, 2 * tile_count), jnp.int32),
         ids,
         tile_source[None],
         tile_offset[None],
@@ -159,6 +240,7 @@
         shape = (2 * mine.shape[0],) + mine.shape[1:]
         return call(join_kernel, name, pltpu.VMEM(shape, mine.dtype), mine, other, weight=weight)
 
+    own_code = code
     for bit in exchange_bits[:0:-1]:
         code = join("join", code, hop(code, bit), 8)
     far_code = hop(code, exchange_bits[0])
@@ -167,18 +249,16 @@
         pieces = join("gather", pieces, arrived, 0)
         arrived = hop(pieces, bit, gather_bits[0]) if paired else hop(pieces, bit)
 
-    half = code.shape[0]
-    plan = (size, slab_shift, shift, lag_shift, gather_bits if paired else None)
-
-    def select(name, sizes, places, weight):
-        places = [
-            (sum(((d >> i) & 1) << (len(exchange_bits) - 1 - i) for i in range(len(exchange_bits))), out, k)
-            for d, out, k in places
-        ]
+    n_hops = len(exchange_bits)
+
+    def select(name, groups, rows, weight):
+        def request(d):
+            return sum(((d >> i) & 1) << (n_hops - 1 - i) for i in range(n_hops)) or None
+
         return call(
-            lambda *refs: select_kernel(plan, places, *refs),
+            lambda *refs: select_kernel(plan, [[request(d) for d in g] for g in groups], *refs),
             name,
-            [pltpu.VMEM((n, tile_count, size), jnp.bfloat16) for n in sizes],
+            [pltpu.VMEM((n, size), jnp.bfloat16) for n in rows],
             code,
             far_code,
             pieces,
@@ -186,30 +266,39 @@
             weight=weight,
         )
 
-    (send,) = select("select_send", [half - 1], [(2 * k + 1, 0, k - 1) for k in range(1, half)], 16)
-    direct, keep = select(
-        "select_keep", [1, half], [(1, 0, 0)] + [(2 * k, 1, k) for k in range(half)], 16
-    )
-
-    ended = []
-    for bit in exchange_bits:
-        if keep.shape[0] > 1:
+    def passes(i):
+        return [d for d in range(1 << n_hops) if d >> i > 1 and (d >> i) & 1 and d % (1 << i) == 0]
+
+    first_pass = passes(0)
+    (send,) = select("select_send", [first_pass], [plan.slots * len(first_pass)], 16)
+    rest = [1] + [d for d in range(2, 1 << n_hops) if d % 2 == 0]
+    *picks, keep = select(
+        "select_keep", [[d] for d in rest] + [[0]], [plan.slots] * len(rest) + [tile_count], 16
+    )
+    held = dict(zip(rest, picks))
+    landed = []
+    for i, bit in enumerate(exchange_bits):
+        onward, rows = passes(i), plan.slots << i
+        if onward:
+            if i:
+                send = jnp.concatenate([held[d] for d in onward], axis=0)
             passed = hop(send, bit)
-            ended.append(hop(direct, bit))
-            onward = keep[1::2] + passed[0::2]
-            direct, send = onward[:1], onward[1:]
-            keep = jnp.concatenate([keep[:1], keep[2::2] + passed[1::2]], axis=0)
-        else:
-            keep, turned = call(
-                turn_kernel,
+        if i == n_hops - 1:
+            keep, turned, *maps = call(
+                lambda *refs: turn_kernel(plan, *refs),
                 "turn",
-                (in_vmem(keep), pltpu.VMEM((tile_count * size, size), tile_blocks.dtype)),
+                [in_vmem(keep), pltpu.VMEM((tile_count * size, size), tile_blocks.dtype)]
+                + [pltpu.VMEM((tile_count, plan.slots << k), jnp.bfloat16) for k in range(n_hops)],
                 keep,
+                own_code,
                 tile_blocks,
                 weight=4,
             )
-            ended.append(hop(direct, bit))
-    mine = sum(ended, keep).reshape(tile_count, size)
+        landed.append(hop(held[1 << i], bit))
+        for k, d in enumerate(onward):
+            here = d ^ (1 << i)
+            held[here] = jnp.concatenate([held[here], passed[k * rows : (k + 1) * rows]], axis=0)
+    mine = call(spread_kernel, "spread", in_vmem(keep), keep, *maps, *landed)
     if n_lag == 2:
         other = lax.ppermute(mine, "lag", [(0, 1), (1, 0)])
     else:

time: 21.5 us -> 21.1 us (0.981)
  waiting for transfers between devices: 4.13 us -> 3.83 us
    ppermute x7, waiting for transfers between devices: 3.27 us -> 2.97 us  [hop(): return lax.ppermute(value, ('blk', 'lag'), pairs)]
    pallas_call x8 -> x9, Pallas kernels: 3.61 us -> 3.74 us  [call(): pl.pallas_call(kernel, out_shape=outs, in_specs=[VMEM] * len(operands), o...]
where the time goes in v5:
time: 21.1 us; the launch traced here: 21 us
  starting transfers between devices  13.3 us (63%)
  waiting for transfers between devices  3.83 us (18%)
  Pallas kernels  3.74 us (18%)
    ppermute x7, starting transfers between devices, hop(): return lax.ppermute(value, ('blk', 'lag'), pairs)  12.8 us
    pallas_call x9, Pallas kernels, call(): pl.pallas_call(kernel, out_shape=outs, in_specs=[VMEM] * len(operands), o...  3.74 us
    ppermute x7, waiting for transfers between devices, hop(): return lax.ppermute(value, ('blk', 'lag'), pairs)  2.97 us
    ppermute x1, waiting for transfers between devices, body(): other = lax.ppermute(mine, 'lag', [(0, 1), (1, 0)])  0.86 us
    ppermute x1, starting transfers between devices, body(): other = lax.ppermute(mine, 'lag', [(0, 1), (1, 0)])  0.5 us
  transfers between devices with their start and end apart: 8, of which 5 were waited for; matrix products, arithmetic and copies ran while one was open for 0% of the time, Pallas kernels for 8%

profile of v5, /device:TPU:0, one launch (start us, length us, event | category | flops | bytes accessed | tf_op | source)
XLA Modules:
  0.0 21.0 jit_solution(8612407663792848967)
XLA Ops:
  0.0 0.0 copy-start.3
  0.0 3.0 %collective-permute-start.2 = (bf16[1,32,1024]{2,1,0:T(8,128)(2,1)}, bf16[1,32,1024]{2,1,0:T(8,128)(2,1)S(1)}, u32[]{:S(2)}, u32[]{:S(2)}) collective-permute-start(bf16[1,32,1024]{2,1,0:T(8,128)(2,1)} %bitcast.7), channel_id=1, source_target_pairs={{0,2},{1,5},{2,0},{3,7},{4,6},{5,1},{6,4},{7,3},{8,10},{9,13},{10,... | collective-permute-start | bytes 196616 | tf_op jit(solution)/shard_map/ppermute | solution.py:222
  3.0 0.0 copy-done.3
  3.0 0.0 copy-done.4
  3.0 0.0 copy-done.5
  3.1 0.1 request.1.mine_ref.refs_1_
  3.2 1.8 %collective-permute-start = (s32[1,256]{1,0:T(1,128)S(1)}, s32[1,256]{1,0:T(1,128)S(1)}, u32[]{:S(2)}, u32[]{:S(2)}) collective-permute-start(s32[1,256]{1,0:T(1,128)S(1)} %request.1.mine_ref.refs_1_), channel_id=1, source_target_pairs={{0,17},{1,16},{2,19},{3,18},{4,21},{5,20},{6,23},{7,22},{8,25},{9,... | collective-permute-start | bytes 3080 | tf_op jit(solution)/shard_map/ppermute | solution.py:222
  5.0 0.5 %collective-permute-done.2.other_ref = bf16[1,32,1024]{2,1,0:T(8,128)(2,1)S(1)} collective-permute-done((bf16[1,32,1024]{2,1,0:T(8,128)(2,1)}, bf16[1,32,1024]{2,1,0:T(8,128)(2,1)S(1)}, u32[]{:S(2)}, u32[]{:S(2)}) %collective-permute-start.2) | collective-permute-done | bytes 65568 | tf_op jit(solution)/shard_map/ppermute | solution.py:222
  5.5 0.0 copy-done.1
  5.5 1.6 %collective-permute-start.3 = (bf16[2,32,1024]{2,1,0:T(8,128)(2,1)S(1)}, bf16[2,32,1024]{2,1,0:T(8,128)(2,1)S(1)}, u32[]{:S(2)}, u32[]{:S(2)}) collective-permute-start(bf16[2,32,1024]{2,1,0:T(8,128)(2,1)S(1)} %gather.1.refs_2_), channel_id=1, source_target_pairs={{0,5},{1,2},{2,7},{3,0},{4,1},{5,6},{6,3},{7,4},{8,13},{9,10},{10,... | collective-permute-start | bytes 393224 | tf_op jit(solution)/shard_map/ppermute | solution.py:222
  7.1 0.0 collective-permute-done.other_ref
  7.1 1.7 %collective-permute-start.1 = (s32[2,256]{1,0:T(2,128)S(1)}, s32[2,256]{1,0:T(2,128)S(1)}, u32[]{:S(2)}, u32[]{:S(2)}) collective-permute-start(s32[2,256]{1,0:T(2,128)S(1)} %join.1.refs_0_), channel_id=1, source_target_pairs={{0,9},{1,8},{2,11},{3,10},{4,13},{5,12},{6,15},{7,14},{8,1},{9,0},... | collective-permute-start | bytes 6152 | tf_op jit(solution)/shard_map/ppermute | solution.py:222
  8.9 1.3 %collective-permute-done.1.refs_1_ = s32[2,256]{1,0:T(2,128)S(1)} collective-permute-done((s32[2,256]{1,0:T(2,128)S(1)}, s32[2,256]{1,0:T(2,128)S(1)}, u32[]{:S(2)}, u32[]{:S(2)}) %collective-permute-start.1) | collective-permute-done | bytes 2080 | tf_op jit(solution)/shard_map/ppermute | solution.py:222
  10.2 0.0 collective-permute-done.3.refs_3_
  10.2 0.3 %select_send.1 = bf16[48,128]{1,0:T(8,128)(2,1)S(1)} custom-call(s32[2,256]{1,0:T(2,128)S(1)} %join.1.refs_0_, s32[2,256]{1,0:T(2,128)S(1)} %collective-permute-done.1.refs_1_, bf16[2,32,1024]{2,1,0:T(8,128)(2,1)S(1)} %gather.1.refs_2_, bf16[2,32,1024]{2,1,0:T(8,128)(2,1)S(1)} %collective-permute-done.3.refs_3_), custom_call_target="tpu_custom_call" | custom-call | flops 68719476736 | bytes 268435456 | tf_op jit(solution)/shard_map/select_send/pallas_call | solution.py:26
  10.4 0.0 copy-start.7
  10.5 1.8 %collective-permute-start.5 = (bf16[48,128]{1,0:T(8,128)(2,1)S(1)}, bf16[48,128]{1,0:T(8,128)(2,1)S(1)}, u32[]{:S(2)}, u32[]{:S(2)}) collective-permute-start(bf16[48,128]{1,0:T(8,128)(2,1)S(1)} %select_send.1), channel_id=1, source_target_pairs={{0,9},{1,8},{2,11},{3,10},{4,13},{5,12},{6,15},{7,14},{8,1},{9,0},... | collective-permute-start | bytes 36872 | tf_op jit(solution)/shard_map/ppermute | solution.py:222
  12.2 0.4 %select_keep.1 = (bf16[48,128]{1,0:T(8,128)(2,1)S(1)}, bf16[48,128]{1,0:T(8,128)(2,1)S(1)}, bf16[128,128]{1,0:T(8,128)(2,1)S(1)}) custom-call(s32[2,256]{1,0:T(2,128)S(1)} %join.1.refs_0_, s32[2,256]{1,0:T(2,128)S(1)} %collective-permute-done.1.refs_1_, bf16[2,32,1024]{2,1,0:T(8,128)(2,1)S(1)} %gather.1.refs_2_, ...), custom_call_target="tpu_custom_call" | custom-call | flops 68719476736 | bytes 268435456 | tf_op jit(solution)/shard_map/select_keep/pallas_call | solution.py:26
  12.6 0.1 collective-permute-start.4
  12.7 0.9 %collective-permute-done.5 = bf16[48,128]{1,0:T(8,128)(2,1)S(1)} collective-permute-done((bf16[48,128]{1,0:T(8,128)(2,1)S(1)}, bf16[48,128]{1,0:T(8,128)(2,1)S(1)}, u32[]{:S(2)}, u32[]{:S(2)}) %collective-permute-start.5) | collective-permute-done | bytes 12320 | tf_op jit(solution)/shard_map/ppermute | solution.py:222
  13.7 2.7 %collective-permute-start.6 = (bf16[96,128]{1,0:T(8,128)(2,1)S(1)}, bf16[96,128]{1,0:T(8,128)(2,1)S(1)}, u32[]{:S(2)}, u32[]{:S(2)}) collective-permute-start(bf16[96,128]{1,0:T(8,128)(2,1)S(1)} %pad_maximum_fusion), channel_id=1, source_target_pairs={{0,17},{1,16},{2,19},{3,18},{4,21},{5,20},{6,23},{7,22},{8,25},{9,... | collective-permute-start | bytes 73736 | tf_op jit(solution)/shard_map/ppermute | solution.py:222
  16.4 0.0 copy-done.7
  16.4 1.2 %turn.1 = (bf16[128,128]{1,0:T(8,128)(2,1)S(1)}, bf16[16384,128]{1,0:T(8,128)(2,1)S(1)}, bf16[128,48]{1,0:T(8,128)(2,1)S(1)}, bf16[128,96]{1,0:T(8,128)(2,1)S(1)}) custom-call(bf16[128,128]{1,0:T(8,128)(2,1)S(1)} %get-tuple-element.12.refs_0_, s32[1,256]{1,0:T(1,128)S(1)} %request.1.mine_ref.refs_1_, bf16[128,128,128]{2,1,0:T(8,128)(2,1)S(1)} %copy-done.7), custom_call_target="tpu_custom_call" | custom-call | flops 17179869184 | bytes 67108864 | tf_op jit(solution)/shard_map/turn/pallas_call | solution.py:26
  17.6 0.0 collective-permute-done.4.refs_3_
  17.6 0.3 %collective-permute-done.6.refs_4_ = bf16[96,128]{1,0:T(8,128)(2,1)S(1)} collective-permute-done((bf16[96,128]{1,0:T(8,128)(2,1)S(1)}, bf16[96,128]{1,0:T(8,128)(2,1)S(1)}, u32[]{:S(2)}, u32[]{:S(2)}) %collective-permute-start.6) | collective-permute-done | bytes 24608 | tf_op jit(solution)/shard_map/ppermute | solution.py:222
  17.9 0.1 spread.1.mine_ref
  18.0 0.5 %collective-permute-start.7 = (bf16[128,128]{1,0:T(8,128)(2,1)S(1)}, bf16[128,128]{1,0:T(8,128)(2,1)S(1)}, u32[]{:S(2)}, u32[]{:S(2)}) collective-permute-start(bf16[128,128]{1,0:T(8,128)(2,1)S(1)} %spread.1.mine_ref), channel_id=1, source_target_pairs={{0,1},{1,0},{2,3},{3,2},{4,5},{5,4},{6,7},{7,6},{8,9},{9,8},{10,11... | collective-permute-start | bytes 98312 | tf_op jit(solution)/shard_map/ppermute | solution.py:303
  18.5 0.9 %collective-permute-done.7.other_ref = bf16[128,128]{1,0:T(8,128)(2,1)S(1)} collective-permute-done((bf16[128,128]{1,0:T(8,128)(2,1)S(1)}, bf16[128,128]{1,0:T(8,128)(2,1)S(1)}, u32[]{:S(2)}, u32[]{:S(2)}) %collective-permute-start.7) | collective-permute-done | bytes 32800 | tf_op jit(solution)/shard_map/ppermute | solution.py:303
  19.4 0.0 copy-done
  19.4 0.0 copy-done.2
  19.4 0.0 copy-done.6
  19.4 1.6 %couple.1 = f32[8,128]{1,0:T(8,128)} custom-call(bf16[128,128]{1,0:T(8,128)(2,1)S(1)} %spread.1.mine_ref, bf16[128,128]{1,0:T(8,128)(2,1)S(1)} %collective-permute-done.7.other_ref, bf16[16384,128]{1,0:T(8,128)(2,1)S(1)} %get-tuple-element.18.turned_ref, s32[1,128]{1,0:T(1,128)S(1)} %bitcast.13, f32[8,128]{1,0:T(8,128)S(1)} %bitcast.9, ...), custom_call_target="tpu_custom_call" | custom-call | tf_op jit(solution)/shard_map/couple/pallas_call | solution.py:26
  (10 shorter events, 0.0 us)
Async XLA Ops:
  0.0 3.0 %copy-start.3 = (s32[128]{0:T(128)S(1)}, s32[128]{0:T(128)}, u32[]{:S(2)}) copy-start(s32[128]{0:T(128)} %param.11) | copy-start | bytes 1540
  0.0 3.0 %copy-start.4 = (s32[128]{0:T(128)S(1)}, s32[128]{0:T(128)}, u32[]{:S(2)}) copy-start(s32[128]{0:T(128)} %param.12) | copy-start | bytes 1540
  0.0 3.0 %copy-start.5 = (s32[128]{0:T(128)S(1)}, s32[128]{0:T(128)}, u32[]{:S(2)}) copy-start(s32[128]{0:T(128)} %param.13) | copy-start | bytes 1540
  0.0 5.5 %copy-start.1 = (bf16[32,1024]{1,0:T(8,128)(2,1)S(1)}, bf16[32,1024]{1,0:T(8,128)(2,1)}, u32[]{:S(2)}) copy-start(bf16[32,1024]{1,0:T(8,128)(2,1)} %param.8) | copy-start | bytes 196612
  0.0 5.5 %collective-permute-start.2 = (bf16[1,32,1024]{2,1,0:T(8,128)(2,1)}, bf16[1,32,1024]{2,1,0:T(8,128)(2,1)S(1)}, u32[]{:S(2)}, u32[]{:S(2)}) collective-permute-start(bf16[1,32,1024]{2,1,0:T(8,128)(2,1)} %bitcast.7), channel_id=1, source_target_pairs={{0,2},{1,5},{2,0},{3,7},{4,6},{5,1},{6,4},{7,3},{8,10},{9,13},{10,... | collective-permute-start | bytes 196616 | tf_op jit(solution)/shard_map/ppermute | solution.py:222
  3.2 4.0 %collective-permute-start = (s32[1,256]{1,0:T(1,128)S(1)}, s32[1,256]{1,0:T(1,128)S(1)}, u32[]{:S(2)}, u32[]{:S(2)}) collective-permute-start(s32[1,256]{1,0:T(1,128)S(1)} %request.1.mine_ref.refs_1_), channel_id=1, source_target_pairs={{0,17},{1,16},{2,19},{3,18},{4,21},{5,20},{6,23},{7,22},{8,25},{9,... | collective-permute-start | bytes 3080 | tf_op jit(solution)/shard_map/ppermute | solution.py:222
  5.5 4.7 %collective-permute-start.3 = (bf16[2,32,1024]{2,1,0:T(8,128)(2,1)S(1)}, bf16[2,32,1024]{2,1,0:T(8,128)(2,1)S(1)}, u32[]{:S(2)}, u32[]{:S(2)}) collective-permute-start(bf16[2,32,1024]{2,1,0:T(8,128)(2,1)S(1)} %gather.1.refs_2_), channel_id=1, source_target_pairs={{0,5},{1,2},{2,7},{3,0},{4,1},{5,6},{6,3},{7,4},{8,13},{9,10},{10,... | collective-permute-start | bytes 393224 | tf_op jit(solution)/shard_map/ppermute | solution.py:222
  7.1 3.0 %collective-permute-start.1 = (s32[2,256]{1,0:T(2,128)S(1)}, s32[2,256]{1,0:T(2,128)S(1)}, u32[]{:S(2)}, u32[]{:S(2)}) collective-permute-start(s32[2,256]{1,0:T(2,128)S(1)} %join.1.refs_0_), channel_id=1, source_target_pairs={{0,9},{1,8},{2,11},{3,10},{4,13},{5,12},{6,15},{7,14},{8,1},{9,0},... | collective-permute-start | bytes 6152 | tf_op jit(solution)/shard_map/ppermute | solution.py:222
  10.4 5.9 %copy-start.7 = (bf16[128,128,128]{2,1,0:T(8,128)(2,1)S(1)}, bf16[128,128,128]{2,1,0:T(8,128)(2,1)}, u32[]{:S(2)}) copy-start(bf16[128,128,128]{2,1,0:T(8,128)(2,1)} %refs_2_.1) | copy-start | bytes 12582916
  10.5 3.2 %collective-permute-start.5 = (bf16[48,128]{1,0:T(8,128)(2,1)S(1)}, bf16[48,128]{1,0:T(8,128)(2,1)S(1)}, u32[]{:S(2)}, u32[]{:S(2)}) collective-permute-start(bf16[48,128]{1,0:T(8,128)(2,1)S(1)} %select_send.1), channel_id=1, source_target_pairs={{0,9},{1,8},{2,11},{3,10},{4,13},{5,12},{6,15},{7,14},{8,1},{9,0},... | collective-permute-start | bytes 36872 | tf_op jit(solution)/shard_map/ppermute | solution.py:222
  12.6 5.0 %collective-permute-start.4 = (bf16[48,128]{1,0:T(8,128)(2,1)S(1)}, bf16[48,128]{1,0:T(8,128)(2,1)S(1)}, u32[]{:S(2)}, u32[]{:S(2)}) collective-permute-start(bf16[48,128]{1,0:T(8,128)(2,1)S(1)} %get-tuple-element.16), channel_id=1, source_target_pairs={{0,9},{1,8},{2,11},{3,10},{4,13},{5,12},{6,15},{7,14},{8,1},{9,0},... | collective-permute-start | bytes 36872 | tf_op jit(solution)/shard_map/ppermute | solution.py:222
  13.7 4.2 %collective-permute-start.6 = (bf16[96,128]{1,0:T(8,128)(2,1)S(1)}, bf16[96,128]{1,0:T(8,128)(2,1)S(1)}, u32[]{:S(2)}, u32[]{:S(2)}) collective-permute-start(bf16[96,128]{1,0:T(8,128)(2,1)S(1)} %pad_maximum_fusion), channel_id=1, source_target_pairs={{0,17},{1,16},{2,19},{3,18},{4,21},{5,20},{6,23},{7,22},{8,25},{9,... | collective-permute-start | bytes 73736 | tf_op jit(solution)/shard_map/ppermute | solution.py:222
  16.4 3.0 %copy-start = (f32[8,128,128]{2,1,0:T(8,128)S(1)}, f32[8,128,128]{2,1,0:T(8,128)}, u32[]{:S(2)}) copy-start(f32[8,128,128]{2,1,0:T(8,128)} %inverse_ref.1) | copy-start | bytes 1572868
  16.4 3.0 %copy-start.2 = (f32[1024]{0:T(1024)S(1)}, f32[1024]{0:T(1024)}, u32[]{:S(2)}) copy-start(f32[1024]{0:T(1024)} %param.14) | copy-start | bytes 12292
  16.4 3.0 %copy-start.6 = (s32[128]{0:T(128)S(1)}, s32[128]{0:T(128)}, u32[]{:S(2)}) copy-start(s32[128]{0:T(128)} %param.10) | copy-start | bytes 1540
  18.0 1.4 %collective-permute-start.7 = (bf16[128,128]{1,0:T(8,128)(2,1)S(1)}, bf16[128,128]{1,0:T(8,128)(2,1)S(1)}, u32[]{:S(2)}, u32[]{:S(2)}) collective-permute-start(bf16[128,128]{1,0:T(8,128)(2,1)S(1)} %spread.1.mine_ref), channel_id=1, source_target_pairs={{0,1},{1,0},{2,3},{3,2},{4,5},{5,4},{6,7},{7,6},{8,9},{9,8},{10,11... | collective-permute-start | bytes 98312 | tf_op jit(solution)/shard_map/ppermute | solution.py:303

commit v6 on v5

--- a/solution.py
+++ b/solution.py
@@ -85,9 +85,11 @@
     blk, lag = lax.axis_index("blk"), lax.axis_index("lag")
     slabs = [r[q] for r in (near_pieces_ref, far_pieces_ref) for q in range(r.shape[0])]
     width = slabs[0].shape[1]
+    table = [s[:, b : b + size] for s in slabs for b in range(0, width, size)]
     table = jnp.concatenate(
-        [s[:, b : b + size] for s in slabs for b in range(0, width, size)], axis=0
-    )
+        [jnp.concatenate(table[: len(table) // 2]), jnp.concatenate(table[len(table) // 2 :])], axis=1
+    )
+    depth = table.shape[0]
     code = jnp.concatenate([near_ref[...], far_ref[...]], axis=0)
     tiles = code.shape[1] // 2
     address, place = code[:, :tiles], code[:, tiles:]
@@ -111,19 +113,23 @@
 
     def picked(chosen):
         lane = lax.broadcasted_iota(jnp.int32, chosen.shape, 1)
+        low = chosen & (depth - 1)
         onehot = jnp.concatenate(
             [
-                jnp.where(chosen == lane + first, 1.0, 0.0).astype(jnp.bfloat16)
-                for first in range(0, table.shape[0], size)
+                jnp.where(low == lane + first, 1.0, 0.0).astype(jnp.bfloat16)
+                for first in range(0, depth, size)
             ],
             axis=1,
         )
-        return jnp.dot(onehot, table, preferred_element_type=jnp.float32).astype(jnp.bfloat16)
+        both = jnp.dot(onehot, table, preferred_element_type=jnp.float32)
+        upper = chosen >> (depth.bit_length() - 1)
+        rows = jnp.where(upper == 0, both[:, :size], jnp.where(upper == 1, both[:, size:], 0.0))
+        return rows.astype(jnp.bfloat16)
 
     slot_id = lax.broadcasted_iota(jnp.int32, (plan.slots, tiles), 0)
     for group, out_ref in zip(groups, out_refs):
         for k, d in enumerate(group):
-            if d is None:
+            if d == 0:
                 out_ref[...] = picked(jnp.transpose(jnp.broadcast_to(row[:1], (size, tiles))))
             else:
                 there = jnp.where(slot_id == slot[d : d + 1], row[d : d + 1] + 1, 0)
@@ -132,14 +138,19 @@
                 out_ref[k * plan.slots : (k + 1) * plan.slots, :] = picked(chosen)
 
 
-def turn_kernel(plan, held_ref, code_ref, tiles_ref, passed_ref, turned_ref, *map_refs):
+def turn_kernel(
+    plan, held_ref, code_ref, target_ref, tiles_ref, passed_ref, turned_ref, column_ref, *map_refs
+):
     tiles, size = tiles_ref.shape[:2]
     passed_ref[...] = held_ref[...]
+    column_ref[...] = jnp.transpose(jnp.broadcast_to(target_ref[...], (size, tiles)))
     blk, lag = lax.axis_index("blk"), lax.axis_index("lag")
     source = code_ref[:, :tiles] & ((1 << plan.shift) - 1)
     place = code_ref[:, tiles:]
     apart = (source >> plan.slab_shift) ^ blk
-    piece, plane = apart & (plan.pieces - 1), apart >> (plan.pieces.bit_length() - 1)
+    piece, high = apart & (plan.pieces - 1), apart >> (plan.pieces.bit_length() - 1)
+    hops = len(map_refs)
+    plane = sum(((high >> (hops - 1 - i)) & 1) << i for i in range(hops))
     sender = jnp.zeros_like(plane) + lag
     if plan.split:
         for i in range(len(map_refs)):
@@ -148,34 +159,33 @@
     for i, map_ref in enumerate(map_refs):
         column = ((plane - (1 << i)) * plan.slots) + rank * plan.cap + place
         column = jnp.where((rank >= 0) & ((plane >> i) == 1), column, -1)
-        column = jnp.transpose(jnp.broadcast_to(column, (size, tiles)))[:, : map_ref.shape[1]]
+        wide = -(-map_ref.shape[1] // size) * size
+        column = jnp.transpose(jnp.broadcast_to(column, (wide, tiles)))[:, : map_ref.shape[1]]
         lane = lax.broadcasted_iota(jnp.int32, map_ref.shape, 1)
         map_ref[...] = jnp.where(column == lane, 1.0, 0.0).astype(map_ref.dtype)
     for t in range(tiles):
         turned_ref[t * size : (t + 1) * size, :] = jnp.transpose(tiles_ref[t])
 
 
-def spread_kernel(*refs):
-    hops = (len(refs) - 2) // 2
-    total = refs[0][...].astype(jnp.float32)
-    for map_ref, rows_ref in zip(refs[1 : 1 + hops], refs[1 + hops : 1 + 2 * hops]):
-        total = total + jnp.dot(
+def couple_kernel(turned_ref, target_ref, keep_ref, *refs):
+    *refs, out_ref = refs
+    hops = len(refs) // 2
+    vectors = keep_ref[...].astype(jnp.float32)
+    for map_ref, rows_ref in zip(refs[:hops], refs[hops:]):
+        vectors = vectors + jnp.dot(
             map_ref[...], rows_ref[...], preferred_element_type=jnp.float32
         )
-    refs[-1][...] = total.astype(refs[-1].dtype)
-
-
-def couple_kernel(
-    mine_ref, other_ref, turned_ref, target_ref, incident_ref, inverse_ref, out_ref
-):
-    blocks, size = incident_ref.shape
-    tiles = mine_ref.shape[0]
-    vectors = mine_ref[...].astype(jnp.float32) + other_ref[...].astype(jnp.float32)
-    target = jnp.transpose(jnp.broadcast_to(target_ref[...], (size, tiles)))
+    tiles, size = vectors.shape
+    blocks = out_ref.shape[0]
+    target = target_ref[...]
     left = jnp.stack([jnp.where(target == b, vectors, 0.0) for b in range(blocks)], axis=0)
     left = left.astype(jnp.bfloat16).reshape(blocks, tiles * size)
-    total = jnp.dot(left, turned_ref[...], preferred_element_type=jnp.float32)
-    excite = incident_ref[...] - total
+    out_ref[...] = jnp.dot(left, turned_ref[...], preferred_element_type=jnp.float32)
+
+
+def solve_kernel(mine_ref, other_ref, incident_ref, inverse_ref, out_ref):
+    blocks, size = incident_ref.shape
+    excite = incident_ref[...] - (mine_ref[...] + other_ref[...])
     lane = lax.broadcasted_iota(jnp.int32, (size, blocks), 1)
     solved = jnp.zeros((size, blocks), jnp.float32)
     for b in range(blocks):
@@ -196,7 +206,7 @@
     shift = all_blocks.bit_length() - 1
     slab_shift = slab_blocks.bit_length() - 1
     gather_bits = [1 << i for i in range(bits // 2)]
-    exchange_bits = [1 << i for i in range(bits // 2, bits)]
+    exchange_bits = [1 << i for i in range(bits - 1, bits // 2 - 1, -1)]
     lag_shift = lag_rows.bit_length() - 1
     paired = n_lag == 2 and len(gather_bits) == 2
     cap = 2 * tile_count // n_blk
@@ -241,9 +251,9 @@
         return call(join_kernel, name, pltpu.VMEM(shape, mine.dtype), mine, other, weight=weight)
 
     own_code = code
-    for bit in exchange_bits[:0:-1]:
+    for bit in exchange_bits[:-1]:
         code = join("join", code, hop(code, bit), 8)
-    far_code = hop(code, exchange_bits[0])
+    far_code = hop(code, exchange_bits[-1])
     pieces, arrived = history[None], first
     for bit in gather_bits[1:]:
         pieces = join("gather", pieces, arrived, 0)
@@ -252,11 +262,8 @@
     n_hops = len(exchange_bits)
 
     def select(name, groups, rows, weight):
-        def request(d):
-            return sum(((d >> i) & 1) << (n_hops - 1 - i) for i in range(n_hops)) or None
-
         return call(
-            lambda *refs: select_kernel(plan, [[request(d) for d in g] for g in groups], *refs),
+            lambda *refs: select_kernel(plan, groups, *refs),
             name,
             [pltpu.VMEM((n, size), jnp.bfloat16) for n in rows],
             code,
@@ -284,13 +291,18 @@
                 send = jnp.concatenate([held[d] for d in onward], axis=0)
             passed = hop(send, bit)
         if i == n_hops - 1:
-            keep, turned, *maps = call(
+            keep, turned, targets, *maps = call(
                 lambda *refs: turn_kernel(plan, *refs),
                 "turn",
-                [in_vmem(keep), pltpu.VMEM((tile_count * size, size), tile_blocks.dtype)]
+                [
+                    in_vmem(keep),
+                    pltpu.VMEM((tile_count * size, size), tile_blocks.dtype),
+                    pltpu.VMEM((tile_count, size), jnp.int32),
+                ]
                 + [pltpu.VMEM((tile_count, plan.slots << k), jnp.bfloat16) for k in range(n_hops)],
                 keep,
                 own_code,
+                tile_target[None],
                 tile_blocks,
                 weight=4,
             )
@@ -298,20 +310,26 @@
         for k, d in enumerate(onward):
             here = d ^ (1 << i)
             held[here] = jnp.concatenate([held[here], passed[k * rows : (k + 1) * rows]], axis=0)
-    mine = call(spread_kernel, "spread", in_vmem(keep), keep, *maps, *landed)
+    mine = call(
+        couple_kernel,
+        "couple",
+        pltpu.VMEM((slab_blocks, size), jnp.float32),
+        turned,
+        targets,
+        keep,
+        *maps,
+        *landed,
+    )
     if n_lag == 2:
         other = lax.ppermute(mine, "lag", [(0, 1), (1, 0)])
     else:
         other = lax.psum(mine, "lag") - mine
-
     solved = call(
-        couple_kernel,
-        "couple",
+        solve_kernel,
+        "solve",
         jax.ShapeDtypeStruct((slab_blocks, size), jnp.float32),
         mine,
         other,
-        turned,
-        tile_target[None],
         incident.reshape(slab_blocks, size),
         self_inv,
     )

time: 21.1 us -> 21 us (level)
    ppermute x7, waiting for transfers between devices: 2.97 us -> 3.18 us  [hop(): return lax.ppermute(value, ('blk', 'lag'), pairs)]
  transfers between devices with their start and end apart: 8 -> 8, of which waited for: 5 -> 6; matrix products, arithmetic and copies ran while one was open for 0% -> 0% of each run, Pallas kernels for 8% -> 8%
where the time goes in v6:
time: 21 us; the launch traced here: 20.8 us
  starting transfers between devices  13.1 us (62%)
  waiting for transfers between devices  4.01 us (19%)
  Pallas kernels  3.57 us (17%)
    ppermute x7, starting transfers between devices, hop(): return lax.ppermute(value, ('blk', 'lag'), pairs)  12.7 us
    pallas_call x9, Pallas kernels, call(): pl.pallas_call(kernel, out_shape=outs, in_specs=[VMEM] * len(operands), o...  3.57 us
    ppermute x7, waiting for transfers between devices, hop(): return lax.ppermute(value, ('blk', 'lag'), pairs)  3.18 us
    ppermute x1, waiting for transfers between devices, body(): other = lax.ppermute(mine, 'lag', [(0, 1), (1, 0)])  0.82 us
    ppermute x1, starting transfers between devices, body(): other = lax.ppermute(mine, 'lag', [(0, 1), (1, 0)])  0.45 us
  transfers between devices with their start and end apart: 8, of which 6 were waited for; matrix products, arithmetic and copies ran while one was open for 0% of the time, Pallas kernels for 8%

profile of v6, /device:TPU:0, one launch (start us, length us, event | category | flops | bytes accessed | tf_op | source)
XLA Modules:
  0.0 20.8 jit_solution(5233322884714087039)
XLA Ops:
  0.0 3.0 %collective-permute-start.2 = (bf16[1,32,1024]{2,1,0:T(8,128)(2,1)}, bf16[1,32,1024]{2,1,0:T(8,128)(2,1)S(1)}, u32[]{:S(2)}, u32[]{:S(2)}) collective-permute-start(bf16[1,32,1024]{2,1,0:T(8,128)(2,1)} %bitcast.7), channel_id=1, source_target_pairs={{0,2},{1,5},{2,0},{3,7},{4,6},{5,1},{6,4},{7,3},{8,10},{9,13},{10,... | collective-permute-start | bytes 196616 | tf_op jit(solution)/shard_map/ppermute | solution.py:232
  3.0 0.0 copy-done.3
  3.0 0.0 copy-done.4
  3.0 0.0 copy-done.5
  3.1 0.1 request.1.mine_ref.refs_1_
  3.2 1.8 %collective-permute-start = (s32[1,256]{1,0:T(1,128)S(1)}, s32[1,256]{1,0:T(1,128)S(1)}, u32[]{:S(2)}, u32[]{:S(2)}) collective-permute-start(s32[1,256]{1,0:T(1,128)S(1)} %request.1.mine_ref.refs_1_), channel_id=1, source_target_pairs={{0,17},{1,16},{2,19},{3,18},{4,21},{5,20},{6,23},{7,22},{8,25},{9,... | collective-permute-start | bytes 3080 | tf_op jit(solution)/shard_map/ppermute | solution.py:232
  5.0 0.5 %collective-permute-done.2.other_ref = bf16[1,32,1024]{2,1,0:T(8,128)(2,1)S(1)} collective-permute-done((bf16[1,32,1024]{2,1,0:T(8,128)(2,1)}, bf16[1,32,1024]{2,1,0:T(8,128)(2,1)S(1)}, u32[]{:S(2)}, u32[]{:S(2)}) %collective-permute-start.2) | collective-permute-done | bytes 65568 | tf_op jit(solution)/shard_map/ppermute | solution.py:232
  5.5 0.0 copy-done.1
  5.5 1.6 %collective-permute-start.3 = (bf16[2,32,1024]{2,1,0:T(8,128)(2,1)S(1)}, bf16[2,32,1024]{2,1,0:T(8,128)(2,1)S(1)}, u32[]{:S(2)}, u32[]{:S(2)}) collective-permute-start(bf16[2,32,1024]{2,1,0:T(8,128)(2,1)S(1)} %gather.1.refs_2_), channel_id=1, source_target_pairs={{0,5},{1,2},{2,7},{3,0},{4,1},{5,6},{6,3},{7,4},{8,13},{9,10},{10,... | collective-permute-start | bytes 393224 | tf_op jit(solution)/shard_map/ppermute | solution.py:232
  7.1 0.0 collective-permute-done.other_ref
  7.1 1.7 %collective-permute-start.1 = (s32[2,256]{1,0:T(2,128)S(1)}, s32[2,256]{1,0:T(2,128)S(1)}, u32[]{:S(2)}, u32[]{:S(2)}) collective-permute-start(s32[2,256]{1,0:T(2,128)S(1)} %join.1.refs_0_), channel_id=1, source_target_pairs={{0,9},{1,8},{2,11},{3,10},{4,13},{5,12},{6,15},{7,14},{8,1},{9,0},... | collective-permute-start | bytes 6152 | tf_op jit(solution)/shard_map/ppermute | solution.py:232
  8.9 1.3 %collective-permute-done.1.refs_1_ = s32[2,256]{1,0:T(2,128)S(1)} collective-permute-done((s32[2,256]{1,0:T(2,128)S(1)}, s32[2,256]{1,0:T(2,128)S(1)}, u32[]{:S(2)}, u32[]{:S(2)}) %collective-permute-start.1) | collective-permute-done | bytes 2080 | tf_op jit(solution)/shard_map/ppermute | solution.py:232
  10.2 0.0 collective-permute-done.3.refs_3_
  10.2 0.2 %select_send.1 = bf16[48,128]{1,0:T(8,128)(2,1)S(1)} custom-call(s32[2,256]{1,0:T(2,128)S(1)} %join.1.refs_0_, s32[2,256]{1,0:T(2,128)S(1)} %collective-permute-done.1.refs_1_, bf16[2,32,1024]{2,1,0:T(8,128)(2,1)S(1)} %gather.1.refs_2_, bf16[2,32,1024]{2,1,0:T(8,128)(2,1)S(1)} %collective-permute-done.3.refs_3_), custom_call_target="tpu_custom_call" | custom-call | flops 68719476736 | bytes 268435456 | tf_op jit(solution)/shard_map/select_send/pallas_call | solution.py:26
  10.4 0.0 copy-start.6
  10.4 0.0 copy-start.7
  10.4 2.8 %collective-permute-start.5 = (bf16[48,128]{1,0:T(8,128)(2,1)S(1)}, bf16[48,128]{1,0:T(8,128)(2,1)S(1)}, u32[]{:S(2)}, u32[]{:S(2)}) collective-permute-start(bf16[48,128]{1,0:T(8,128)(2,1)S(1)} %select_send.1), channel_id=1, source_target_pairs={{0,17},{1,16},{2,19},{3,18},{4,21},{5,20},{6,23},{7,22},{8,25},{9,... | collective-permute-start | bytes 36872 | tf_op jit(solution)/shard_map/ppermute | solution.py:232
  13.2 0.3 %select_keep.1 = (bf16[48,128]{1,0:T(8,128)(2,1)S(1)}, bf16[48,128]{1,0:T(8,128)(2,1)S(1)}, bf16[128,128]{1,0:T(8,128)(2,1)S(1)}) custom-call(s32[2,256]{1,0:T(2,128)S(1)} %join.1.refs_0_, s32[2,256]{1,0:T(2,128)S(1)} %collective-permute-done.1.refs_1_, bf16[2,32,1024]{2,1,0:T(8,128)(2,1)S(1)} %gather.1.refs_2_, ...), custom_call_target="tpu_custom_call" | custom-call | flops 68719476736 | bytes 268435456 | tf_op jit(solution)/shard_map/select_keep/pallas_call | solution.py:26
  13.6 0.1 collective-permute-start.4
  13.7 1.0 %collective-permute-done.5 = bf16[48,128]{1,0:T(8,128)(2,1)S(1)} collective-permute-done((bf16[48,128]{1,0:T(8,128)(2,1)S(1)}, bf16[48,128]{1,0:T(8,128)(2,1)S(1)}, u32[]{:S(2)}, u32[]{:S(2)}) %collective-permute-start.5) | collective-permute-done | bytes 12320 | tf_op jit(solution)/shard_map/ppermute | solution.py:232
  14.6 1.6 %collective-permute-start.6 = (bf16[96,128]{1,0:T(8,128)(2,1)S(1)}, bf16[96,128]{1,0:T(8,128)(2,1)S(1)}, u32[]{:S(2)}, u32[]{:S(2)}) collective-permute-start(bf16[96,128]{1,0:T(8,128)(2,1)S(1)} %pad_maximum_fusion), channel_id=1, source_target_pairs={{0,9},{1,8},{2,11},{3,10},{4,13},{5,12},{6,15},{7,14},{8,1},{9,0},... | collective-permute-start | bytes 73736 | tf_op jit(solution)/shard_map/ppermute | solution.py:232
  16.2 0.0 copy-done.7
  16.2 1.2 %turn.1 = (bf16[128,128]{1,0:T(8,128)(2,1)S(1)}, bf16[16384,128]{1,0:T(8,128)(2,1)S(1)}, s32[128,128]{1,0:T(8,128)S(1)}, bf16[128,48]{1,0:T(8,128)(2,1)S(1)}, bf16[128,96]{1,0:T(8,128)(2,1)S(1)}) custom-call(bf16[128,128]{1,0:T(8,128)(2,1)S(1)} %get-tuple-element.13.refs_0_, s32[1,256]{1,0:T(1,128)S(1)} %request.1.mine_ref.refs_1_, s32[1,128]{1,0:T(1,128)S(1)} %bitcast.13, ...), custom_call_target="tpu_custom_call" | custom-call | flops 17179869184 | bytes 67108864 | tf_op jit(solution)/shard_map/turn/pallas_call | solution.py:26
  17.5 0.0 copy-start
  17.5 0.0 copy-start.2
  17.5 0.2 collective-permute-done.4.refs_2_
  17.7 0.3 %collective-permute-done.6.refs_3_ = bf16[96,128]{1,0:T(8,128)(2,1)S(1)} collective-permute-done((bf16[96,128]{1,0:T(8,128)(2,1)S(1)}, bf16[96,128]{1,0:T(8,128)(2,1)S(1)}, u32[]{:S(2)}, u32[]{:S(2)}) %collective-permute-start.6) | collective-permute-done | bytes 24608 | tf_op jit(solution)/shard_map/ppermute | solution.py:232
  17.9 0.8 %couple.1.mine_ref = f32[8,128]{1,0:T(8,128)S(1)} custom-call(bf16[16384,128]{1,0:T(8,128)(2,1)S(1)} %get-tuple-element.14.turned_ref, s32[128,128]{1,0:T(8,128)S(1)} %get-tuple-element.15.target_ref, bf16[128,128]{1,0:T(8,128)(2,1)S(1)} %get-tuple-element.16.keep_ref, bf16[128,48]{1,0:T(8,128)(2,1)S(1)} %get-tuple-element.17.refs_0_, ...), custom_call_target="tpu_custom_call" | custom-call | tf_op jit(solution)/shard_map/couple/pallas_call | solution.py:26
  18.7 0.5 %collective-permute-start.7 = (f32[8,128]{1,0:T(8,128)S(1)}, f32[8,128]{1,0:T(8,128)S(1)}, u32[]{:S(2)}, u32[]{:S(2)}) collective-permute-start(f32[8,128]{1,0:T(8,128)S(1)} %couple.1.mine_ref), channel_id=1, source_target_pairs={{0,1},{1,0},{2,3},{3,2},{4,5},{5,4},{6,7},{7,6},{8,9},{9,8},{10,11... | collective-permute-start | bytes 12296 | tf_op jit(solution)/shard_map/ppermute | solution.py:324
  19.2 0.8 %collective-permute-done.7.other_ref = f32[8,128]{1,0:T(8,128)S(1)} collective-permute-done((f32[8,128]{1,0:T(8,128)S(1)}, f32[8,128]{1,0:T(8,128)S(1)}, u32[]{:S(2)}, u32[]{:S(2)}) %collective-permute-start.7) | collective-permute-done | bytes 4128 | tf_op jit(solution)/shard_map/ppermute | solution.py:324
  20.0 0.0 copy-done.2
  20.0 0.8 %solve.1 = f32[8,128]{1,0:T(8,128)} custom-call(f32[8,128]{1,0:T(8,128)S(1)} %couple.1.mine_ref, f32[8,128]{1,0:T(8,128)S(1)} %collective-permute-done.7.other_ref, f32[8,128]{1,0:T(8,128)S(1)} %bitcast.9, f32[8,128,128]{2,1,0:T(8,128)S(1)} %copy-done), custom_call_target="tpu_custom_call" | custom-call | tf_op jit(solution)/shard_map/solve/pallas_call | solution.py:26
  (10 shorter events, 0.0 us)
Async XLA Ops:
  0.0 3.0 %copy-start.3 = (s32[128]{0:T(128)S(1)}, s32[128]{0:T(128)}, u32[]{:S(2)}) copy-start(s32[128]{0:T(128)} %param.11) | copy-start | bytes 1540
  0.0 3.0 %copy-start.4 = (s32[128]{0:T(128)S(1)}, s32[128]{0:T(128)}, u32[]{:S(2)}) copy-start(s32[128]{0:T(128)} %param.12) | copy-start | bytes 1540
  0.0 3.0 %copy-start.5 = (s32[128]{0:T(128)S(1)}, s32[128]{0:T(128)}, u32[]{:S(2)}) copy-start(s32[128]{0:T(128)} %param.13) | copy-start | bytes 1540
  0.0 5.5 %copy-start.1 = (bf16[32,1024]{1,0:T(8,128)(2,1)S(1)}, bf16[32,1024]{1,0:T(8,128)(2,1)}, u32[]{:S(2)}) copy-start(bf16[32,1024]{1,0:T(8,128)(2,1)} %param.8) | copy-start | bytes 196612
  0.0 5.5 %collective-permute-start.2 = (bf16[1,32,1024]{2,1,0:T(8,128)(2,1)}, bf16[1,32,1024]{2,1,0:T(8,128)(2,1)S(1)}, u32[]{:S(2)}, u32[]{:S(2)}) collective-permute-start(bf16[1,32,1024]{2,1,0:T(8,128)(2,1)} %bitcast.7), channel_id=1, source_target_pairs={{0,2},{1,5},{2,0},{3,7},{4,6},{5,1},{6,4},{7,3},{8,10},{9,13},{10,... | collective-permute-start | bytes 196616 | tf_op jit(solution)/shard_map/ppermute | solution.py:232
  3.2 4.0 %collective-permute-start = (s32[1,256]{1,0:T(1,128)S(1)}, s32[1,256]{1,0:T(1,128)S(1)}, u32[]{:S(2)}, u32[]{:S(2)}) collective-permute-start(s32[1,256]{1,0:T(1,128)S(1)} %request.1.mine_ref.refs_1_), channel_id=1, source_target_pairs={{0,17},{1,16},{2,19},{3,18},{4,21},{5,20},{6,23},{7,22},{8,25},{9,... | collective-permute-start | bytes 3080 | tf_op jit(solution)/shard_map/ppermute | solution.py:232
  5.5 4.7 %collective-permute-start.3 = (bf16[2,32,1024]{2,1,0:T(8,128)(2,1)S(1)}, bf16[2,32,1024]{2,1,0:T(8,128)(2,1)S(1)}, u32[]{:S(2)}, u32[]{:S(2)}) collective-permute-start(bf16[2,32,1024]{2,1,0:T(8,128)(2,1)S(1)} %gather.1.refs_2_), channel_id=1, source_target_pairs={{0,5},{1,2},{2,7},{3,0},{4,1},{5,6},{6,3},{7,4},{8,13},{9,10},{10,... | collective-permute-start | bytes 393224 | tf_op jit(solution)/shard_map/ppermute | solution.py:232
  7.1 3.0 %collective-permute-start.1 = (s32[2,256]{1,0:T(2,128)S(1)}, s32[2,256]{1,0:T(2,128)S(1)}, u32[]{:S(2)}, u32[]{:S(2)}) collective-permute-start(s32[2,256]{1,0:T(2,128)S(1)} %join.1.refs_0_), channel_id=1, source_target_pairs={{0,9},{1,8},{2,11},{3,10},{4,13},{5,12},{6,15},{7,14},{8,1},{9,0},... | collective-permute-start | bytes 6152 | tf_op jit(solution)/shard_map/ppermute | solution.py:232
  10.4 5.8 %copy-start.6 = (bf16[128,128,128]{2,1,0:T(8,128)(2,1)S(1)}, bf16[128,128,128]{2,1,0:T(8,128)(2,1)}, u32[]{:S(2)}) copy-start(bf16[128,128,128]{2,1,0:T(8,128)(2,1)} %refs_3_.1) | copy-start | bytes 12582916
  10.4 5.8 %copy-start.7 = (s32[128]{0:T(128)S(1)}, s32[128]{0:T(128)}, u32[]{:S(2)}) copy-start(s32[128]{0:T(128)} %param.10) | copy-start | bytes 1540
  10.4 4.2 %collective-permute-start.5 = (bf16[48,128]{1,0:T(8,128)(2,1)S(1)}, bf16[48,128]{1,0:T(8,128)(2,1)S(1)}, u32[]{:S(2)}, u32[]{:S(2)}) collective-permute-start(bf16[48,128]{1,0:T(8,128)(2,1)S(1)} %select_send.1), channel_id=1, source_target_pairs={{0,17},{1,16},{2,19},{3,18},{4,21},{5,20},{6,23},{7,22},{8,25},{9,... | collective-permute-start | bytes 36872 | tf_op jit(solution)/shard_map/ppermute | solution.py:232
  13.6 4.1 %collective-permute-start.4 = (bf16[48,128]{1,0:T(8,128)(2,1)S(1)}, bf16[48,128]{1,0:T(8,128)(2,1)S(1)}, u32[]{:S(2)}, u32[]{:S(2)}) collective-permute-start(bf16[48,128]{1,0:T(8,128)(2,1)S(1)} %get-tuple-element.19), channel_id=1, source_target_pairs={{0,17},{1,16},{2,19},{3,18},{4,21},{5,20},{6,23},{7,22},{8,25},{9,... | collective-permute-start | bytes 36872 | tf_op jit(solution)/shard_map/ppermute | solution.py:232
  14.6 3.3 %collective-permute-start.6 = (bf16[96,128]{1,0:T(8,128)(2,1)S(1)}, bf16[96,128]{1,0:T(8,128)(2,1)S(1)}, u32[]{:S(2)}, u32[]{:S(2)}) collective-permute-start(bf16[96,128]{1,0:T(8,128)(2,1)S(1)} %pad_maximum_fusion), channel_id=1, source_target_pairs={{0,9},{1,8},{2,11},{3,10},{4,13},{5,12},{6,15},{7,14},{8,1},{9,0},... | collective-permute-start | bytes 73736 | tf_op jit(solution)/shard_map/ppermute | solution.py:232
  17.5 2.5 %copy-start = (f32[8,128,128]{2,1,0:T(8,128)S(1)}, f32[8,128,128]{2,1,0:T(8,128)}, u32[]{:S(2)}) copy-start(f32[8,128,128]{2,1,0:T(8,128)} %inverse_ref.1) | copy-start | bytes 1572868
  17.5 2.5 %copy-start.2 = (f32[1024]{0:T(1024)S(1)}, f32[1024]{0:T(1024)}, u32[]{:S(2)}) copy-start(f32[1024]{0:T(1024)} %param.14) | copy-start | bytes 12292
  18.7 1.3 %collective-permute-start.7 = (f32[8,128]{1,0:T(8,128)S(1)}, f32[8,128]{1,0:T(8,128)S(1)}, u32[]{:S(2)}, u32[]{:S(2)}) collective-permute-start(f32[8,128]{1,0:T(8,128)S(1)} %couple.1.mine_ref), channel_id=1, source_target_pairs={{0,1},{1,0},{2,3},{3,2},{4,5},{5,4},{6,7},{7,6},{8,9},{9,8},{10,11... | collective-permute-start | bytes 12296 | tf_op jit(solution)/shard_map/ppermute | solution.py:324

commit v7 on v6

--- a/solution.py
+++ b/solution.py
@@ -22,12 +22,13 @@
     split: tuple
 
 
-def call(kernel, name, outs, *operands, weight=0):
+def call(kernel, name, outs, *operands, weight=0, scratch=()):
     return pl.pallas_call(
         kernel,
         out_shape=outs,
         in_specs=[VMEM] * len(operands),
         out_specs=jax.tree.map(lambda _: VMEM, outs),
+        scratch_shapes=scratch,
         compiler_params=pltpu.CompilerParams(vmem_limit_bytes=16 * 1024 * 1024),
         cost_estimate=pl.CostEstimate(
             flops=weight << 32, bytes_accessed=weight << 24, transcendentals=0
@@ -129,58 +130,84 @@
     slot_id = lax.broadcasted_iota(jnp.int32, (plan.slots, tiles), 0)
     for group, out_ref in zip(groups, out_refs):
         for k, d in enumerate(group):
-            if d == 0:
-                out_ref[...] = picked(jnp.transpose(jnp.broadcast_to(row[:1], (size, tiles))))
-            else:
-                there = jnp.where(slot_id == slot[d : d + 1], row[d : d + 1] + 1, 0)
-                chosen = jnp.sum(there, axis=1, keepdims=True) - 1
-                chosen = jnp.broadcast_to(chosen, (plan.slots, size))
-                out_ref[k * plan.slots : (k + 1) * plan.slots, :] = picked(chosen)
-
-
-def turn_kernel(
-    plan, held_ref, code_ref, target_ref, tiles_ref, passed_ref, turned_ref, column_ref, *map_refs
+            there = jnp.where(slot_id == slot[d : d + 1], row[d : d + 1] + 1, 0)
+            chosen = jnp.sum(there, axis=1, keepdims=True) - 1
+            chosen = jnp.broadcast_to(chosen, (plan.slots, size))
+            out_ref[k * plan.slots : (k + 1) * plan.slots, :] = picked(chosen)
+
+
+def order_kernel(
+    plan, hops, count, code_ref, target_ref, held_ref, tiles_ref, passed_ref, tile_ref, column_ref, turned_ref, *scratch
 ):
     tiles, size = tiles_ref.shape[:2]
     passed_ref[...] = held_ref[...]
-    column_ref[...] = jnp.transpose(jnp.broadcast_to(target_ref[...], (size, tiles)))
     blk, lag = lax.axis_index("blk"), lax.axis_index("lag")
     source = code_ref[:, :tiles] & ((1 << plan.shift) - 1)
     place = code_ref[:, tiles:]
     apart = (source >> plan.slab_shift) ^ blk
     piece, high = apart & (plan.pieces - 1), apart >> (plan.pieces.bit_length() - 1)
-    hops = len(map_refs)
     plane = sum(((high >> (hops - 1 - i)) & 1) << i for i in range(hops))
     sender = jnp.zeros_like(plane) + lag
     if plan.split:
-        for i in range(len(map_refs)):
+        for i in range(hops):
             sender = sender ^ ((plane >> i) & 1)
     rank = ordinal(plan, piece, sender)
-    for i, map_ref in enumerate(map_refs):
-        column = ((plane - (1 << i)) * plan.slots) + rank * plan.cap + place
-        column = jnp.where((rank >= 0) & ((plane >> i) == 1), column, -1)
-        wide = -(-map_ref.shape[1] // size) * size
-        column = jnp.transpose(jnp.broadcast_to(column, (wide, tiles)))[:, : map_ref.shape[1]]
-        lane = lax.broadcasted_iota(jnp.int32, map_ref.shape, 1)
-        map_ref[...] = jnp.where(column == lane, 1.0, 0.0).astype(map_ref.dtype)
-    for t in range(tiles):
-        turned_ref[t * size : (t + 1) * size, :] = jnp.transpose(tiles_ref[t])
-
-
-def couple_kernel(turned_ref, target_ref, keep_ref, *refs):
-    *refs, out_ref = refs
-    hops = len(refs) // 2
-    vectors = keep_ref[...].astype(jnp.float32)
-    for map_ref, rows_ref in zip(refs[:hops], refs[hops:]):
-        vectors = vectors + jnp.dot(
-            map_ref[...], rows_ref[...], preferred_element_type=jnp.float32
-        )
-    tiles, size = vectors.shape
-    blocks = out_ref.shape[0]
-    target = target_ref[...]
-    left = jnp.stack([jnp.where(target == b, vectors, 0.0) for b in range(blocks)], axis=0)
-    left = left.astype(jnp.bfloat16).reshape(blocks, tiles * size)
-    out_ref[...] = jnp.dot(left, turned_ref[...], preferred_element_type=jnp.float32)
+    slot = jnp.where(rank >= 0, plane * plan.slots + rank * plan.cap + place, -1)
+    wide = tile_ref.shape[1]
+    slot = jnp.transpose(jnp.broadcast_to(slot, (wide, tiles)))
+    target = jnp.transpose(jnp.broadcast_to(target_ref[...], (wide, tiles)))
+    here = slot == lax.broadcasted_iota(jnp.int32, (tiles, wide), 1)
+    tile = jnp.where(here, lax.broadcasted_iota(jnp.int32, (tiles, wide), 0), 0)
+    tile_ref[...] = jnp.minimum(jnp.sum(tile, axis=0, keepdims=True), tiles - 1)
+    target = jnp.sum(jnp.where(here, target + 1, 0), axis=0, keepdims=True) - 1
+    column_ref[...] = jnp.transpose(jnp.broadcast_to(target, (size, wide)))[: column_ref.shape[0], :]
+    turn(0, count, tile_ref, tiles_ref, turned_ref, *scratch)
+
+
+def turn(first, count, tile_ref, tiles_ref, turned_ref, index, sem):
+    copy = pltpu.make_async_copy(tile_ref, index, sem)
+    copy.start()
+    copy.wait()
+    size = tiles_ref.shape[1]
+    for s in range(count):
+        turned_ref[s * size : (s + 1) * size, :] = jnp.transpose(tiles_ref[index[0, first + s]])
+
+
+def turn_kernel(first, count, held_ref, tile_ref, tiles_ref, passed_ref, turned_ref, *scratch):
+    passed_ref[...] = held_ref[...]
+    turn(first, count, tile_ref, tiles_ref, turned_ref, *scratch)
+
+
+def products(first, column_ref, row_refs, turned_refs, blocks):
+    rows = jnp.concatenate([r[...] for r in row_refs], axis=0).astype(jnp.float32)
+    count, size = rows.shape
+    target = column_ref[first : first + count, :]
+    left = jnp.stack([jnp.where(target == b, rows, 0.0) for b in range(blocks)], axis=0)
+    left = left.astype(jnp.bfloat16)
+    total = jnp.zeros((blocks, size), jnp.float32)
+    for turned_ref, start, held in turned_refs:
+        low, high = max(first, start), min(first + count, start + held)
+        if low < high:
+            part = left[:, low - first : high - first].reshape(blocks, (high - low) * size)
+            total = total + jnp.dot(
+                part,
+                turned_ref[(low - start) * size : (high - start) * size, :],
+                preferred_element_type=jnp.float32,
+            )
+    return total
+
+
+def early_kernel(cuts, n_rows, column_ref, tile_ref, tiles_ref, turned0_ref, turned1_ref, *refs):
+    row_refs, (sum_ref, turned_ref, index, sem) = refs[:n_rows], refs[n_rows:]
+    turned = [(turned0_ref, cuts[0], cuts[1] - cuts[0]), (turned1_ref, cuts[1], cuts[2] - cuts[1])]
+    sum_ref[...] = products(0, column_ref, row_refs, turned, sum_ref.shape[0])
+    turn(cuts[2], cuts[3] - cuts[2], tile_ref, tiles_ref, turned_ref, index, sem)
+
+
+def couple_kernel(cuts, early_ref, column_ref, turned1_ref, turned2_ref, rows_ref, out_ref):
+    turned = [(turned1_ref, cuts[1], cuts[2] - cuts[1]), (turned2_ref, cuts[2], cuts[3] - cuts[2])]
+    first = cuts[3] - rows_ref.shape[0]
+    out_ref[...] = early_ref[...] + products(first, column_ref, [rows_ref], turned, out_ref.shape[0])
 
 
 def solve_kernel(mine_ref, other_ref, incident_ref, inverse_ref, out_ref):
@@ -244,11 +271,20 @@
         tile_source[None],
         tile_offset[None],
         delay_bins[None],
-    )
-
-    def join(name, mine, other, weight):
+        weight=0,
+    )
+
+    def join(name, mine, other, weight, *extra):
         shape = (2 * mine.shape[0],) + mine.shape[1:]
-        return call(join_kernel, name, pltpu.VMEM(shape, mine.dtype), mine, other, weight=weight)
+        return call(
+            lambda *refs: join_kernel(refs[0], refs[1], refs[-1]),
+            name,
+            pltpu.VMEM(shape, mine.dtype),
+            mine,
+            other,
+            *extra,
+            weight=weight,
+        )
 
     own_code = code
     for bit in exchange_bits[:-1]:
@@ -256,16 +292,37 @@
     far_code = hop(code, exchange_bits[-1])
     pieces, arrived = history[None], first
     for bit in gather_bits[1:]:
-        pieces = join("gather", pieces, arrived, 0)
+        pieces = join("gather", pieces, arrived, 0, tile_blocks)
         arrived = hop(pieces, bit, gather_bits[0]) if paired else hop(pieces, bit)
 
     n_hops = len(exchange_bits)
 
-    def select(name, groups, rows, weight):
+    n_slots = plan.slots << n_hops
+    cuts = [0, n_slots // 64 * 16, n_slots // 192 * 112, n_slots]
+    wide = -(-n_slots // 128) * 128
+    scratch = [pltpu.SMEM((1, wide), jnp.int32), pltpu.SemaphoreType.DMA]
+
+    def turned_tiles(run):
+        return pltpu.VMEM(((cuts[run + 1] - cuts[run]) * size, size), tile_blocks.dtype)
+
+    code, slot_tiles, columns, turned0 = call(
+        lambda *refs: order_kernel(plan, n_hops, cuts[1], *refs),
+        "order",
+        (in_vmem(code), pltpu.VMEM((1, wide), jnp.int32), pltpu.VMEM((n_slots, size), jnp.int32), turned_tiles(0)),
+        own_code,
+        tile_target[None],
+        code,
+        tile_blocks,
+        weight=0,
+        scratch=scratch,
+    )
+
+    def select(name, groups, rows, weight, *after):
         return call(
-            lambda *refs: select_kernel(plan, groups, *refs),
+            lambda *refs: select_kernel(plan, groups, *refs[len(after) :]),
             name,
             [pltpu.VMEM((n, size), jnp.bfloat16) for n in rows],
+            *after,
             code,
             far_code,
             pieces,
@@ -276,49 +333,58 @@
     def passes(i):
         return [d for d in range(1 << n_hops) if d >> i > 1 and (d >> i) & 1 and d % (1 << i) == 0]
 
-    first_pass = passes(0)
+    first_pass = passes(0) + [1]
     (send,) = select("select_send", [first_pass], [plan.slots * len(first_pass)], 16)
-    rest = [1] + [d for d in range(2, 1 << n_hops) if d % 2 == 0]
-    *picks, keep = select(
-        "select_keep", [[d] for d in rest] + [[0]], [plan.slots] * len(rest) + [tile_count], 16
-    )
+    rest = [d for d in range(2, 1 << n_hops) if d % 2 == 0]
+    *picks, keep = select("select_keep", [[d] for d in rest + [0]], [plan.slots] * (len(rest) + 1), 16, send)
     held = dict(zip(rest, picks))
+    keep, turned1 = call(
+        lambda *refs: turn_kernel(cuts[1], cuts[2] - cuts[1], *refs),
+        "turn",
+        (in_vmem(keep), turned_tiles(1)),
+        keep,
+        slot_tiles,
+        tile_blocks,
+        weight=4,
+        scratch=scratch,
+    )
     landed = []
     for i, bit in enumerate(exchange_bits):
         onward, rows = passes(i), plan.slots << i
         if onward:
             if i:
-                send = jnp.concatenate([held[d] for d in onward], axis=0)
+                send = jnp.concatenate([held[d] for d in onward + [1 << i]], axis=0)
             passed = hop(send, bit)
+            landed.append(passed[len(onward) * rows :])
         if i == n_hops - 1:
-            keep, turned, targets, *maps = call(
-                lambda *refs: turn_kernel(plan, *refs),
-                "turn",
-                [
-                    in_vmem(keep),
-                    pltpu.VMEM((tile_count * size, size), tile_blocks.dtype),
-                    pltpu.VMEM((tile_count, size), jnp.int32),
-                ]
-                + [pltpu.VMEM((tile_count, plan.slots << k), jnp.bfloat16) for k in range(n_hops)],
+            early, turned2 = call(
+                lambda *refs: early_kernel(cuts, n_hops, *refs),
+                "early",
+                (pltpu.VMEM((slab_blocks, size), jnp.float32), turned_tiles(2)),
+                columns,
+                slot_tiles,
+                tile_blocks,
+                turned0,
+                turned1,
                 keep,
-                own_code,
-                tile_target[None],
-                tile_blocks,
+                *landed,
                 weight=4,
+                scratch=scratch,
             )
-        landed.append(hop(held[1 << i], bit))
+        if not onward:
+            landed.append(hop(held[1 << i], bit))
         for k, d in enumerate(onward):
             here = d ^ (1 << i)
             held[here] = jnp.concatenate([held[here], passed[k * rows : (k + 1) * rows]], axis=0)
     mine = call(
-        couple_kernel,
+        lambda *refs: couple_kernel(cuts, *refs),
         "couple",
         pltpu.VMEM((slab_blocks, size), jnp.float32),
-        turned,
-        targets,
-        keep,
-        *maps,
-        *landed,
+        early,
+        columns,
+        turned1,
+        turned2,
+        landed[-1],
     )
     if n_lag == 2:
         other = lax.ppermute(mine, "lag", [(0, 1), (1, 0)])

time: 21 us -> 20.9 us (level)
  waiting for transfers between devices: 4.01 us -> 1.84 us
  Pallas kernels: 3.57 us -> 5.65 us
    ppermute x7 -> x6, waiting for transfers between devices: 3.18 us -> 1.02 us  [hop(): return lax.ppermute(value, ('blk', 'lag'), pairs)]
    pallas_call x9 -> x11, Pallas kernels: 3.57 us -> 5.65 us  [call(): pl.pallas_call(kernel, out_shape=outs, in_specs=[VMEM] * len(operands), o...]
    ppermute x7 -> x6, starting transfers between devices: 12.7 us -> 12.6 us  [hop(): return lax.ppermute(value, ('blk', 'lag'), pairs)]
  transfers between devices with their start and end apart: 8 -> 7, of which waited for: 6 -> 5; matrix products, arithmetic and copies ran while one was open for 0% -> 0% of each run, Pallas kernels for 8% -> 19%
where the time goes in v7:
time: 20.9 us; the launch traced here: 20.8 us
  starting transfers between devices  13.1 us (63%)
  Pallas kernels  5.65 us (27%)
  waiting for transfers between devices  1.84 us (9%)
    ppermute x6, starting transfers between devices, hop(): return lax.ppermute(value, ('blk', 'lag'), pairs)  12.6 us
    pallas_call x11, Pallas kernels, call(): pl.pallas_call(kernel, out_shape=outs, in_specs=[VMEM] * len(operands), o...  5.65 us
    ppermute x6, waiting for transfers between devices, hop(): return lax.ppermute(value, ('blk', 'lag'), pairs)  1.02 us
    ppermute x1, waiting for transfers between devices, body(): other = lax.ppermute(mine, 'lag', [(0, 1), (1, 0)])  0.82 us
    ppermute x1, starting transfers between devices, body(): other = lax.ppermute(mine, 'lag', [(0, 1), (1, 0)])  0.49 us
  transfers between devices with their start and end apart: 7, of which 5 were waited for; matrix products, arithmetic and copies ran while one was open for 0% of the time, Pallas kernels for 19%

profile of v7, /device:TPU:0, one launch (start us, length us, event | category | flops | bytes accessed | tf_op | source)
XLA Modules:
  0.0 20.8 jit_solution(4030633808015376918)
XLA Ops:
  0.0 3.0 %collective-permute-start.2 = (bf16[1,32,1024]{2,1,0:T(8,128)(2,1)}, bf16[1,32,1024]{2,1,0:T(8,128)(2,1)S(1)}, u32[]{:S(2)}, u32[]{:S(2)}) collective-permute-start(bf16[1,32,1024]{2,1,0:T(8,128)(2,1)} %bitcast.7), channel_id=1, source_target_pairs={{0,2},{1,5},{2,0},{3,7},{4,6},{5,1},{6,4},{7,3},{8,10},{9,13},{10,... | collective-permute-start | bytes 196616 | tf_op jit(solution)/shard_map/ppermute | solution.py:259
  3.0 0.0 copy-done.4
  3.0 0.0 copy-done.5
  3.1 0.0 copy-done.6
  3.1 0.1 request.1.refs_0_
  3.2 1.8 %collective-permute-start = (s32[1,256]{1,0:T(1,128)S(1)}, s32[1,256]{1,0:T(1,128)S(1)}, u32[]{:S(2)}, u32[]{:S(2)}) collective-permute-start(s32[1,256]{1,0:T(1,128)S(1)} %request.1.refs_0_), channel_id=1, source_target_pairs={{0,17},{1,16},{2,19},{3,18},{4,21},{5,20},{6,23},{7,22},{8,25},{9,... | collective-permute-start | bytes 3080 | tf_op jit(solution)/shard_map/ppermute | solution.py:259
  5.0 0.5 %collective-permute-done.2.refs_1_ = bf16[1,32,1024]{2,1,0:T(8,128)(2,1)S(1)} collective-permute-done((bf16[1,32,1024]{2,1,0:T(8,128)(2,1)}, bf16[1,32,1024]{2,1,0:T(8,128)(2,1)S(1)}, u32[]{:S(2)}, u32[]{:S(2)}) %collective-permute-start.2) | collective-permute-done | bytes 65568 | tf_op jit(solution)/shard_map/ppermute | solution.py:259
  5.5 0.0 copy-done.2
  5.5 0.0 copy-done
  5.5 0.0 copy-start.7
  5.5 1.7 %collective-permute-start.3 = (bf16[2,32,1024]{2,1,0:T(8,128)(2,1)S(1)}, bf16[2,32,1024]{2,1,0:T(8,128)(2,1)S(1)}, u32[]{:S(2)}, u32[]{:S(2)}) collective-permute-start(bf16[2,32,1024]{2,1,0:T(8,128)(2,1)S(1)} %gather.1.refs_2_.refs_3_), channel_id=1, source_target_pairs={{0,5},{1,2},{2,7},{3,0},{4,1},{5,6},{6,3},{7,4},{8,13},{9,10},{10,... | collective-permute-start | bytes 393224 | tf_op jit(solution)/shard_map/ppermute | solution.py:259
  7.2 0.0 collective-permute-done.refs_1_
  7.2 1.7 %collective-permute-start.1 = (s32[2,256]{1,0:T(2,128)S(1)}, s32[2,256]{1,0:T(2,128)S(1)}, u32[]{:S(2)}, u32[]{:S(2)}) collective-permute-start(s32[2,256]{1,0:T(2,128)S(1)} %join.1.refs_2_), channel_id=1, source_target_pairs={{0,9},{1,8},{2,11},{3,10},{4,13},{5,12},{6,15},{7,14},{8,1},{9,0},... | collective-permute-start | bytes 6152 | tf_op jit(solution)/shard_map/ppermute | solution.py:259
  8.9 0.0 copy-done.7
  8.9 1.2 %order.1 = (s32[2,256]{1,0:T(2,128)S(1)}, s32[1,256]{1,0:T(1,128)S(1)}, s32[192,128]{1,0:T(8,128)S(1)}, bf16[6144,128]{1,0:T(8,128)(2,1)S(1)}) custom-call(s32[1,256]{1,0:T(1,128)S(1)} %request.1.refs_0_, s32[1,128]{1,0:T(1,128)S(1)} %bitcast.13, s32[2,256]{1,0:T(2,128)S(1)} %join.1.refs_2_, bf16[128,128,128]{2,1,0:T(8,128)(2,1)S(1)} %copy-done), custom_call_target="tpu_custom_call" | custom-call | tf_op jit(solution)/shard_map/order/pallas_call | solution.py:26
  10.1 0.1 collective-permute-done.1.refs_1_.refs_2_
  10.2 0.0 collective-permute-done.3.refs_3_.refs_4_
  10.2 0.3 %select_send.1.refs_0_ = bf16[96,128]{1,0:T(8,128)(2,1)S(1)} custom-call(s32[2,256]{1,0:T(2,128)S(1)} %get-tuple-element.18.refs_0_.refs_1_, s32[2,256]{1,0:T(2,128)S(1)} %collective-permute-done.1.refs_1_.refs_2_, bf16[2,32,1024]{2,1,0:T(8,128)(2,1)S(1)} %gather.1.refs_2_.refs_3_, bf16[2,32,1024]{2,1,0:T(8,128)(2,1)S(1)} %collective-permute-done.3.refs_3_.refs_4_), custom_call_target="tpu_custom_call" | custom-call | flops 68719476736 | bytes 268435456 | tf_op jit(solution)/shard_map/select_send/pallas_call | solution.py:26
  10.5 2.8 %collective-permute-start.4 = (bf16[96,128]{1,0:T(8,128)(2,1)S(1)}, bf16[96,128]{1,0:T(8,128)(2,1)S(1)}, u32[]{:S(2)}, u32[]{:S(2)}) collective-permute-start(bf16[96,128]{1,0:T(8,128)(2,1)S(1)} %select_send.1.refs_0_), channel_id=1, source_target_pairs={{0,17},{1,16},{2,19},{3,18},{4,21},{5,20},{6,23},{7,22},{8,25},{9,... | collective-permute-start | bytes 73736 | tf_op jit(solution)/shard_map/ppermute | solution.py:259
  13.3 0.3 %select_keep.1 = (bf16[48,128]{1,0:T(8,128)(2,1)S(1)}, bf16[48,128]{1,0:T(8,128)(2,1)S(1)}) custom-call(bf16[96,128]{1,0:T(8,128)(2,1)S(1)} %select_send.1.refs_0_, s32[2,256]{1,0:T(2,128)S(1)} %get-tuple-element.18.refs_0_.refs_1_, s32[2,256]{1,0:T(2,128)S(1)} %collective-permute-done.1.refs_1_.refs_2_, bf16[2,32,1024]{2,1,0:T(8,128)(2,1)S(1)} %gather.1.refs_2_.refs_3_, ...), custom_call_target="tpu_custom_call" | custom-call | flops 68719476736 | bytes 268435456 | tf_op jit(solution)/shard_map/select_keep/pallas_call | solution.py:26
  13.5 1.2 %turn.1 = (bf16[48,128]{1,0:T(8,128)(2,1)S(1)}, bf16[8192,128]{1,0:T(8,128)(2,1)S(1)}) custom-call(bf16[48,128]{1,0:T(8,128)(2,1)S(1)} %get-tuple-element.19.refs_0_, s32[1,256]{1,0:T(1,128)S(1)} %get-tuple-element.16.refs_1_, bf16[128,128,128]{2,1,0:T(8,128)(2,1)S(1)} %copy-done), custom_call_target="tpu_custom_call" | custom-call | flops 17179869184 | bytes 67108864 | tf_op jit(solution)/shard_map/turn/pallas_call | solution.py:26
  14.7 0.1 collective-permute-done.4
  14.8 1.6 %collective-permute-start.5 = (bf16[96,128]{1,0:T(8,128)(2,1)S(1)}, bf16[96,128]{1,0:T(8,128)(2,1)S(1)}, u32[]{:S(2)}, u32[]{:S(2)}) collective-permute-start(bf16[96,128]{1,0:T(8,128)(2,1)S(1)} %pad_maximum_fusion), channel_id=1, source_target_pairs={{0,9},{1,8},{2,11},{3,10},{4,13},{5,12},{6,15},{7,14},{8,1},{9,0},... | collective-permute-start | bytes 73736 | tf_op jit(solution)/shard_map/ppermute | solution.py:259
  16.4 1.3 %early.1 = (f32[8,128]{1,0:T(8,128)S(1)}, bf16[10240,128]{1,0:T(8,128)(2,1)S(1)}) custom-call(s32[192,128]{1,0:T(8,128)S(1)} %get-tuple-element.15.refs_0_.refs_1_, s32[1,256]{1,0:T(1,128)S(1)} %get-tuple-element.16.refs_1_, bf16[128,128,128]{2,1,0:T(8,128)(2,1)S(1)} %copy-done, bf16[6144,128]{1,0:T(8,128)(2,1)S(1)} %get-tuple-element.17.refs_3_, ...), custom_call_target="tpu_custom_call" | custom-call | flops 17179869184 | bytes 67108864 | tf_op jit(solution)/shard_map/early/pallas_call | solution.py:26
  17.7 0.0 copy-start.1
  17.7 0.0 copy-start.3
  17.7 0.3 %collective-permute-done.5.refs_4_ = bf16[96,128]{1,0:T(8,128)(2,1)S(1)} collective-permute-done((bf16[96,128]{1,0:T(8,128)(2,1)S(1)}, bf16[96,128]{1,0:T(8,128)(2,1)S(1)}, u32[]{:S(2)}, u32[]{:S(2)}) %collective-permute-start.5) | collective-permute-done | bytes 24608 | tf_op jit(solution)/shard_map/ppermute | solution.py:259
  18.1 0.5 %couple.1.mine_ref = f32[8,128]{1,0:T(8,128)S(1)} custom-call(f32[8,128]{1,0:T(8,128)S(1)} %get-tuple-element.22.refs_0_, s32[192,128]{1,0:T(8,128)S(1)} %get-tuple-element.15.refs_0_.refs_1_, bf16[8192,128]{1,0:T(8,128)(2,1)S(1)} %get-tuple-element.20.refs_4_.refs_2_, bf16[10240,128]{1,0:T(8,128)(2,1)S(1)} %get-tuple-element.23.refs_3_, ...), custom_call_target="tpu_custom_call" | custom-call | tf_op jit(solution)/shard_map/couple/pallas_call | solution.py:26
  18.6 0.5 %collective-permute-start.6 = (f32[8,128]{1,0:T(8,128)S(1)}, f32[8,128]{1,0:T(8,128)S(1)}, u32[]{:S(2)}, u32[]{:S(2)}) collective-permute-start(f32[8,128]{1,0:T(8,128)S(1)} %couple.1.mine_ref), channel_id=1, source_target_pairs={{0,1},{1,0},{2,3},{3,2},{4,5},{5,4},{6,7},{7,6},{8,9},{9,8},{10,11... | collective-permute-start | bytes 12296 | tf_op jit(solution)/shard_map/ppermute | solution.py:390
  19.1 0.8 %collective-permute-done.6.other_ref = f32[8,128]{1,0:T(8,128)S(1)} collective-permute-done((f32[8,128]{1,0:T(8,128)S(1)}, f32[8,128]{1,0:T(8,128)S(1)}, u32[]{:S(2)}, u32[]{:S(2)}) %collective-permute-start.6) | collective-permute-done | bytes 4128 | tf_op jit(solution)/shard_map/ppermute | solution.py:390
  19.9 0.0 copy-done.1
  19.9 0.8 %solve.1 = f32[8,128]{1,0:T(8,128)} custom-call(f32[8,128]{1,0:T(8,128)S(1)} %couple.1.mine_ref, f32[8,128]{1,0:T(8,128)S(1)} %collective-permute-done.6.other_ref, f32[8,128]{1,0:T(8,128)S(1)} %bitcast.9, f32[8,128,128]{2,1,0:T(8,128)S(1)} %copy-done.1), custom_call_target="tpu_custom_call" | custom-call | tf_op jit(solution)/shard_map/solve/pallas_call | solution.py:26
  (11 shorter events, 0.0 us)
Async XLA Ops:
  0.0 3.0 %copy-start.4 = (s32[128]{0:T(128)S(1)}, s32[128]{0:T(128)}, u32[]{:S(2)}) copy-start(s32[128]{0:T(128)} %param.11) | copy-start | bytes 1540
  0.0 3.0 %copy-start.5 = (s32[128]{0:T(128)S(1)}, s32[128]{0:T(128)}, u32[]{:S(2)}) copy-start(s32[128]{0:T(128)} %param.12) | copy-start | bytes 1540
  0.0 3.1 %copy-start.6 = (s32[128]{0:T(128)S(1)}, s32[128]{0:T(128)}, u32[]{:S(2)}) copy-start(s32[128]{0:T(128)} %param.13) | copy-start | bytes 1540
  0.0 5.5 %copy-start.2 = (bf16[32,1024]{1,0:T(8,128)(2,1)S(1)}, bf16[32,1024]{1,0:T(8,128)(2,1)}, u32[]{:S(2)}) copy-start(bf16[32,1024]{1,0:T(8,128)(2,1)} %param.8) | copy-start | bytes 196612
  0.0 5.5 %collective-permute-start.2 = (bf16[1,32,1024]{2,1,0:T(8,128)(2,1)}, bf16[1,32,1024]{2,1,0:T(8,128)(2,1)S(1)}, u32[]{:S(2)}, u32[]{:S(2)}) collective-permute-start(bf16[1,32,1024]{2,1,0:T(8,128)(2,1)} %bitcast.7), channel_id=1, source_target_pairs={{0,2},{1,5},{2,0},{3,7},{4,6},{5,1},{6,4},{7,3},{8,10},{9,13},{10,... | collective-permute-start | bytes 196616 | tf_op jit(solution)/shard_map/ppermute | solution.py:259
  3.0 2.5 %copy-start = (bf16[128,128,128]{2,1,0:T(8,128)(2,1)S(1)}, bf16[128,128,128]{2,1,0:T(8,128)(2,1)}, u32[]{:S(2)}) copy-start(bf16[128,128,128]{2,1,0:T(8,128)(2,1)} %refs_2_.5) | copy-start | bytes 12582916
  3.2 4.0 %collective-permute-start = (s32[1,256]{1,0:T(1,128)S(1)}, s32[1,256]{1,0:T(1,128)S(1)}, u32[]{:S(2)}, u32[]{:S(2)}) collective-permute-start(s32[1,256]{1,0:T(1,128)S(1)} %request.1.refs_0_), channel_id=1, source_target_pairs={{0,17},{1,16},{2,19},{3,18},{4,21},{5,20},{6,23},{7,22},{8,25},{9,... | collective-permute-start | bytes 3080 | tf_op jit(solution)/shard_map/ppermute | solution.py:259
  5.5 3.4 %copy-start.7 = (s32[128]{0:T(128)S(1)}, s32[128]{0:T(128)}, u32[]{:S(2)}) copy-start(s32[128]{0:T(128)} %param.10) | copy-start | bytes 1540
  5.5 4.7 %collective-permute-start.3 = (bf16[2,32,1024]{2,1,0:T(8,128)(2,1)S(1)}, bf16[2,32,1024]{2,1,0:T(8,128)(2,1)S(1)}, u32[]{:S(2)}, u32[]{:S(2)}) collective-permute-start(bf16[2,32,1024]{2,1,0:T(8,128)(2,1)S(1)} %gather.1.refs_2_.refs_3_), channel_id=1, source_target_pairs={{0,5},{1,2},{2,7},{3,0},{4,1},{5,6},{6,3},{7,4},{8,13},{9,10},{10,... | collective-permute-start | bytes 393224 | tf_op jit(solution)/shard_map/ppermute | solution.py:259
  7.2 3.0 %collective-permute-start.1 = (s32[2,256]{1,0:T(2,128)S(1)}, s32[2,256]{1,0:T(2,128)S(1)}, u32[]{:S(2)}, u32[]{:S(2)}) collective-permute-start(s32[2,256]{1,0:T(2,128)S(1)} %join.1.refs_2_), channel_id=1, source_target_pairs={{0,9},{1,8},{2,11},{3,10},{4,13},{5,12},{6,15},{7,14},{8,1},{9,0},... | collective-permute-start | bytes 6152 | tf_op jit(solution)/shard_map/ppermute | solution.py:259
  10.5 4.3 %collective-permute-start.4 = (bf16[96,128]{1,0:T(8,128)(2,1)S(1)}, bf16[96,128]{1,0:T(8,128)(2,1)S(1)}, u32[]{:S(2)}, u32[]{:S(2)}) collective-permute-start(bf16[96,128]{1,0:T(8,128)(2,1)S(1)} %select_send.1.refs_0_), channel_id=1, source_target_pairs={{0,17},{1,16},{2,19},{3,18},{4,21},{5,20},{6,23},{7,22},{8,25},{9,... | collective-permute-start | bytes 73736 | tf_op jit(solution)/shard_map/ppermute | solution.py:259
  14.8 3.3 %collective-permute-start.5 = (bf16[96,128]{1,0:T(8,128)(2,1)S(1)}, bf16[96,128]{1,0:T(8,128)(2,1)S(1)}, u32[]{:S(2)}, u32[]{:S(2)}) collective-permute-start(bf16[96,128]{1,0:T(8,128)(2,1)S(1)} %pad_maximum_fusion), channel_id=1, source_target_pairs={{0,9},{1,8},{2,11},{3,10},{4,13},{5,12},{6,15},{7,14},{8,1},{9,0},... | collective-permute-start | bytes 73736 | tf_op jit(solution)/shard_map/ppermute | solution.py:259
  17.7 2.2 %copy-start.1 = (f32[8,128,128]{2,1,0:T(8,128)S(1)}, f32[8,128,128]{2,1,0:T(8,128)}, u32[]{:S(2)}) copy-start(f32[8,128,128]{2,1,0:T(8,128)} %inverse_ref.1) | copy-start | bytes 1572868
  17.7 2.2 %copy-start.3 = (f32[1024]{0:T(1024)S(1)}, f32[1024]{0:T(1024)}, u32[]{:S(2)}) copy-start(f32[1024]{0:T(1024)} %param.14) | copy-start | bytes 12292
  18.6 1.3 %collective-permute-start.6 = (f32[8,128]{1,0:T(8,128)S(1)}, f32[8,128]{1,0:T(8,128)S(1)}, u32[]{:S(2)}, u32[]{:S(2)}) collective-permute-start(f32[8,128]{1,0:T(8,128)S(1)} %couple.1.mine_ref), channel_id=1, source_target_pairs={{0,1},{1,0},{2,3},{3,2},{4,5},{5,4},{6,7},{7,6},{8,9},{9,8},{10,11... | collective-permute-start | bytes 12296 | tf_op jit(solution)/shard_map/ppermute | solution.py:390

commit v8 on v7

--- a/solution.py
+++ b/solution.py
@@ -298,7 +298,7 @@
     n_hops = len(exchange_bits)
 
     n_slots = plan.slots << n_hops
-    cuts = [0, n_slots // 64 * 16, n_slots // 192 * 112, n_slots]
+    cuts = [0, n_slots // 64 * 16, max(n_slots // 2, n_slots * 7 // 12 // 16 * 16), n_slots]
     wide = -(-n_slots // 128) * 128
     scratch = [pltpu.SMEM((1, wide), jnp.int32), pltpu.SemaphoreType.DMA]
 

time: 20.9 us -> 20.9 us (level)
  no operation moved by 1% of the time
where the time goes in v8:
time: 20.9 us; the launch traced here: 20.8 us
  starting transfers between devices  13.1 us (63%)
  Pallas kernels  5.65 us (27%)
  waiting for transfers between devices  1.84 us (9%)
    ppermute x6, starting transfers between devices, hop(): return lax.ppermute(value, ('blk', 'lag'), pairs)  12.6 us
    pallas_call x11, Pallas kernels, call(): pl.pallas_call(kernel, out_shape=outs, in_specs=[VMEM] * len(operands), o...  5.65 us
    ppermute x6, waiting for transfers between devices, hop(): return lax.ppermute(value, ('blk', 'lag'), pairs)  1.02 us
    ppermute x1, waiting for transfers between devices, body(): other = lax.ppermute(mine, 'lag', [(0, 1), (1, 0)])  0.82 us
    ppermute x1, starting transfers between devices, body(): other = lax.ppermute(mine, 'lag', [(0, 1), (1, 0)])  0.49 us
  transfers between devices with their start and end apart: 7, of which 5 were waited for; matrix products, arithmetic and copies ran while one was open for 0% of the time, Pallas kernels for 19%

profile of v8, /device:TPU:0, one launch (start us, length us, event | category | flops | bytes accessed | tf_op | source)
XLA Modules:
  0.0 20.8 jit_solution(4030633808015376918)
XLA Ops:
  0.0 3.0 %collective-permute-start.2 = (bf16[1,32,1024]{2,1,0:T(8,128)(2,1)}, bf16[1,32,1024]{2,1,0:T(8,128)(2,1)S(1)}, u32[]{:S(2)}, u32[]{:S(2)}) collective-permute-start(bf16[1,32,1024]{2,1,0:T(8,128)(2,1)} %bitcast.7), channel_id=1, source_target_pairs={{0,2},{1,5},{2,0},{3,7},{4,6},{5,1},{6,4},{7,3},{8,10},{9,13},{10,... | collective-permute-start | bytes 196616 | tf_op jit(solution)/shard_map/ppermute | solution.py:259
  3.0 0.0 copy-done.4
  3.0 0.0 copy-done.5
  3.1 0.0 copy-done.6
  3.1 0.1 request.1.refs_0_
  3.2 1.8 %collective-permute-start = (s32[1,256]{1,0:T(1,128)S(1)}, s32[1,256]{1,0:T(1,128)S(1)}, u32[]{:S(2)}, u32[]{:S(2)}) collective-permute-start(s32[1,256]{1,0:T(1,128)S(1)} %request.1.refs_0_), channel_id=1, source_target_pairs={{0,17},{1,16},{2,19},{3,18},{4,21},{5,20},{6,23},{7,22},{8,25},{9,... | collective-permute-start | bytes 3080 | tf_op jit(solution)/shard_map/ppermute | solution.py:259
  5.0 0.5 %collective-permute-done.2.refs_1_ = bf16[1,32,1024]{2,1,0:T(8,128)(2,1)S(1)} collective-permute-done((bf16[1,32,1024]{2,1,0:T(8,128)(2,1)}, bf16[1,32,1024]{2,1,0:T(8,128)(2,1)S(1)}, u32[]{:S(2)}, u32[]{:S(2)}) %collective-permute-start.2) | collective-permute-done | bytes 65568 | tf_op jit(solution)/shard_map/ppermute | solution.py:259
  5.5 0.0 copy-done.2
  5.5 0.0 copy-done
  5.5 0.0 copy-start.7
  5.5 1.7 %collective-permute-start.3 = (bf16[2,32,1024]{2,1,0:T(8,128)(2,1)S(1)}, bf16[2,32,1024]{2,1,0:T(8,128)(2,1)S(1)}, u32[]{:S(2)}, u32[]{:S(2)}) collective-permute-start(bf16[2,32,1024]{2,1,0:T(8,128)(2,1)S(1)} %gather.1.refs_2_.refs_3_), channel_id=1, source_target_pairs={{0,5},{1,2},{2,7},{3,0},{4,1},{5,6},{6,3},{7,4},{8,13},{9,10},{10,... | collective-permute-start | bytes 393224 | tf_op jit(solution)/shard_map/ppermute | solution.py:259
  7.2 0.0 collective-permute-done.refs_1_
  7.2 1.7 %collective-permute-start.1 = (s32[2,256]{1,0:T(2,128)S(1)}, s32[2,256]{1,0:T(2,128)S(1)}, u32[]{:S(2)}, u32[]{:S(2)}) collective-permute-start(s32[2,256]{1,0:T(2,128)S(1)} %join.1.refs_2_), channel_id=1, source_target_pairs={{0,9},{1,8},{2,11},{3,10},{4,13},{5,12},{6,15},{7,14},{8,1},{9,0},... | collective-permute-start | bytes 6152 | tf_op jit(solution)/shard_map/ppermute | solution.py:259
  8.9 0.0 copy-done.7
  8.9 1.2 %order.1 = (s32[2,256]{1,0:T(2,128)S(1)}, s32[1,256]{1,0:T(1,128)S(1)}, s32[192,128]{1,0:T(8,128)S(1)}, bf16[6144,128]{1,0:T(8,128)(2,1)S(1)}) custom-call(s32[1,256]{1,0:T(1,128)S(1)} %request.1.refs_0_, s32[1,128]{1,0:T(1,128)S(1)} %bitcast.13, s32[2,256]{1,0:T(2,128)S(1)} %join.1.refs_2_, bf16[128,128,128]{2,1,0:T(8,128)(2,1)S(1)} %copy-done), custom_call_target="tpu_custom_call" | custom-call | tf_op jit(solution)/shard_map/order/pallas_call | solution.py:26
  10.1 0.1 collective-permute-done.1.refs_1_.refs_2_
  10.2 0.0 collective-permute-done.3.refs_3_.refs_4_
  10.2 0.3 %select_send.1.refs_0_ = bf16[96,128]{1,0:T(8,128)(2,1)S(1)} custom-call(s32[2,256]{1,0:T(2,128)S(1)} %get-tuple-element.18.refs_0_.refs_1_, s32[2,256]{1,0:T(2,128)S(1)} %collective-permute-done.1.refs_1_.refs_2_, bf16[2,32,1024]{2,1,0:T(8,128)(2,1)S(1)} %gather.1.refs_2_.refs_3_, bf16[2,32,1024]{2,1,0:T(8,128)(2,1)S(1)} %collective-permute-done.3.refs_3_.refs_4_), custom_call_target="tpu_custom_call" | custom-call | flops 68719476736 | bytes 268435456 | tf_op jit(solution)/shard_map/select_send/pallas_call | solution.py:26
  10.5 2.8 %collective-permute-start.4 = (bf16[96,128]{1,0:T(8,128)(2,1)S(1)}, bf16[96,128]{1,0:T(8,128)(2,1)S(1)}, u32[]{:S(2)}, u32[]{:S(2)}) collective-permute-start(bf16[96,128]{1,0:T(8,128)(2,1)S(1)} %select_send.1.refs_0_), channel_id=1, source_target_pairs={{0,17},{1,16},{2,19},{3,18},{4,21},{5,20},{6,23},{7,22},{8,25},{9,... | collective-permute-start | bytes 73736 | tf_op jit(solution)/shard_map/ppermute | solution.py:259
  13.3 0.3 %select_keep.1 = (bf16[48,128]{1,0:T(8,128)(2,1)S(1)}, bf16[48,128]{1,0:T(8,128)(2,1)S(1)}) custom-call(bf16[96,128]{1,0:T(8,128)(2,1)S(1)} %select_send.1.refs_0_, s32[2,256]{1,0:T(2,128)S(1)} %get-tuple-element.18.refs_0_.refs_1_, s32[2,256]{1,0:T(2,128)S(1)} %collective-permute-done.1.refs_1_.refs_2_, bf16[2,32,1024]{2,1,0:T(8,128)(2,1)S(1)} %gather.1.refs_2_.refs_3_, ...), custom_call_target="tpu_custom_call" | custom-call | flops 68719476736 | bytes 268435456 | tf_op jit(solution)/shard_map/select_keep/pallas_call | solution.py:26
  13.5 1.2 %turn.1 = (bf16[48,128]{1,0:T(8,128)(2,1)S(1)}, bf16[8192,128]{1,0:T(8,128)(2,1)S(1)}) custom-call(bf16[48,128]{1,0:T(8,128)(2,1)S(1)} %get-tuple-element.19.refs_0_, s32[1,256]{1,0:T(1,128)S(1)} %get-tuple-element.16.refs_1_, bf16[128,128,128]{2,1,0:T(8,128)(2,1)S(1)} %copy-done), custom_call_target="tpu_custom_call" | custom-call | flops 17179869184 | bytes 67108864 | tf_op jit(solution)/shard_map/turn/pallas_call | solution.py:26
  14.7 0.1 collective-permute-done.4
  14.8 1.6 %collective-permute-start.5 = (bf16[96,128]{1,0:T(8,128)(2,1)S(1)}, bf16[96,128]{1,0:T(8,128)(2,1)S(1)}, u32[]{:S(2)}, u32[]{:S(2)}) collective-permute-start(bf16[96,128]{1,0:T(8,128)(2,1)S(1)} %pad_maximum_fusion), channel_id=1, source_target_pairs={{0,9},{1,8},{2,11},{3,10},{4,13},{5,12},{6,15},{7,14},{8,1},{9,0},... | collective-permute-start | bytes 73736 | tf_op jit(solution)/shard_map/ppermute | solution.py:259
  16.4 1.3 %early.1 = (f32[8,128]{1,0:T(8,128)S(1)}, bf16[10240,128]{1,0:T(8,128)(2,1)S(1)}) custom-call(s32[192,128]{1,0:T(8,128)S(1)} %get-tuple-element.15.refs_0_.refs_1_, s32[1,256]{1,0:T(1,128)S(1)} %get-tuple-element.16.refs_1_, bf16[128,128,128]{2,1,0:T(8,128)(2,1)S(1)} %copy-done, bf16[6144,128]{1,0:T(8,128)(2,1)S(1)} %get-tuple-element.17.refs_3_, ...), custom_call_target="tpu_custom_call" | custom-call | flops 17179869184 | bytes 67108864 | tf_op jit(solution)/shard_map/early/pallas_call | solution.py:26
  17.7 0.0 copy-start.1
  17.7 0.0 copy-start.3
  17.7 0.3 %collective-permute-done.5.refs_4_ = bf16[96,128]{1,0:T(8,128)(2,1)S(1)} collective-permute-done((bf16[96,128]{1,0:T(8,128)(2,1)S(1)}, bf16[96,128]{1,0:T(8,128)(2,1)S(1)}, u32[]{:S(2)}, u32[]{:S(2)}) %collective-permute-start.5) | collective-permute-done | bytes 24608 | tf_op jit(solution)/shard_map/ppermute | solution.py:259
  18.1 0.5 %couple.1.mine_ref = f32[8,128]{1,0:T(8,128)S(1)} custom-call(f32[8,128]{1,0:T(8,128)S(1)} %get-tuple-element.22.refs_0_, s32[192,128]{1,0:T(8,128)S(1)} %get-tuple-element.15.refs_0_.refs_1_, bf16[8192,128]{1,0:T(8,128)(2,1)S(1)} %get-tuple-element.20.refs_4_.refs_2_, bf16[10240,128]{1,0:T(8,128)(2,1)S(1)} %get-tuple-element.23.refs_3_, ...), custom_call_target="tpu_custom_call" | custom-call | tf_op jit(solution)/shard_map/couple/pallas_call | solution.py:26
  18.6 0.5 %collective-permute-start.6 = (f32[8,128]{1,0:T(8,128)S(1)}, f32[8,128]{1,0:T(8,128)S(1)}, u32[]{:S(2)}, u32[]{:S(2)}) collective-permute-start(f32[8,128]{1,0:T(8,128)S(1)} %couple.1.mine_ref), channel_id=1, source_target_pairs={{0,1},{1,0},{2,3},{3,2},{4,5},{5,4},{6,7},{7,6},{8,9},{9,8},{10,11... | collective-permute-start | bytes 12296 | tf_op jit(solution)/shard_map/ppermute | solution.py:390
  19.1 0.8 %collective-permute-done.6.other_ref = f32[8,128]{1,0:T(8,128)S(1)} collective-permute-done((f32[8,128]{1,0:T(8,128)S(1)}, f32[8,128]{1,0:T(8,128)S(1)}, u32[]{:S(2)}, u32[]{:S(2)}) %collective-permute-start.6) | collective-permute-done | bytes 4128 | tf_op jit(solution)/shard_map/ppermute | solution.py:390
  19.9 0.0 copy-done.1
  19.9 0.8 %solve.1 = f32[8,128]{1,0:T(8,128)} custom-call(f32[8,128]{1,0:T(8,128)S(1)} %couple.1.mine_ref, f32[8,128]{1,0:T(8,128)S(1)} %collective-permute-done.6.other_ref, f32[8,128]{1,0:T(8,128)S(1)} %bitcast.9, f32[8,128,128]{2,1,0:T(8,128)S(1)} %copy-done.1), custom_call_target="tpu_custom_call" | custom-call | tf_op jit(solution)/shard_map/solve/pallas_call | solution.py:26
  (11 shorter events, 0.0 us)
Async XLA Ops:
  0.0 3.0 %copy-start.4 = (s32[128]{0:T(128)S(1)}, s32[128]{0:T(128)}, u32[]{:S(2)}) copy-start(s32[128]{0:T(128)} %param.11) | copy-start | bytes 1540
  0.0 3.0 %copy-start.5 = (s32[128]{0:T(128)S(1)}, s32[128]{0:T(128)}, u32[]{:S(2)}) copy-start(s32[128]{0:T(128)} %param.12) | copy-start | bytes 1540
  0.0 3.1 %copy-start.6 = (s32[128]{0:T(128)S(1)}, s32[128]{0:T(128)}, u32[]{:S(2)}) copy-start(s32[128]{0:T(128)} %param.13) | copy-start | bytes 1540
  0.0 5.5 %copy-start.2 = (bf16[32,1024]{1,0:T(8,128)(2,1)S(1)}, bf16[32,1024]{1,0:T(8,128)(2,1)}, u32[]{:S(2)}) copy-start(bf16[32,1024]{1,0:T(8,128)(2,1)} %param.8) | copy-start | bytes 196612
  0.0 5.5 %collective-permute-start.2 = (bf16[1,32,1024]{2,1,0:T(8,128)(2,1)}, bf16[1,32,1024]{2,1,0:T(8,128)(2,1)S(1)}, u32[]{:S(2)}, u32[]{:S(2)}) collective-permute-start(bf16[1,32,1024]{2,1,0:T(8,128)(2,1)} %bitcast.7), channel_id=1, source_target_pairs={{0,2},{1,5},{2,0},{3,7},{4,6},{5,1},{6,4},{7,3},{8,10},{9,13},{10,... | collective-permute-start | bytes 196616 | tf_op jit(solution)/shard_map/ppermute | solution.py:259
  3.0 2.5 %copy-start = (bf16[128,128,128]{2,1,0:T(8,128)(2,1)S(1)}, bf16[128,128,128]{2,1,0:T(8,128)(2,1)}, u32[]{:S(2)}) copy-start(bf16[128,128,128]{2,1,0:T(8,128)(2,1)} %refs_2_.5) | copy-start | bytes 12582916
  3.2 4.0 %collective-permute-start = (s32[1,256]{1,0:T(1,128)S(1)}, s32[1,256]{1,0:T(1,128)S(1)}, u32[]{:S(2)}, u32[]{:S(2)}) collective-permute-start(s32[1,256]{1,0:T(1,128)S(1)} %request.1.refs_0_), channel_id=1, source_target_pairs={{0,17},{1,16},{2,19},{3,18},{4,21},{5,20},{6,23},{7,22},{8,25},{9,... | collective-permute-start | bytes 3080 | tf_op jit(solution)/shard_map/ppermute | solution.py:259
  5.5 3.4 %copy-start.7 = (s32[128]{0:T(128)S(1)}, s32[128]{0:T(128)}, u32[]{:S(2)}) copy-start(s32[128]{0:T(128)} %param.10) | copy-start | bytes 1540
  5.5 4.7 %collective-permute-start.3 = (bf16[2,32,1024]{2,1,0:T(8,128)(2,1)S(1)}, bf16[2,32,1024]{2,1,0:T(8,128)(2,1)S(1)}, u32[]{:S(2)}, u32[]{:S(2)}) collective-permute-start(bf16[2,32,1024]{2,1,0:T(8,128)(2,1)S(1)} %gather.1.refs_2_.refs_3_), channel_id=1, source_target_pairs={{0,5},{1,2},{2,7},{3,0},{4,1},{5,6},{6,3},{7,4},{8,13},{9,10},{10,... | collective-permute-start | bytes 393224 | tf_op jit(solution)/shard_map/ppermute | solution.py:259
  7.2 3.0 %collective-permute-start.1 = (s32[2,256]{1,0:T(2,128)S(1)}, s32[2,256]{1,0:T(2,128)S(1)}, u32[]{:S(2)}, u32[]{:S(2)}) collective-permute-start(s32[2,256]{1,0:T(2,128)S(1)} %join.1.refs_2_), channel_id=1, source_target_pairs={{0,9},{1,8},{2,11},{3,10},{4,13},{5,12},{6,15},{7,14},{8,1},{9,0},... | collective-permute-start | bytes 6152 | tf_op jit(solution)/shard_map/ppermute | solution.py:259
  10.5 4.3 %collective-permute-start.4 = (bf16[96,128]{1,0:T(8,128)(2,1)S(1)}, bf16[96,128]{1,0:T(8,128)(2,1)S(1)}, u32[]{:S(2)}, u32[]{:S(2)}) collective-permute-start(bf16[96,128]{1,0:T(8,128)(2,1)S(1)} %select_send.1.refs_0_), channel_id=1, source_target_pairs={{0,17},{1,16},{2,19},{3,18},{4,21},{5,20},{6,23},{7,22},{8,25},{9,... | collective-permute-start | bytes 73736 | tf_op jit(solution)/shard_map/ppermute | solution.py:259
  14.8 3.3 %collective-permute-start.5 = (bf16[96,128]{1,0:T(8,128)(2,1)S(1)}, bf16[96,128]{1,0:T(8,128)(2,1)S(1)}, u32[]{:S(2)}, u32[]{:S(2)}) collective-permute-start(bf16[96,128]{1,0:T(8,128)(2,1)S(1)} %pad_maximum_fusion), channel_id=1, source_target_pairs={{0,9},{1,8},{2,11},{3,10},{4,13},{5,12},{6,15},{7,14},{8,1},{9,0},... | collective-permute-start | bytes 73736 | tf_op jit(solution)/shard_map/ppermute | solution.py:259
  17.7 2.2 %copy-start.1 = (f32[8,128,128]{2,1,0:T(8,128)S(1)}, f32[8,128,128]{2,1,0:T(8,128)}, u32[]{:S(2)}) copy-start(f32[8,128,128]{2,1,0:T(8,128)} %inverse_ref.1) | copy-start | bytes 1572868
  17.7 2.2 %copy-start.3 = (f32[1024]{0:T(1024)S(1)}, f32[1024]{0:T(1024)}, u32[]{:S(2)}) copy-start(f32[1024]{0:T(1024)} %param.14) | copy-start | bytes 12292
  18.6 1.3 %collective-permute-start.6 = (f32[8,128]{1,0:T(8,128)S(1)}, f32[8,128]{1,0:T(8,128)S(1)}, u32[]{:S(2)}, u32[]{:S(2)}) collective-permute-start(f32[8,128]{1,0:T(8,128)S(1)} %couple.1.mine_ref), channel_id=1, source_target_pairs={{0,1},{1,0},{2,3},{3,2},{4,5},{5,4},{6,7},{7,6},{8,9},{9,8},{10,11... | collective-permute-start | bytes 12296 | tf_op jit(solution)/shard_map/ppermute | solution.py:390

commit v9 on v8

--- a/solution.py
+++ b/solution.py
@@ -197,11 +197,20 @@
     return total
 
 
-def early_kernel(cuts, n_rows, column_ref, tile_ref, tiles_ref, turned0_ref, turned1_ref, *refs):
-    row_refs, (sum_ref, turned_ref, index, sem) = refs[:n_rows], refs[n_rows:]
+def early_kernel(
+    cuts, n_rows, column_ref, tile_ref, tiles_ref, inverse_ref, turned0_ref, turned1_ref, *refs
+):
+    row_refs, (sum_ref, turned_ref, high_ref, low_ref, index, sem) = refs[:n_rows], refs[n_rows:]
     turned = [(turned0_ref, cuts[0], cuts[1] - cuts[0]), (turned1_ref, cuts[1], cuts[2] - cuts[1])]
     sum_ref[...] = products(0, column_ref, row_refs, turned, sum_ref.shape[0])
     turn(cuts[2], cuts[3] - cuts[2], tile_ref, tiles_ref, turned_ref, index, sem)
+    blocks, size = inverse_ref.shape[:2]
+    for b in range(blocks):
+        whole = jnp.transpose(inverse_ref[b])
+        high = whole.astype(jnp.bfloat16)
+        high_ref[b * size : (b + 1) * size, :] = high
+        low = whole - high.astype(jnp.float32)
+        low_ref[b * size : (b + 1) * size, :] = low.astype(jnp.bfloat16)
 
 
 def couple_kernel(cuts, early_ref, column_ref, turned1_ref, turned2_ref, rows_ref, out_ref):
@@ -210,15 +219,20 @@
     out_ref[...] = early_ref[...] + products(first, column_ref, [rows_ref], turned, out_ref.shape[0])
 
 
-def solve_kernel(mine_ref, other_ref, incident_ref, inverse_ref, out_ref):
+def solve_kernel(mine_ref, other_ref, incident_ref, high_ref, low_ref, out_ref):
     blocks, size = incident_ref.shape
     excite = incident_ref[...] - (mine_ref[...] + other_ref[...])
-    lane = lax.broadcasted_iota(jnp.int32, (size, blocks), 1)
-    solved = jnp.zeros((size, blocks), jnp.float32)
-    for b in range(blocks):
-        product = inverse_ref[b] * jnp.broadcast_to(excite[b : b + 1, :], (size, size))
-        solved = jnp.where(lane == b, jnp.sum(product, axis=1, keepdims=True), solved)
-    out_ref[...] = jnp.transpose(solved)
+    high = excite.astype(jnp.bfloat16).astype(jnp.float32)
+    block_id = lax.broadcasted_iota(jnp.int32, (blocks, size), 0)
+
+    def spread(rows):
+        parts = [jnp.where(block_id == b, rows, 0.0) for b in range(blocks)]
+        return jnp.concatenate(parts, axis=1)
+
+    left = jnp.concatenate([spread(high), spread(excite - high)], axis=0).astype(jnp.bfloat16)
+    first = jnp.dot(left, high_ref[...], preferred_element_type=jnp.float32)
+    second = jnp.dot(left, low_ref[...], preferred_element_type=jnp.float32)
+    out_ref[...] = first[:blocks] + (first[blocks:] + second[:blocks])
 
 
 def body(
@@ -357,13 +371,15 @@
             passed = hop(send, bit)
             landed.append(passed[len(onward) * rows :])
         if i == n_hops - 1:
-            early, turned2 = call(
+            inverse = pltpu.VMEM((slab_blocks * size, size), jnp.bfloat16)
+            early, turned2, *inverses = call(
                 lambda *refs: early_kernel(cuts, n_hops, *refs),
                 "early",
-                (pltpu.VMEM((slab_blocks, size), jnp.float32), turned_tiles(2)),
+                (pltpu.VMEM((slab_blocks, size), jnp.float32), turned_tiles(2), inverse, inverse),
                 columns,
                 slot_tiles,
                 tile_blocks,
+                self_inv,
                 turned0,
                 turned1,
                 keep,
@@ -397,7 +413,7 @@
         mine,
         other,
         incident.reshape(slab_blocks, size),
-        self_inv,
+        *inverses,
     )
     return solved.reshape(slab_blocks * size)
 

time: 20.9 us -> 20.8 us (level)
  transfers between devices with their start and end apart: 7 -> 7, of which waited for: 5 -> 5; matrix products, arithmetic and copies ran while one was open for 0% -> 0% of each run, Pallas kernels for 19% -> 20%
where the time goes in v9:
time: 20.8 us; the launch traced here: 20.7 us
  starting transfers between devices  13.1 us (63%)
  Pallas kernels  5.74 us (28%)
  waiting for transfers between devices  1.69 us (8%)
    ppermute x6, starting transfers between devices, hop(): return lax.ppermute(value, ('blk', 'lag'), pairs)  12.6 us
    pallas_call x11, Pallas kernels, call(): pl.pallas_call(kernel, out_shape=outs, in_specs=[VMEM] * len(operands), o...  5.74 us
    ppermute x6, waiting for transfers between devices, hop(): return lax.ppermute(value, ('blk', 'lag'), pairs)  0.87 us
    ppermute x1, waiting for transfers between devices, body(): other = lax.ppermute(mine, 'lag', [(0, 1), (1, 0)])  0.82 us
    ppermute x1, starting transfers between devices, body(): other = lax.ppermute(mine, 'lag', [(0, 1), (1, 0)])  0.49 us
  transfers between devices with their start and end apart: 7, of which 5 were waited for; matrix products, arithmetic and copies ran while one was open for 0% of the time, Pallas kernels for 20%

profile of v9, /device:TPU:0, one launch (start us, length us, event | category | flops | bytes accessed | tf_op | source)
XLA Modules:
  0.0 20.7 jit_solution(8355920623031408448)
XLA Ops:
  0.0 3.0 %collective-permute-start.2 = (bf16[1,32,1024]{2,1,0:T(8,128)(2,1)}, bf16[1,32,1024]{2,1,0:T(8,128)(2,1)S(1)}, u32[]{:S(2)}, u32[]{:S(2)}) collective-permute-start(bf16[1,32,1024]{2,1,0:T(8,128)(2,1)} %bitcast.7), channel_id=1, source_target_pairs={{0,2},{1,5},{2,0},{3,7},{4,6},{5,1},{6,4},{7,3},{8,10},{9,13},{10,... | collective-permute-start | bytes 196616 | tf_op jit(solution)/shard_map/ppermute | solution.py:273
  3.0 0.0 copy-done.3
  3.0 0.0 copy-done.4
  3.1 0.0 copy-done.5
  3.1 0.1 request.1.refs_0_
  3.2 1.8 %collective-permute-start = (s32[1,256]{1,0:T(1,128)S(1)}, s32[1,256]{1,0:T(1,128)S(1)}, u32[]{:S(2)}, u32[]{:S(2)}) collective-permute-start(s32[1,256]{1,0:T(1,128)S(1)} %request.1.refs_0_), channel_id=1, source_target_pairs={{0,17},{1,16},{2,19},{3,18},{4,21},{5,20},{6,23},{7,22},{8,25},{9,... | collective-permute-start | bytes 3080 | tf_op jit(solution)/shard_map/ppermute | solution.py:273
  5.0 0.5 %collective-permute-done.2.refs_1_ = bf16[1,32,1024]{2,1,0:T(8,128)(2,1)S(1)} collective-permute-done((bf16[1,32,1024]{2,1,0:T(8,128)(2,1)}, bf16[1,32,1024]{2,1,0:T(8,128)(2,1)S(1)}, u32[]{:S(2)}, u32[]{:S(2)}) %collective-permute-start.2) | collective-permute-done | bytes 65568 | tf_op jit(solution)/shard_map/ppermute | solution.py:273
  5.5 0.0 copy-done.1
  5.5 0.0 copy-done
  5.5 0.0 copy-start.6
  5.5 1.7 %collective-permute-start.3 = (bf16[2,32,1024]{2,1,0:T(8,128)(2,1)S(1)}, bf16[2,32,1024]{2,1,0:T(8,128)(2,1)S(1)}, u32[]{:S(2)}, u32[]{:S(2)}) collective-permute-start(bf16[2,32,1024]{2,1,0:T(8,128)(2,1)S(1)} %gather.1.refs_2_.refs_3_), channel_id=1, source_target_pairs={{0,5},{1,2},{2,7},{3,0},{4,1},{5,6},{6,3},{7,4},{8,13},{9,10},{10,... | collective-permute-start | bytes 393224 | tf_op jit(solution)/shard_map/ppermute | solution.py:273
  7.2 0.0 collective-permute-done.refs_1_
  7.2 1.7 %collective-permute-start.1 = (s32[2,256]{1,0:T(2,128)S(1)}, s32[2,256]{1,0:T(2,128)S(1)}, u32[]{:S(2)}, u32[]{:S(2)}) collective-permute-start(s32[2,256]{1,0:T(2,128)S(1)} %join.1.refs_2_), channel_id=1, source_target_pairs={{0,9},{1,8},{2,11},{3,10},{4,13},{5,12},{6,15},{7,14},{8,1},{9,0},... | collective-permute-start | bytes 6152 | tf_op jit(solution)/shard_map/ppermute | solution.py:273
  8.9 0.0 copy-done.6
  8.9 1.2 %order.1 = (s32[2,256]{1,0:T(2,128)S(1)}, s32[1,256]{1,0:T(1,128)S(1)}, s32[192,128]{1,0:T(8,128)S(1)}, bf16[6144,128]{1,0:T(8,128)(2,1)S(1)}) custom-call(s32[1,256]{1,0:T(1,128)S(1)} %request.1.refs_0_, s32[1,128]{1,0:T(1,128)S(1)} %bitcast.13, s32[2,256]{1,0:T(2,128)S(1)} %join.1.refs_2_, bf16[128,128,128]{2,1,0:T(8,128)(2,1)S(1)} %copy-done), custom_call_target="tpu_custom_call" | custom-call | tf_op jit(solution)/shard_map/order/pallas_call | solution.py:26
  10.1 0.1 collective-permute-done.1.refs_1_.refs_2_
  10.2 0.0 collective-permute-done.3.refs_3_.refs_4_
  10.2 0.3 %select_send.1.refs_0_ = bf16[96,128]{1,0:T(8,128)(2,1)S(1)} custom-call(s32[2,256]{1,0:T(2,128)S(1)} %get-tuple-element.20.refs_0_.refs_1_, s32[2,256]{1,0:T(2,128)S(1)} %collective-permute-done.1.refs_1_.refs_2_, bf16[2,32,1024]{2,1,0:T(8,128)(2,1)S(1)} %gather.1.refs_2_.refs_3_, bf16[2,32,1024]{2,1,0:T(8,128)(2,1)S(1)} %collective-permute-done.3.refs_3_.refs_4_), custom_call_target="tpu_custom_call" | custom-call | flops 68719476736 | bytes 268435456 | tf_op jit(solution)/shard_map/select_send/pallas_call | solution.py:26
  10.5 2.8 %collective-permute-start.4 = (bf16[96,128]{1,0:T(8,128)(2,1)S(1)}, bf16[96,128]{1,0:T(8,128)(2,1)S(1)}, u32[]{:S(2)}, u32[]{:S(2)}) collective-permute-start(bf16[96,128]{1,0:T(8,128)(2,1)S(1)} %select_send.1.refs_0_), channel_id=1, source_target_pairs={{0,17},{1,16},{2,19},{3,18},{4,21},{5,20},{6,23},{7,22},{8,25},{9,... | collective-permute-start | bytes 73736 | tf_op jit(solution)/shard_map/ppermute | solution.py:273
  13.3 0.3 %select_keep.1 = (bf16[48,128]{1,0:T(8,128)(2,1)S(1)}, bf16[48,128]{1,0:T(8,128)(2,1)S(1)}) custom-call(bf16[96,128]{1,0:T(8,128)(2,1)S(1)} %select_send.1.refs_0_, s32[2,256]{1,0:T(2,128)S(1)} %get-tuple-element.20.refs_0_.refs_1_, s32[2,256]{1,0:T(2,128)S(1)} %collective-permute-done.1.refs_1_.refs_2_, bf16[2,32,1024]{2,1,0:T(8,128)(2,1)S(1)} %gather.1.refs_2_.refs_3_, ...), custom_call_target="tpu_custom_call" | custom-call | flops 68719476736 | bytes 268435456 | tf_op jit(solution)/shard_map/select_keep/pallas_call | solution.py:26
  13.5 0.0 copy-start.7
  13.6 1.2 %turn.1 = (bf16[48,128]{1,0:T(8,128)(2,1)S(1)}, bf16[8192,128]{1,0:T(8,128)(2,1)S(1)}) custom-call(bf16[48,128]{1,0:T(8,128)(2,1)S(1)} %get-tuple-element.21.refs_0_, s32[1,256]{1,0:T(1,128)S(1)} %get-tuple-element.18.refs_1_, bf16[128,128,128]{2,1,0:T(8,128)(2,1)S(1)} %copy-done), custom_call_target="tpu_custom_call" | custom-call | flops 17179869184 | bytes 67108864 | tf_op jit(solution)/shard_map/turn/pallas_call | solution.py:26
  14.7 0.1 collective-permute-done.4
  14.8 1.6 %collective-permute-start.5 = (bf16[96,128]{1,0:T(8,128)(2,1)S(1)}, bf16[96,128]{1,0:T(8,128)(2,1)S(1)}, u32[]{:S(2)}, u32[]{:S(2)}) collective-permute-start(bf16[96,128]{1,0:T(8,128)(2,1)S(1)} %pad_maximum_fusion), channel_id=1, source_target_pairs={{0,9},{1,8},{2,11},{3,10},{4,13},{5,12},{6,15},{7,14},{8,1},{9,0},... | collective-permute-start | bytes 73736 | tf_op jit(solution)/shard_map/ppermute | solution.py:273
  16.4 0.0 copy-done.7
  16.4 1.4 %early.1 = (f32[8,128]{1,0:T(8,128)S(1)}, bf16[10240,128]{1,0:T(8,128)(2,1)S(1)}, bf16[1024,128]{1,0:T(8,128)(2,1)S(1)}, bf16[1024,128]{1,0:T(8,128)(2,1)S(1)}) custom-call(s32[192,128]{1,0:T(8,128)S(1)} %get-tuple-element.17.refs_0_.refs_1_, s32[1,256]{1,0:T(1,128)S(1)} %get-tuple-element.18.refs_1_, bf16[128,128,128]{2,1,0:T(8,128)(2,1)S(1)} %copy-done, ...), custom_call_target="tpu_custom_call" | custom-call | flops 17179869184 | bytes 67108864 | tf_op jit(solution)/shard_map/early/pallas_call | solution.py:26
  17.9 0.0 copy-start.2
  17.9 0.2 collective-permute-done.5.refs_4_
  18.1 0.5 %couple.1.mine_ref = f32[8,128]{1,0:T(8,128)S(1)} custom-call(f32[8,128]{1,0:T(8,128)S(1)} %get-tuple-element.24.refs_0_, s32[192,128]{1,0:T(8,128)S(1)} %get-tuple-element.17.refs_0_.refs_1_, bf16[8192,128]{1,0:T(8,128)(2,1)S(1)} %get-tuple-element.22.refs_5_.refs_2_, bf16[10240,128]{1,0:T(8,128)(2,1)S(1)} %get-tuple-element.25.refs_3_, ...), custom_call_target="tpu_custom_call" | custom-call | tf_op jit(solution)/shard_map/couple/pallas_call | solution.py:26
  18.6 0.5 %collective-permute-start.6 = (f32[8,128]{1,0:T(8,128)S(1)}, f32[8,128]{1,0:T(8,128)S(1)}, u32[]{:S(2)}, u32[]{:S(2)}) collective-permute-start(f32[8,128]{1,0:T(8,128)S(1)} %couple.1.mine_ref), channel_id=1, source_target_pairs={{0,1},{1,0},{2,3},{3,2},{4,5},{5,4},{6,7},{7,6},{8,9},{9,8},{10,11... | collective-permute-start | bytes 12296 | tf_op jit(solution)/shard_map/ppermute | solution.py:406
  19.1 0.8 %collective-permute-done.6.other_ref = f32[8,128]{1,0:T(8,128)S(1)} collective-permute-done((f32[8,128]{1,0:T(8,128)S(1)}, f32[8,128]{1,0:T(8,128)S(1)}, u32[]{:S(2)}, u32[]{:S(2)}) %collective-permute-start.6) | collective-permute-done | bytes 4128 | tf_op jit(solution)/shard_map/ppermute | solution.py:406
  19.9 0.8 %solve.1 = f32[8,128]{1,0:T(8,128)} custom-call(f32[8,128]{1,0:T(8,128)S(1)} %couple.1.mine_ref, f32[8,128]{1,0:T(8,128)S(1)} %collective-permute-done.6.other_ref, f32[8,128]{1,0:T(8,128)S(1)} %bitcast.9, bf16[1024,128]{1,0:T(8,128)(2,1)S(1)} %get-tuple-element.27.high_ref, bf16[1024,128]{1,0:T(8,128)(2,1)S(1)} %get-tuple-element.28.low_ref), custom_call_target="tpu_custom_call" | custom-call | tf_op jit(solution)/shard_map/solve/pallas_call | solution.py:26
  (11 shorter events, 0.0 us)
Async XLA Ops:
  0.0 3.0 %copy-start.3 = (s32[128]{0:T(128)S(1)}, s32[128]{0:T(128)}, u32[]{:S(2)}) copy-start(s32[128]{0:T(128)} %param.11) | copy-start | bytes 1540
  0.0 3.0 %copy-start.4 = (s32[128]{0:T(128)S(1)}, s32[128]{0:T(128)}, u32[]{:S(2)}) copy-start(s32[128]{0:T(128)} %param.12) | copy-start | bytes 1540
  0.0 3.1 %copy-start.5 = (s32[128]{0:T(128)S(1)}, s32[128]{0:T(128)}, u32[]{:S(2)}) copy-start(s32[128]{0:T(128)} %param.13) | copy-start | bytes 1540
  0.0 5.5 %copy-start.1 = (bf16[32,1024]{1,0:T(8,128)(2,1)S(1)}, bf16[32,1024]{1,0:T(8,128)(2,1)}, u32[]{:S(2)}) copy-start(bf16[32,1024]{1,0:T(8,128)(2,1)} %param.8) | copy-start | bytes 196612
  0.0 5.5 %collective-permute-start.2 = (bf16[1,32,1024]{2,1,0:T(8,128)(2,1)}, bf16[1,32,1024]{2,1,0:T(8,128)(2,1)S(1)}, u32[]{:S(2)}, u32[]{:S(2)}) collective-permute-start(bf16[1,32,1024]{2,1,0:T(8,128)(2,1)} %bitcast.7), channel_id=1, source_target_pairs={{0,2},{1,5},{2,0},{3,7},{4,6},{5,1},{6,4},{7,3},{8,10},{9,13},{10,... | collective-permute-start | bytes 196616 | tf_op jit(solution)/shard_map/ppermute | solution.py:273
  3.0 2.5 %copy-start = (bf16[128,128,128]{2,1,0:T(8,128)(2,1)S(1)}, bf16[128,128,128]{2,1,0:T(8,128)(2,1)}, u32[]{:S(2)}) copy-start(bf16[128,128,128]{2,1,0:T(8,128)(2,1)} %refs_2_.5) | copy-start | bytes 12582916
  3.2 4.0 %collective-permute-start = (s32[1,256]{1,0:T(1,128)S(1)}, s32[1,256]{1,0:T(1,128)S(1)}, u32[]{:S(2)}, u32[]{:S(2)}) collective-permute-start(s32[1,256]{1,0:T(1,128)S(1)} %request.1.refs_0_), channel_id=1, source_target_pairs={{0,17},{1,16},{2,19},{3,18},{4,21},{5,20},{6,23},{7,22},{8,25},{9,... | collective-permute-start | bytes 3080 | tf_op jit(solution)/shard_map/ppermute | solution.py:273
  5.5 3.4 %copy-start.6 = (s32[128]{0:T(128)S(1)}, s32[128]{0:T(128)}, u32[]{:S(2)}) copy-start(s32[128]{0:T(128)} %param.10) | copy-start | bytes 1540
  5.5 4.7 %collective-permute-start.3 = (bf16[2,32,1024]{2,1,0:T(8,128)(2,1)S(1)}, bf16[2,32,1024]{2,1,0:T(8,128)(2,1)S(1)}, u32[]{:S(2)}, u32[]{:S(2)}) collective-permute-start(bf16[2,32,1024]{2,1,0:T(8,128)(2,1)S(1)} %gather.1.refs_2_.refs_3_), channel_id=1, source_target_pairs={{0,5},{1,2},{2,7},{3,0},{4,1},{5,6},{6,3},{7,4},{8,13},{9,10},{10,... | collective-permute-start | bytes 393224 | tf_op jit(solution)/shard_map/ppermute | solution.py:273
  7.2 3.0 %collective-permute-start.1 = (s32[2,256]{1,0:T(2,128)S(1)}, s32[2,256]{1,0:T(2,128)S(1)}, u32[]{:S(2)}, u32[]{:S(2)}) collective-permute-start(s32[2,256]{1,0:T(2,128)S(1)} %join.1.refs_2_), channel_id=1, source_target_pairs={{0,9},{1,8},{2,11},{3,10},{4,13},{5,12},{6,15},{7,14},{8,1},{9,0},... | collective-permute-start | bytes 6152 | tf_op jit(solution)/shard_map/ppermute | solution.py:273
  10.5 4.3 %collective-permute-start.4 = (bf16[96,128]{1,0:T(8,128)(2,1)S(1)}, bf16[96,128]{1,0:T(8,128)(2,1)S(1)}, u32[]{:S(2)}, u32[]{:S(2)}) collective-permute-start(bf16[96,128]{1,0:T(8,128)(2,1)S(1)} %select_send.1.refs_0_), channel_id=1, source_target_pairs={{0,17},{1,16},{2,19},{3,18},{4,21},{5,20},{6,23},{7,22},{8,25},{9,... | collective-permute-start | bytes 73736 | tf_op jit(solution)/shard_map/ppermute | solution.py:273
  13.5 2.9 %copy-start.7 = (f32[8,128,128]{2,1,0:T(8,128)S(1)}, f32[8,128,128]{2,1,0:T(8,128)}, u32[]{:S(2)}) copy-start(f32[8,128,128]{2,1,0:T(8,128)} %refs_3_.3) | copy-start | bytes 1572868
  14.8 3.3 %collective-permute-start.5 = (bf16[96,128]{1,0:T(8,128)(2,1)S(1)}, bf16[96,128]{1,0:T(8,128)(2,1)S(1)}, u32[]{:S(2)}, u32[]{:S(2)}) collective-permute-start(bf16[96,128]{1,0:T(8,128)(2,1)S(1)} %pad_maximum_fusion), channel_id=1, source_target_pairs={{0,9},{1,8},{2,11},{3,10},{4,13},{5,12},{6,15},{7,14},{8,1},{9,0},... | collective-permute-start | bytes 73736 | tf_op jit(solution)/shard_map/ppermute | solution.py:273
  17.9 2.1 %copy-start.2 = (f32[1024]{0:T(1024)S(1)}, f32[1024]{0:T(1024)}, u32[]{:S(2)}) copy-start(f32[1024]{0:T(1024)} %param.14) | copy-start | bytes 12292
  18.6 1.3 %collective-permute-start.6 = (f32[8,128]{1,0:T(8,128)S(1)}, f32[8,128]{1,0:T(8,128)S(1)}, u32[]{:S(2)}, u32[]{:S(2)}) collective-permute-start(f32[8,128]{1,0:T(8,128)S(1)} %couple.1.mine_ref), channel_id=1, source_target_pairs={{0,1},{1,0},{2,3},{3,2},{4,5},{5,4},{6,7},{7,6},{8,9},{9,8},{10,11... | collective-permute-start | bytes 12296 | tf_op jit(solution)/shard_map/ppermute | solution.py:406

commit v10 on v9

--- a/solution.py
+++ b/solution.py
@@ -232,7 +232,7 @@
     left = jnp.concatenate([spread(high), spread(excite - high)], axis=0).astype(jnp.bfloat16)
     first = jnp.dot(left, high_ref[...], preferred_element_type=jnp.float32)
     second = jnp.dot(left, low_ref[...], preferred_element_type=jnp.float32)
-    out_ref[...] = first[:blocks] + (first[blocks:] + second[:blocks])
+    out_ref[...] = first[:blocks] + (first[blocks:] + (second[:blocks] + second[blocks:]))
 
 
 def body(

time: 20.8 us -> 20.8 us (level)
  no operation moved by 1% of the time
where the time goes in v10:
time: 20.8 us; the launch traced here: 20.7 us
  starting transfers between devices  13.1 us (63%)
  Pallas kernels  5.75 us (28%)
  waiting for transfers between devices  1.69 us (8%)
    ppermute x6, starting transfers between devices, hop(): return lax.ppermute(value, ('blk', 'lag'), pairs)  12.6 us
    pallas_call x11, Pallas kernels, call(): pl.pallas_call(kernel, out_shape=outs, in_specs=[VMEM] * len(operands), o...  5.75 us
    ppermute x6, waiting for transfers between devices, hop(): return lax.ppermute(value, ('blk', 'lag'), pairs)  0.87 us
    ppermute x1, waiting for transfers between devices, body(): other = lax.ppermute(mine, 'lag', [(0, 1), (1, 0)])  0.82 us
    ppermute x1, starting transfers between devices, body(): other = lax.ppermute(mine, 'lag', [(0, 1), (1, 0)])  0.49 us
  transfers between devices with their start and end apart: 7, of which 5 were waited for; matrix products, arithmetic and copies ran while one was open for 0% of the time, Pallas kernels for 20%

profile of v10, /device:TPU:0, one launch (start us, length us, event | category | flops | bytes accessed | tf_op | source)
XLA Modules:
  0.0 20.7 jit_solution(554656824351066173)
XLA Ops:
  0.0 3.0 %collective-permute-start.2 = (bf16[1,32,1024]{2,1,0:T(8,128)(2,1)}, bf16[1,32,1024]{2,1,0:T(8,128)(2,1)S(1)}, u32[]{:S(2)}, u32[]{:S(2)}) collective-permute-start(bf16[1,32,1024]{2,1,0:T(8,128)(2,1)} %bitcast.7), channel_id=1, source_target_pairs={{0,2},{1,5},{2,0},{3,7},{4,6},{5,1},{6,4},{7,3},{8,10},{9,13},{10,... | collective-permute-start | bytes 196616 | tf_op jit(solution)/shard_map/ppermute | solution.py:273
  3.0 0.0 copy-done.3
  3.0 0.0 copy-done.4
  3.1 0.0 copy-done.5
  3.1 0.1 request.1.refs_0_
  3.2 1.8 %collective-permute-start = (s32[1,256]{1,0:T(1,128)S(1)}, s32[1,256]{1,0:T(1,128)S(1)}, u32[]{:S(2)}, u32[]{:S(2)}) collective-permute-start(s32[1,256]{1,0:T(1,128)S(1)} %request.1.refs_0_), channel_id=1, source_target_pairs={{0,17},{1,16},{2,19},{3,18},{4,21},{5,20},{6,23},{7,22},{8,25},{9,... | collective-permute-start | bytes 3080 | tf_op jit(solution)/shard_map/ppermute | solution.py:273
  5.0 0.5 %collective-permute-done.2.refs_1_ = bf16[1,32,1024]{2,1,0:T(8,128)(2,1)S(1)} collective-permute-done((bf16[1,32,1024]{2,1,0:T(8,128)(2,1)}, bf16[1,32,1024]{2,1,0:T(8,128)(2,1)S(1)}, u32[]{:S(2)}, u32[]{:S(2)}) %collective-permute-start.2) | collective-permute-done | bytes 65568 | tf_op jit(solution)/shard_map/ppermute | solution.py:273
  5.5 0.0 copy-done.1
  5.5 0.0 copy-done
  5.5 0.0 copy-start.6
  5.5 1.7 %collective-permute-start.3 = (bf16[2,32,1024]{2,1,0:T(8,128)(2,1)S(1)}, bf16[2,32,1024]{2,1,0:T(8,128)(2,1)S(1)}, u32[]{:S(2)}, u32[]{:S(2)}) collective-permute-start(bf16[2,32,1024]{2,1,0:T(8,128)(2,1)S(1)} %gather.1.refs_2_.refs_3_), channel_id=1, source_target_pairs={{0,5},{1,2},{2,7},{3,0},{4,1},{5,6},{6,3},{7,4},{8,13},{9,10},{10,... | collective-permute-start | bytes 393224 | tf_op jit(solution)/shard_map/ppermute | solution.py:273
  7.2 0.0 collective-permute-done.refs_1_
  7.2 1.7 %collective-permute-start.1 = (s32[2,256]{1,0:T(2,128)S(1)}, s32[2,256]{1,0:T(2,128)S(1)}, u32[]{:S(2)}, u32[]{:S(2)}) collective-permute-start(s32[2,256]{1,0:T(2,128)S(1)} %join.1.refs_2_), channel_id=1, source_target_pairs={{0,9},{1,8},{2,11},{3,10},{4,13},{5,12},{6,15},{7,14},{8,1},{9,0},... | collective-permute-start | bytes 6152 | tf_op jit(solution)/shard_map/ppermute | solution.py:273
  8.9 0.0 copy-done.6
  8.9 1.2 %order.1 = (s32[2,256]{1,0:T(2,128)S(1)}, s32[1,256]{1,0:T(1,128)S(1)}, s32[192,128]{1,0:T(8,128)S(1)}, bf16[6144,128]{1,0:T(8,128)(2,1)S(1)}) custom-call(s32[1,256]{1,0:T(1,128)S(1)} %request.1.refs_0_, s32[1,128]{1,0:T(1,128)S(1)} %bitcast.13, s32[2,256]{1,0:T(2,128)S(1)} %join.1.refs_2_, bf16[128,128,128]{2,1,0:T(8,128)(2,1)S(1)} %copy-done), custom_call_target="tpu_custom_call" | custom-call | tf_op jit(solution)/shard_map/order/pallas_call | solution.py:26
  10.1 0.1 collective-permute-done.1.refs_1_.refs_2_
  10.2 0.0 collective-permute-done.3.refs_3_.refs_4_
  10.2 0.3 %select_send.1.refs_0_ = bf16[96,128]{1,0:T(8,128)(2,1)S(1)} custom-call(s32[2,256]{1,0:T(2,128)S(1)} %get-tuple-element.20.refs_0_.refs_1_, s32[2,256]{1,0:T(2,128)S(1)} %collective-permute-done.1.refs_1_.refs_2_, bf16[2,32,1024]{2,1,0:T(8,128)(2,1)S(1)} %gather.1.refs_2_.refs_3_, bf16[2,32,1024]{2,1,0:T(8,128)(2,1)S(1)} %collective-permute-done.3.refs_3_.refs_4_), custom_call_target="tpu_custom_call" | custom-call | flops 68719476736 | bytes 268435456 | tf_op jit(solution)/shard_map/select_send/pallas_call | solution.py:26
  10.5 2.8 %collective-permute-start.4 = (bf16[96,128]{1,0:T(8,128)(2,1)S(1)}, bf16[96,128]{1,0:T(8,128)(2,1)S(1)}, u32[]{:S(2)}, u32[]{:S(2)}) collective-permute-start(bf16[96,128]{1,0:T(8,128)(2,1)S(1)} %select_send.1.refs_0_), channel_id=1, source_target_pairs={{0,17},{1,16},{2,19},{3,18},{4,21},{5,20},{6,23},{7,22},{8,25},{9,... | collective-permute-start | bytes 73736 | tf_op jit(solution)/shard_map/ppermute | solution.py:273
  13.3 0.3 %select_keep.1 = (bf16[48,128]{1,0:T(8,128)(2,1)S(1)}, bf16[48,128]{1,0:T(8,128)(2,1)S(1)}) custom-call(bf16[96,128]{1,0:T(8,128)(2,1)S(1)} %select_send.1.refs_0_, s32[2,256]{1,0:T(2,128)S(1)} %get-tuple-element.20.refs_0_.refs_1_, s32[2,256]{1,0:T(2,128)S(1)} %collective-permute-done.1.refs_1_.refs_2_, bf16[2,32,1024]{2,1,0:T(8,128)(2,1)S(1)} %gather.1.refs_2_.refs_3_, ...), custom_call_target="tpu_custom_call" | custom-call | flops 68719476736 | bytes 268435456 | tf_op jit(solution)/shard_map/select_keep/pallas_call | solution.py:26
  13.5 0.0 copy-start.7
  13.6 1.2 %turn.1 = (bf16[48,128]{1,0:T(8,128)(2,1)S(1)}, bf16[8192,128]{1,0:T(8,128)(2,1)S(1)}) custom-call(bf16[48,128]{1,0:T(8,128)(2,1)S(1)} %get-tuple-element.21.refs_0_, s32[1,256]{1,0:T(1,128)S(1)} %get-tuple-element.18.refs_1_, bf16[128,128,128]{2,1,0:T(8,128)(2,1)S(1)} %copy-done), custom_call_target="tpu_custom_call" | custom-call | flops 17179869184 | bytes 67108864 | tf_op jit(solution)/shard_map/turn/pallas_call | solution.py:26
  14.7 0.1 collective-permute-done.4
  14.8 1.6 %collective-permute-start.5 = (bf16[96,128]{1,0:T(8,128)(2,1)S(1)}, bf16[96,128]{1,0:T(8,128)(2,1)S(1)}, u32[]{:S(2)}, u32[]{:S(2)}) collective-permute-start(bf16[96,128]{1,0:T(8,128)(2,1)S(1)} %pad_maximum_fusion), channel_id=1, source_target_pairs={{0,9},{1,8},{2,11},{3,10},{4,13},{5,12},{6,15},{7,14},{8,1},{9,0},... | collective-permute-start | bytes 73736 | tf_op jit(solution)/shard_map/ppermute | solution.py:273
  16.4 0.0 copy-done.7
  16.4 1.4 %early.1 = (f32[8,128]{1,0:T(8,128)S(1)}, bf16[10240,128]{1,0:T(8,128)(2,1)S(1)}, bf16[1024,128]{1,0:T(8,128)(2,1)S(1)}, bf16[1024,128]{1,0:T(8,128)(2,1)S(1)}) custom-call(s32[192,128]{1,0:T(8,128)S(1)} %get-tuple-element.17.refs_0_.refs_1_, s32[1,256]{1,0:T(1,128)S(1)} %get-tuple-element.18.refs_1_, bf16[128,128,128]{2,1,0:T(8,128)(2,1)S(1)} %copy-done, ...), custom_call_target="tpu_custom_call" | custom-call | flops 17179869184 | bytes 67108864 | tf_op jit(solution)/shard_map/early/pallas_call | solution.py:26
  17.9 0.0 copy-start.2
  17.9 0.2 collective-permute-done.5.refs_4_
  18.1 0.5 %couple.1.mine_ref = f32[8,128]{1,0:T(8,128)S(1)} custom-call(f32[8,128]{1,0:T(8,128)S(1)} %get-tuple-element.24.refs_0_, s32[192,128]{1,0:T(8,128)S(1)} %get-tuple-element.17.refs_0_.refs_1_, bf16[8192,128]{1,0:T(8,128)(2,1)S(1)} %get-tuple-element.22.refs_5_.refs_2_, bf16[10240,128]{1,0:T(8,128)(2,1)S(1)} %get-tuple-element.25.refs_3_, ...), custom_call_target="tpu_custom_call" | custom-call | tf_op jit(solution)/shard_map/couple/pallas_call | solution.py:26
  18.6 0.5 %collective-permute-start.6 = (f32[8,128]{1,0:T(8,128)S(1)}, f32[8,128]{1,0:T(8,128)S(1)}, u32[]{:S(2)}, u32[]{:S(2)}) collective-permute-start(f32[8,128]{1,0:T(8,128)S(1)} %couple.1.mine_ref), channel_id=1, source_target_pairs={{0,1},{1,0},{2,3},{3,2},{4,5},{5,4},{6,7},{7,6},{8,9},{9,8},{10,11... | collective-permute-start | bytes 12296 | tf_op jit(solution)/shard_map/ppermute | solution.py:406
  19.1 0.8 %collective-permute-done.6.other_ref = f32[8,128]{1,0:T(8,128)S(1)} collective-permute-done((f32[8,128]{1,0:T(8,128)S(1)}, f32[8,128]{1,0:T(8,128)S(1)}, u32[]{:S(2)}, u32[]{:S(2)}) %collective-permute-start.6) | collective-permute-done | bytes 4128 | tf_op jit(solution)/shard_map/ppermute | solution.py:406
  19.9 0.8 %solve.1 = f32[8,128]{1,0:T(8,128)} custom-call(f32[8,128]{1,0:T(8,128)S(1)} %couple.1.mine_ref, f32[8,128]{1,0:T(8,128)S(1)} %collective-permute-done.6.other_ref, f32[8,128]{1,0:T(8,128)S(1)} %bitcast.9, bf16[1024,128]{1,0:T(8,128)(2,1)S(1)} %get-tuple-element.27.high_ref, bf16[1024,128]{1,0:T(8,128)(2,1)S(1)} %get-tuple-element.28.low_ref), custom_call_target="tpu_custom_call" | custom-call | tf_op jit(solution)/shard_map/solve/pallas_call | solution.py:26
  (11 shorter events, 0.0 us)
Async XLA Ops:
  0.0 3.0 %copy-start.3 = (s32[128]{0:T(128)S(1)}, s32[128]{0:T(128)}, u32[]{:S(2)}) copy-start(s32[128]{0:T(128)} %param.11) | copy-start | bytes 1540
  0.0 3.0 %copy-start.4 = (s32[128]{0:T(128)S(1)}, s32[128]{0:T(128)}, u32[]{:S(2)}) copy-start(s32[128]{0:T(128)} %param.12) | copy-start | bytes 1540
  0.0 3.1 %copy-start.5 = (s32[128]{0:T(128)S(1)}, s32[128]{0:T(128)}, u32[]{:S(2)}) copy-start(s32[128]{0:T(128)} %param.13) | copy-start | bytes 1540
  0.0 5.5 %copy-start.1 = (bf16[32,1024]{1,0:T(8,128)(2,1)S(1)}, bf16[32,1024]{1,0:T(8,128)(2,1)}, u32[]{:S(2)}) copy-start(bf16[32,1024]{1,0:T(8,128)(2,1)} %param.8) | copy-start | bytes 196612
  0.0 5.5 %collective-permute-start.2 = (bf16[1,32,1024]{2,1,0:T(8,128)(2,1)}, bf16[1,32,1024]{2,1,0:T(8,128)(2,1)S(1)}, u32[]{:S(2)}, u32[]{:S(2)}) collective-permute-start(bf16[1,32,1024]{2,1,0:T(8,128)(2,1)} %bitcast.7), channel_id=1, source_target_pairs={{0,2},{1,5},{2,0},{3,7},{4,6},{5,1},{6,4},{7,3},{8,10},{9,13},{10,... | collective-permute-start | bytes 196616 | tf_op jit(solution)/shard_map/ppermute | solution.py:273
  3.0 2.5 %copy-start = (bf16[128,128,128]{2,1,0:T(8,128)(2,1)S(1)}, bf16[128,128,128]{2,1,0:T(8,128)(2,1)}, u32[]{:S(2)}) copy-start(bf16[128,128,128]{2,1,0:T(8,128)(2,1)} %refs_2_.5) | copy-start | bytes 12582916
  3.2 4.0 %collective-permute-start = (s32[1,256]{1,0:T(1,128)S(1)}, s32[1,256]{1,0:T(1,128)S(1)}, u32[]{:S(2)}, u32[]{:S(2)}) collective-permute-start(s32[1,256]{1,0:T(1,128)S(1)} %request.1.refs_0_), channel_id=1, source_target_pairs={{0,17},{1,16},{2,19},{3,18},{4,21},{5,20},{6,23},{7,22},{8,25},{9,... | collective-permute-start | bytes 3080 | tf_op jit(solution)/shard_map/ppermute | solution.py:273
  5.5 3.4 %copy-start.6 = (s32[128]{0:T(128)S(1)}, s32[128]{0:T(128)}, u32[]{:S(2)}) copy-start(s32[128]{0:T(128)} %param.10) | copy-start | bytes 1540
  5.5 4.7 %collective-permute-start.3 = (bf16[2,32,1024]{2,1,0:T(8,128)(2,1)S(1)}, bf16[2,32,1024]{2,1,0:T(8,128)(2,1)S(1)}, u32[]{:S(2)}, u32[]{:S(2)}) collective-permute-start(bf16[2,32,1024]{2,1,0:T(8,128)(2,1)S(1)} %gather.1.refs_2_.refs_3_), channel_id=1, source_target_pairs={{0,5},{1,2},{2,7},{3,0},{4,1},{5,6},{6,3},{7,4},{8,13},{9,10},{10,... | collective-permute-start | bytes 393224 | tf_op jit(solution)/shard_map/ppermute | solution.py:273
  7.2 3.0 %collective-permute-start.1 = (s32[2,256]{1,0:T(2,128)S(1)}, s32[2,256]{1,0:T(2,128)S(1)}, u32[]{:S(2)}, u32[]{:S(2)}) collective-permute-start(s32[2,256]{1,0:T(2,128)S(1)} %join.1.refs_2_), channel_id=1, source_target_pairs={{0,9},{1,8},{2,11},{3,10},{4,13},{5,12},{6,15},{7,14},{8,1},{9,0},... | collective-permute-start | bytes 6152 | tf_op jit(solution)/shard_map/ppermute | solution.py:273
  10.5 4.3 %collective-permute-start.4 = (bf16[96,128]{1,0:T(8,128)(2,1)S(1)}, bf16[96,128]{1,0:T(8,128)(2,1)S(1)}, u32[]{:S(2)}, u32[]{:S(2)}) collective-permute-start(bf16[96,128]{1,0:T(8,128)(2,1)S(1)} %select_send.1.refs_0_), channel_id=1, source_target_pairs={{0,17},{1,16},{2,19},{3,18},{4,21},{5,20},{6,23},{7,22},{8,25},{9,... | collective-permute-start | bytes 73736 | tf_op jit(solution)/shard_map/ppermute | solution.py:273
  13.5 2.9 %copy-start.7 = (f32[8,128,128]{2,1,0:T(8,128)S(1)}, f32[8,128,128]{2,1,0:T(8,128)}, u32[]{:S(2)}) copy-start(f32[8,128,128]{2,1,0:T(8,128)} %refs_3_.3) | copy-start | bytes 1572868
  14.8 3.3 %collective-permute-start.5 = (bf16[96,128]{1,0:T(8,128)(2,1)S(1)}, bf16[96,128]{1,0:T(8,128)(2,1)S(1)}, u32[]{:S(2)}, u32[]{:S(2)}) collective-permute-start(bf16[96,128]{1,0:T(8,128)(2,1)S(1)} %pad_maximum_fusion), channel_id=1, source_target_pairs={{0,9},{1,8},{2,11},{3,10},{4,13},{5,12},{6,15},{7,14},{8,1},{9,0},... | collective-permute-start | bytes 73736 | tf_op jit(solution)/shard_map/ppermute | solution.py:273
  17.9 2.1 %copy-start.2 = (f32[1024]{0:T(1024)S(1)}, f32[1024]{0:T(1024)}, u32[]{:S(2)}) copy-start(f32[1024]{0:T(1024)} %param.14) | copy-start | bytes 12292
  18.6 1.3 %collective-permute-start.6 = (f32[8,128]{1,0:T(8,128)S(1)}, f32[8,128]{1,0:T(8,128)S(1)}, u32[]{:S(2)}, u32[]{:S(2)}) collective-permute-start(f32[8,128]{1,0:T(8,128)S(1)} %couple.1.mine_ref), channel_id=1, source_target_pairs={{0,1},{1,0},{2,3},{3,2},{4,5},{5,4},{6,7},{7,6},{8,9},{9,8},{10,11... | collective-permute-start | bytes 12296 | tf_op jit(solution)/shard_map/ppermute | solution.py:406

commit v11 on v10

--- a/solution.py
+++ b/solution.py
@@ -312,7 +312,7 @@
     n_hops = len(exchange_bits)
 
     n_slots = plan.slots << n_hops
-    cuts = [0, n_slots // 64 * 16, max(n_slots // 2, n_slots * 7 // 12 // 16 * 16), n_slots]
+    cuts = [0, n_slots // 48 * 16, max(n_slots // 2, n_slots * 2 // 3 // 16 * 16), n_slots]
     wide = -(-n_slots // 128) * 128
     scratch = [pltpu.SMEM((1, wide), jnp.int32), pltpu.SemaphoreType.DMA]
 

time: 20.8 us -> 20.8 us (level)
  transfers between devices with their start and end apart: 7 -> 7, of which waited for: 5 -> 4; matrix products, arithmetic and copies ran while one was open for 0% -> 0% of each run, Pallas kernels for 20% -> 20%
where the time goes in v11:
time: 20.8 us; the launch traced here: 20.7 us
  starting transfers between devices  13.1 us (63%)
  Pallas kernels  5.75 us (28%)
  waiting for transfers between devices  1.7 us (8%)
    ppermute x6, starting transfers between devices, hop(): return lax.ppermute(value, ('blk', 'lag'), pairs)  12.6 us
    pallas_call x11, Pallas kernels, call(): pl.pallas_call(kernel, out_shape=outs, in_specs=[VMEM] * len(operands), o...  5.75 us
    ppermute x6, waiting for transfers between devices, hop(): return lax.ppermute(value, ('blk', 'lag'), pairs)  0.88 us
    ppermute x1, waiting for transfers between devices, body(): other = lax.ppermute(mine, 'lag', [(0, 1), (1, 0)])  0.82 us
    ppermute x1, starting transfers between devices, body(): other = lax.ppermute(mine, 'lag', [(0, 1), (1, 0)])  0.49 us
  transfers between devices with their start and end apart: 7, of which 4 were waited for; matrix products, arithmetic and copies ran while one was open for 0% of the time, Pallas kernels for 20%

profile of v11, /device:TPU:0, one launch (start us, length us, event | category | flops | bytes accessed | tf_op | source)
XLA Modules:
  0.0 20.7 jit_solution(5609286932717283321)
XLA Ops:
  0.0 3.0 %collective-permute-start.2 = (bf16[1,32,1024]{2,1,0:T(8,128)(2,1)}, bf16[1,32,1024]{2,1,0:T(8,128)(2,1)S(1)}, u32[]{:S(2)}, u32[]{:S(2)}) collective-permute-start(bf16[1,32,1024]{2,1,0:T(8,128)(2,1)} %bitcast.7), channel_id=1, source_target_pairs={{0,2},{1,5},{2,0},{3,7},{4,6},{5,1},{6,4},{7,3},{8,10},{9,13},{10,... | collective-permute-start | bytes 196616 | tf_op jit(solution)/shard_map/ppermute | solution.py:273
  3.0 0.0 copy-done.3
  3.0 0.0 copy-done.4
  3.1 0.0 copy-done.5
  3.1 0.1 request.1.refs_0_
  3.2 1.8 %collective-permute-start = (s32[1,256]{1,0:T(1,128)S(1)}, s32[1,256]{1,0:T(1,128)S(1)}, u32[]{:S(2)}, u32[]{:S(2)}) collective-permute-start(s32[1,256]{1,0:T(1,128)S(1)} %request.1.refs_0_), channel_id=1, source_target_pairs={{0,17},{1,16},{2,19},{3,18},{4,21},{5,20},{6,23},{7,22},{8,25},{9,... | collective-permute-start | bytes 3080 | tf_op jit(solution)/shard_map/ppermute | solution.py:273
  5.0 0.5 %collective-permute-done.2.refs_1_ = bf16[1,32,1024]{2,1,0:T(8,128)(2,1)S(1)} collective-permute-done((bf16[1,32,1024]{2,1,0:T(8,128)(2,1)}, bf16[1,32,1024]{2,1,0:T(8,128)(2,1)S(1)}, u32[]{:S(2)}, u32[]{:S(2)}) %collective-permute-start.2) | collective-permute-done | bytes 65568 | tf_op jit(solution)/shard_map/ppermute | solution.py:273
  5.5 0.0 copy-done.1
  5.5 0.0 copy-done
  5.5 0.0 copy-start.6
  5.5 1.7 %collective-permute-start.3 = (bf16[2,32,1024]{2,1,0:T(8,128)(2,1)S(1)}, bf16[2,32,1024]{2,1,0:T(8,128)(2,1)S(1)}, u32[]{:S(2)}, u32[]{:S(2)}) collective-permute-start(bf16[2,32,1024]{2,1,0:T(8,128)(2,1)S(1)} %gather.1.refs_2_.refs_3_), channel_id=1, source_target_pairs={{0,5},{1,2},{2,7},{3,0},{4,1},{5,6},{6,3},{7,4},{8,13},{9,10},{10,... | collective-permute-start | bytes 393224 | tf_op jit(solution)/shard_map/ppermute | solution.py:273
  7.2 0.0 collective-permute-done.refs_1_
  7.2 1.7 %collective-permute-start.1 = (s32[2,256]{1,0:T(2,128)S(1)}, s32[2,256]{1,0:T(2,128)S(1)}, u32[]{:S(2)}, u32[]{:S(2)}) collective-permute-start(s32[2,256]{1,0:T(2,128)S(1)} %join.1.refs_2_), channel_id=1, source_target_pairs={{0,9},{1,8},{2,11},{3,10},{4,13},{5,12},{6,15},{7,14},{8,1},{9,0},... | collective-permute-start | bytes 6152 | tf_op jit(solution)/shard_map/ppermute | solution.py:273
  8.9 0.0 copy-done.6
  8.9 1.3 %order.1 = (s32[2,256]{1,0:T(2,128)S(1)}, s32[1,256]{1,0:T(1,128)S(1)}, s32[192,128]{1,0:T(8,128)S(1)}, bf16[8192,128]{1,0:T(8,128)(2,1)S(1)}) custom-call(s32[1,256]{1,0:T(1,128)S(1)} %request.1.refs_0_, s32[1,128]{1,0:T(1,128)S(1)} %bitcast.13, s32[2,256]{1,0:T(2,128)S(1)} %join.1.refs_2_, bf16[128,128,128]{2,1,0:T(8,128)(2,1)S(1)} %copy-done), custom_call_target="tpu_custom_call" | custom-call | tf_op jit(solution)/shard_map/order/pallas_call | solution.py:26
  10.2 0.0 collective-permute-done.1.refs_1_.refs_2_
  10.2 0.0 collective-permute-done.3.refs_3_.refs_4_
  10.2 0.3 %select_send.1.refs_0_ = bf16[96,128]{1,0:T(8,128)(2,1)S(1)} custom-call(s32[2,256]{1,0:T(2,128)S(1)} %get-tuple-element.20.refs_0_.refs_1_, s32[2,256]{1,0:T(2,128)S(1)} %collective-permute-done.1.refs_1_.refs_2_, bf16[2,32,1024]{2,1,0:T(8,128)(2,1)S(1)} %gather.1.refs_2_.refs_3_, bf16[2,32,1024]{2,1,0:T(8,128)(2,1)S(1)} %collective-permute-done.3.refs_3_.refs_4_), custom_call_target="tpu_custom_call" | custom-call | flops 68719476736 | bytes 268435456 | tf_op jit(solution)/shard_map/select_send/pallas_call | solution.py:26
  10.5 2.8 %collective-permute-start.4 = (bf16[96,128]{1,0:T(8,128)(2,1)S(1)}, bf16[96,128]{1,0:T(8,128)(2,1)S(1)}, u32[]{:S(2)}, u32[]{:S(2)}) collective-permute-start(bf16[96,128]{1,0:T(8,128)(2,1)S(1)} %select_send.1.refs_0_), channel_id=1, source_target_pairs={{0,17},{1,16},{2,19},{3,18},{4,21},{5,20},{6,23},{7,22},{8,25},{9,... | collective-permute-start | bytes 73736 | tf_op jit(solution)/shard_map/ppermute | solution.py:273
  13.3 0.3 %select_keep.1 = (bf16[48,128]{1,0:T(8,128)(2,1)S(1)}, bf16[48,128]{1,0:T(8,128)(2,1)S(1)}) custom-call(bf16[96,128]{1,0:T(8,128)(2,1)S(1)} %select_send.1.refs_0_, s32[2,256]{1,0:T(2,128)S(1)} %get-tuple-element.20.refs_0_.refs_1_, s32[2,256]{1,0:T(2,128)S(1)} %collective-permute-done.1.refs_1_.refs_2_, bf16[2,32,1024]{2,1,0:T(8,128)(2,1)S(1)} %gather.1.refs_2_.refs_3_, ...), custom_call_target="tpu_custom_call" | custom-call | flops 68719476736 | bytes 268435456 | tf_op jit(solution)/shard_map/select_keep/pallas_call | solution.py:26
  13.5 0.0 copy-start.7
  13.6 1.2 %turn.1 = (bf16[48,128]{1,0:T(8,128)(2,1)S(1)}, bf16[8192,128]{1,0:T(8,128)(2,1)S(1)}) custom-call(bf16[48,128]{1,0:T(8,128)(2,1)S(1)} %get-tuple-element.21.refs_0_, s32[1,256]{1,0:T(1,128)S(1)} %get-tuple-element.18.refs_1_, bf16[128,128,128]{2,1,0:T(8,128)(2,1)S(1)} %copy-done), custom_call_target="tpu_custom_call" | custom-call | flops 17179869184 | bytes 67108864 | tf_op jit(solution)/shard_map/turn/pallas_call | solution.py:26
  14.7 0.1 collective-permute-done.4
  14.8 1.6 %collective-permute-start.5 = (bf16[96,128]{1,0:T(8,128)(2,1)S(1)}, bf16[96,128]{1,0:T(8,128)(2,1)S(1)}, u32[]{:S(2)}, u32[]{:S(2)}) collective-permute-start(bf16[96,128]{1,0:T(8,128)(2,1)S(1)} %pad_maximum_fusion), channel_id=1, source_target_pairs={{0,9},{1,8},{2,11},{3,10},{4,13},{5,12},{6,15},{7,14},{8,1},{9,0},... | collective-permute-start | bytes 73736 | tf_op jit(solution)/shard_map/ppermute | solution.py:273
  16.4 0.0 copy-done.7
  16.4 1.3 %early.1 = (f32[8,128]{1,0:T(8,128)S(1)}, bf16[8192,128]{1,0:T(8,128)(2,1)S(1)}, bf16[1024,128]{1,0:T(8,128)(2,1)S(1)}, bf16[1024,128]{1,0:T(8,128)(2,1)S(1)}) custom-call(s32[192,128]{1,0:T(8,128)S(1)} %get-tuple-element.17.refs_0_.refs_1_, s32[1,256]{1,0:T(1,128)S(1)} %get-tuple-element.18.refs_1_, bf16[128,128,128]{2,1,0:T(8,128)(2,1)S(1)} %copy-done, ...), custom_call_target="tpu_custom_call" | custom-call | flops 17179869184 | bytes 67108864 | tf_op jit(solution)/shard_map/early/pallas_call | solution.py:26
  17.7 0.4 %collective-permute-done.5.refs_4_ = bf16[96,128]{1,0:T(8,128)(2,1)S(1)} collective-permute-done((bf16[96,128]{1,0:T(8,128)(2,1)S(1)}, bf16[96,128]{1,0:T(8,128)(2,1)S(1)}, u32[]{:S(2)}, u32[]{:S(2)}) %collective-permute-start.5) | collective-permute-done | bytes 24608 | tf_op jit(solution)/shard_map/ppermute | solution.py:273
  18.1 0.5 %couple.1.mine_ref = f32[8,128]{1,0:T(8,128)S(1)} custom-call(f32[8,128]{1,0:T(8,128)S(1)} %get-tuple-element.24.refs_0_, s32[192,128]{1,0:T(8,128)S(1)} %get-tuple-element.17.refs_0_.refs_1_, bf16[8192,128]{1,0:T(8,128)(2,1)S(1)} %get-tuple-element.22.refs_5_.refs_2_, bf16[8192,128]{1,0:T(8,128)(2,1)S(1)} %get-tuple-element.25.refs_3_, ...), custom_call_target="tpu_custom_call" | custom-call | tf_op jit(solution)/shard_map/couple/pallas_call | solution.py:26
  18.6 0.5 %collective-permute-start.6 = (f32[8,128]{1,0:T(8,128)S(1)}, f32[8,128]{1,0:T(8,128)S(1)}, u32[]{:S(2)}, u32[]{:S(2)}) collective-permute-start(f32[8,128]{1,0:T(8,128)S(1)} %couple.1.mine_ref), channel_id=1, source_target_pairs={{0,1},{1,0},{2,3},{3,2},{4,5},{5,4},{6,7},{7,6},{8,9},{9,8},{10,11... | collective-permute-start | bytes 12296 | tf_op jit(solution)/shard_map/ppermute | solution.py:406
  19.1 0.8 %collective-permute-done.6.other_ref = f32[8,128]{1,0:T(8,128)S(1)} collective-permute-done((f32[8,128]{1,0:T(8,128)S(1)}, f32[8,128]{1,0:T(8,128)S(1)}, u32[]{:S(2)}, u32[]{:S(2)}) %collective-permute-start.6) | collective-permute-done | bytes 4128 | tf_op jit(solution)/shard_map/ppermute | solution.py:406
  19.9 0.0 copy-done.2
  19.9 0.8 %solve.1 = f32[8,128]{1,0:T(8,128)} custom-call(f32[8,128]{1,0:T(8,128)S(1)} %couple.1.mine_ref, f32[8,128]{1,0:T(8,128)S(1)} %collective-permute-done.6.other_ref, f32[8,128]{1,0:T(8,128)S(1)} %bitcast.9, bf16[1024,128]{1,0:T(8,128)(2,1)S(1)} %get-tuple-element.27.high_ref, bf16[1024,128]{1,0:T(8,128)(2,1)S(1)} %get-tuple-element.28.low_ref), custom_call_target="tpu_custom_call" | custom-call | tf_op jit(solution)/shard_map/solve/pallas_call | solution.py:26
  (11 shorter events, 0.0 us)
Async XLA Ops:
  0.0 3.0 %copy-start.3 = (s32[128]{0:T(128)S(1)}, s32[128]{0:T(128)}, u32[]{:S(2)}) copy-start(s32[128]{0:T(128)} %param.11) | copy-start | bytes 1540
  0.0 3.0 %copy-start.4 = (s32[128]{0:T(128)S(1)}, s32[128]{0:T(128)}, u32[]{:S(2)}) copy-start(s32[128]{0:T(128)} %param.12) | copy-start | bytes 1540
  0.0 3.1 %copy-start.5 = (s32[128]{0:T(128)S(1)}, s32[128]{0:T(128)}, u32[]{:S(2)}) copy-start(s32[128]{0:T(128)} %param.13) | copy-start | bytes 1540
  0.0 5.5 %copy-start.1 = (bf16[32,1024]{1,0:T(8,128)(2,1)S(1)}, bf16[32,1024]{1,0:T(8,128)(2,1)}, u32[]{:S(2)}) copy-start(bf16[32,1024]{1,0:T(8,128)(2,1)} %param.8) | copy-start | bytes 196612
  0.0 5.5 %collective-permute-start.2 = (bf16[1,32,1024]{2,1,0:T(8,128)(2,1)}, bf16[1,32,1024]{2,1,0:T(8,128)(2,1)S(1)}, u32[]{:S(2)}, u32[]{:S(2)}) collective-permute-start(bf16[1,32,1024]{2,1,0:T(8,128)(2,1)} %bitcast.7), channel_id=1, source_target_pairs={{0,2},{1,5},{2,0},{3,7},{4,6},{5,1},{6,4},{7,3},{8,10},{9,13},{10,... | collective-permute-start | bytes 196616 | tf_op jit(solution)/shard_map/ppermute | solution.py:273
  3.0 2.5 %copy-start = (bf16[128,128,128]{2,1,0:T(8,128)(2,1)S(1)}, bf16[128,128,128]{2,1,0:T(8,128)(2,1)}, u32[]{:S(2)}) copy-start(bf16[128,128,128]{2,1,0:T(8,128)(2,1)} %refs_2_.5) | copy-start | bytes 12582916
  3.2 4.0 %collective-permute-start = (s32[1,256]{1,0:T(1,128)S(1)}, s32[1,256]{1,0:T(1,128)S(1)}, u32[]{:S(2)}, u32[]{:S(2)}) collective-permute-start(s32[1,256]{1,0:T(1,128)S(1)} %request.1.refs_0_), channel_id=1, source_target_pairs={{0,17},{1,16},{2,19},{3,18},{4,21},{5,20},{6,23},{7,22},{8,25},{9,... | collective-permute-start | bytes 3080 | tf_op jit(solution)/shard_map/ppermute | solution.py:273
  5.5 3.4 %copy-start.6 = (s32[128]{0:T(128)S(1)}, s32[128]{0:T(128)}, u32[]{:S(2)}) copy-start(s32[128]{0:T(128)} %param.10) | copy-start | bytes 1540
  5.5 4.7 %collective-permute-start.3 = (bf16[2,32,1024]{2,1,0:T(8,128)(2,1)S(1)}, bf16[2,32,1024]{2,1,0:T(8,128)(2,1)S(1)}, u32[]{:S(2)}, u32[]{:S(2)}) collective-permute-start(bf16[2,32,1024]{2,1,0:T(8,128)(2,1)S(1)} %gather.1.refs_2_.refs_3_), channel_id=1, source_target_pairs={{0,5},{1,2},{2,7},{3,0},{4,1},{5,6},{6,3},{7,4},{8,13},{9,10},{10,... | collective-permute-start | bytes 393224 | tf_op jit(solution)/shard_map/ppermute | solution.py:273
  7.2 3.0 %collective-permute-start.1 = (s32[2,256]{1,0:T(2,128)S(1)}, s32[2,256]{1,0:T(2,128)S(1)}, u32[]{:S(2)}, u32[]{:S(2)}) collective-permute-start(s32[2,256]{1,0:T(2,128)S(1)} %join.1.refs_2_), channel_id=1, source_target_pairs={{0,9},{1,8},{2,11},{3,10},{4,13},{5,12},{6,15},{7,14},{8,1},{9,0},... | collective-permute-start | bytes 6152 | tf_op jit(solution)/shard_map/ppermute | solution.py:273
  10.5 4.3 %collective-permute-start.4 = (bf16[96,128]{1,0:T(8,128)(2,1)S(1)}, bf16[96,128]{1,0:T(8,128)(2,1)S(1)}, u32[]{:S(2)}, u32[]{:S(2)}) collective-permute-start(bf16[96,128]{1,0:T(8,128)(2,1)S(1)} %select_send.1.refs_0_), channel_id=1, source_target_pairs={{0,17},{1,16},{2,19},{3,18},{4,21},{5,20},{6,23},{7,22},{8,25},{9,... | collective-permute-start | bytes 73736 | tf_op jit(solution)/shard_map/ppermute | solution.py:273
  13.5 2.9 %copy-start.7 = (f32[8,128,128]{2,1,0:T(8,128)S(1)}, f32[8,128,128]{2,1,0:T(8,128)}, u32[]{:S(2)}) copy-start(f32[8,128,128]{2,1,0:T(8,128)} %refs_3_.3) | copy-start | bytes 1572868
  14.8 3.3 %collective-permute-start.5 = (bf16[96,128]{1,0:T(8,128)(2,1)S(1)}, bf16[96,128]{1,0:T(8,128)(2,1)S(1)}, u32[]{:S(2)}, u32[]{:S(2)}) collective-permute-start(bf16[96,128]{1,0:T(8,128)(2,1)S(1)} %pad_maximum_fusion), channel_id=1, source_target_pairs={{0,9},{1,8},{2,11},{3,10},{4,13},{5,12},{6,15},{7,14},{8,1},{9,0},... | collective-permute-start | bytes 73736 | tf_op jit(solution)/shard_map/ppermute | solution.py:273
  18.1 1.8 %copy-start.2 = (f32[1024]{0:T(1024)S(1)}, f32[1024]{0:T(1024)}, u32[]{:S(2)}) copy-start(f32[1024]{0:T(1024)} %param.14) | copy-start | bytes 12292
  18.6 1.3 %collective-permute-start.6 = (f32[8,128]{1,0:T(8,128)S(1)}, f32[8,128]{1,0:T(8,128)S(1)}, u32[]{:S(2)}, u32[]{:S(2)}) collective-permute-start(f32[8,128]{1,0:T(8,128)S(1)} %couple.1.mine_ref), channel_id=1, source_target_pairs={{0,1},{1,0},{2,3},{3,2},{4,5},{5,4},{6,7},{7,6},{8,9},{9,8},{10,11... | collective-permute-start | bytes 12296 | tf_op jit(solution)/shard_map/ppermute | solution.py:406
